TPU v7x, 512 devices: a whole 4x4x16 slice. The times are simulated.
512 devices in a mesh: expert: 64 (over y, z), hidden: 8 (over x, core).
Axes of the slice: x: 4, y: 4, z: 16, core: 2. Of those that a mesh axis runs over, the one named last changes fastest.
Arguments:
- tokens: bfloat16 [4096, 4096], P('expert', 'hidden'), may hold values from -6 to 6
- route_ids: int32 [4096, 8], P('expert'), may hold values from 0 to 63, all different within a row; in each aligned block of 64 rows (0 to 63, 64 to 127, ...) at most 12 rows name the same one
- route_weights: float32 [4096, 8], P('expert'), may hold values from 0.05 to 1
- gate_up: bfloat16 [64, 2, 768, 4096], P('expert', None, 'hidden'), may hold values from -0.09375 to 0.09375
- down_proj: bfloat16 [64, 768, 4096], P('expert', None, 'hidden'), may hold values from -0.21875 to 0.21875
Outputs:
- layer_out: bfloat16 [4096, 4096], P('expert', 'hidden')
- hessian: float32 [64, 768, 768], P('expert', 'hidden')
Inputs may be any that keep to these rules, and one draw needn't show every extreme that they name: `route_ids`: each token names 8 different experts. Within the rows of one device (aligned blocks of 64 tokens) no expert is named more than 12 times, and in some block one expert is named exactly 12 times. Every expert is named by some token.
All inputs are finite; a program needn't handle non-finite values.
Results may differ from a plain program's by a relative error of at most 0.012.
Values may be sent and summed in bfloat16 or wider, within the bound.
No kernel may reach another device: no remote copies, remote signals or barrier semaphores. Data moves between devices by JAX's collectives and lax.ppermute only.
A program may use at most 64 MiB of HBM per device.

v0:
```python
import jax
import jax.numpy as jnp
from jax import lax
from jax.sharding import PartitionSpec as P


def body(tokens, route_ids, route_weights, gate_up, down_proj):
    token_count = tokens.shape[0]
    route_top = route_ids.shape[1]
    local_experts = gate_up.shape[0]
    expert_devices = lax.axis_size("expert")
    all_experts = local_experts * expert_devices
    capacity = 3 * token_count * route_top // (2 * all_experts)
    flat_ids = route_ids.reshape(-1)
    route_total = flat_ids.shape[0]
    onehot = (flat_ids[:, None] == jnp.arange(all_experts, dtype=jnp.int32)[None, :]).astype(
        jnp.int32
    )
    earlier = jnp.cumsum(onehot, axis=0) - onehot
    slot_of = jnp.sum(earlier * onehot, axis=1)
    per_expert = jnp.sum(onehot, axis=0)
    target = flat_ids * capacity + slot_of
    matches = target[None, :] == jnp.arange(all_experts * capacity, dtype=jnp.int32)[:, None]
    filled = jnp.any(matches, axis=1)
    route_token = jnp.arange(route_total, dtype=jnp.int32)[None, :] // route_top
    source_row = jnp.sum(jnp.where(matches, route_token, 0), axis=1)
    sent_counts = per_expert.astype(jnp.bfloat16).reshape(all_experts, 1)
    zero_value = jnp.zeros((), jnp.bfloat16)
    features = lax.all_gather(tokens, "hidden", axis=1, tiled=True)
    outgoing = jnp.where(filled[:, None], features[source_row], zero_value).reshape(
        all_experts, capacity, features.shape[1]
    )
    arrived, arrived_counts = (
        lax.all_to_all(outgoing, "expert", split_axis=0, concat_axis=1, tiled=True),
        lax.all_to_all(sent_counts, "expert", split_axis=0, concat_axis=1, tiled=True),
    )
    projected = jnp.einsum("erd,egfd->ergf", arrived, gate_up, preferred_element_type=jnp.float32)
    hidden = (jax.nn.silu(projected[:, :, 0]) * projected[:, :, 1]).astype(jnp.bfloat16)
    part_rows = lax.all_gather(hidden, "hidden", axis=2, tiled=True)
    columns = jnp.einsum("erf,erg->efg", hidden, part_rows, preferred_element_type=jnp.float32)
    out_part = jnp.einsum("erg,egd->erd", part_rows, down_proj, preferred_element_type=jnp.float32)
    routed = jnp.sum(arrived_counts.astype(jnp.float32), axis=1)
    hessian = columns * (2.0 / routed)[:, None, None]
    returned = lax.all_to_all(
        out_part.astype(jnp.bfloat16), "expert", split_axis=1, concat_axis=0, tiled=True
    )
    feature_dev = returned.shape[2]
    picked = returned.reshape(all_experts * capacity, feature_dev)[target].reshape(
        token_count, route_top, feature_dev
    )
    route_share = route_weights / jnp.sum(route_weights, axis=1, keepdims=True)
    layer_out = jnp.einsum("tk,tkd->td", route_share, picked.astype(jnp.float32))
    return (layer_out.astype(jnp.bfloat16), hessian)


def solution(mesh):
    return jax.shard_map(
        body,
        mesh=mesh,
        in_specs=(
            P("expert", "hidden"),
            P("expert", None),
            P("expert", None),
            P("expert", None, "hidden", None),
            P("expert", None, "hidden"),
        ),
        out_specs=(P("expert", "hidden"), P("expert", "hidden", None)),
        check_vma=False,
    )
```

profile of v0, /device:TPU:1, one launch (start us, length us, event | category | flops | bytes accessed | tf_op | source)
XLA Modules:
  0.0 558.3 jit_solution(3473041793414133790)
XLA Ops:
  7.2 0.0 copy-start
  7.2 0.0 all-gather.2.cloned.1.call-start
  7.2 0.9 copy.23
  8.1 0.1 eq.39
  8.2 0.1 reshape.244
  8.3 1.2 reduce-window.6
  9.5 0.2 slice_reduce_fusion
  9.8 0.2 convert_reduce_fusion
  10.0 0.2 fusion.2
  10.2 0.2 select_reduce_fusion
  10.5 20.0 %all_gather.6 = bf16[64,4096]{1,0:T(8,128)(2,1)S(1)} all-gather(bf16[64,512]{1,0:T(8,128)(2,1)} %param.5), channel_id=1, replica_groups=mesh['expert'=64,'hidden'=8] {'hidden'}, dimensions={1}, use_global_device_ids=true | all-gather | bytes 589824 | tf_op jit(solution)/shard_map/all_gather | solution.py:29
  30.5 5.7 %gather_fusion = bf16[768,4096]{1,0:T(8,128)(2,1)} fusion(bf16[64,4096]{1,0:T(8,128)(2,1)S(1)} %all_gather.6, s32[1024]{0:T(1024)S(1)} %pad_clamp_fusion.1), kind=kCustom, calls=%fused_computation | custom fusion | bytes 12585984 | tf_op jit(solution)/shard_map/gather | solution.py:30
  36.3 9.7 %gather.9 = bf16[64,12,4096]{2,1,0:T(8,128)(2,1)} reshape(bf16[768,4096]{1,0:T(8,128)(2,1)} %gather_fusion) | data formatting | bytes 12582912 | tf_op jit(solution)/shard_map/gather | solution.py:30
  46.0 0.1 broadcast_in_dim.35
  46.1 7.2 %broadcast_select_fusion = bf16[64,12,4096]{2,1,0:T(8,128)(2,1)} fusion(bf16[64,12,4096]{2,1,0:T(8,128)(2,1)} %gather.9, pred[64,12]{1,0:T(8,128)(4,1)S(1)} %broadcast_in_dim.35), kind=kLoop, calls=%fused_computation.2 | loop fusion | flops 3145728 | bytes 12583680 | tf_op jit(solution)/shard_map/jit(_where)/select_n | solution.py:30
  53.3 375.2 %all_to_all.13 = bf16[64,12,4096]{2,1,0:T(8,128)(2,1)} all-to-all(bf16[64,12,4096]{2,1,0:T(8,128)(2,1)} %broadcast_select_fusion), channel_id=1, replica_groups=mesh['expert'=64,'hidden'=8] {'expert'}, dimensions={0} | all-to-all | bytes 12582912 | tf_op jit(solution)/shard_map/all_to_all | solution.py:34
  428.6 9.9 %reshape.268 = bf16[768,4096,1]{1,0,2:T(8,128)(2,1)} reshape(bf16[64,12,4096]{2,1,0:T(8,128)(2,1)} %all_to_all.13) | data formatting | bytes 12582912 | tf_op jit(solution)/shard_map/reshape.10
  438.4 0.0 copy-done
  438.5 5.1 fusion.4
  443.5 0.0 copy-start.1
  443.5 0.8 copy-done.1
  444.4 0.7 fusion.19
  445.1 0.0 all-gather.2.cloned.1.call-update
  445.1 0.7 copy.28
  445.9 13.8 %all-to-all-start.2 = ((bf16[64,1,1]{2,1,0:T(2,128)(2,1)}), bf16[64,1,1]{2,1,0:T(2,128)(2,1)S(1)}, u32[]{:S(2)}, u32[]{:S(2)}) async-start(bf16[64,1,1]{2,1,0:T(2,128)(2,1)} %copy.28), calls=%async_computation.2 | async-start | bytes 65536 | tf_op jit(solution)/shard_map/all_to_all | solution.py:35
  459.7 16.2 %all-gather.2.cloned.1.call-done = bf16[1,768,768]{1,2,0:T(8,128)(2,1)} async-done(((bf16[1,768,96]{1,2,0:T(8,128)(2,1)}), bf16[1,768,768]{1,2,0:T(8,128)(2,1)}) %all-gather.2.cloned.1.call-update) | async-done | bytes 1179664 | tf_op jit(solution)/shard_map/all_gather | solution.py:39
  475.9 0.0 copy-done.5
  475.9 2.1 fusion.3
  478.0 1.2 copy.39
  479.2 0.5 broadcast.135
  479.7 6.3 %reduce.6 = bf16[768,512]{1,0:T(8,128)(2,1)} reduce(bf16[768,1,512]{2,1,0:T(2,128)(2,1)S(1)} %bitcast.76, bf16[]{:T(256)} %broadcast.135), dimensions={1}, to_apply=%bitcast.74.reduce_sub_computation | reduce | bytes 1572866
  486.0 3.2 reshape.274
  489.2 0.0 all-to-all-done.2
  489.2 15.4 %all-to-all-start.1 = ((bf16[64,2,3072]{2,1,0:T(2,128)(2,1)}), bf16[64,2,3072]{2,1,0:T(2,128)(2,1)S(1)}, u32[]{:S(2)}, u32[]{:S(2)}) async-start(bf16[64,2,3072]{2,1,0:T(2,128)(2,1)} %reshape.274), calls=%async_computation.1 | async-start | bytes 1572864 | tf_op jit(solution)/shard_map/all_to_all | solution.py:44
  504.6 0.0 copy-done.3
  504.6 0.1 copy.27
  504.7 0.1 mul.76
  504.8 0.0 copy-done.4
  504.9 0.1 copy.29
  505.0 0.7 convert_reduce_fusion.1
  506.4 0.0 copy-done.2
  506.4 2.5 fusion.13
  508.8 36.1 %all-to-all-done.1 = bf16[64,2,3072]{2,1,0:T(2,128)(2,1)S(1)} async-done(((bf16[64,2,3072]{2,1,0:T(2,128)(2,1)}), bf16[64,2,3072]{2,1,0:T(2,128)(2,1)S(1)}, u32[]{:S(2)}, u32[]{:S(2)}) %all-to-all-start.1) | async-done | bytes 786464 | tf_op jit(solution)/shard_map/all_to_all | solution.py:44
  544.9 2.0 reshape.275
  546.9 1.6 copy.37
  548.5 2.0 gather_fusion.1
  550.5 0.3 fusion.17
  550.8 0.6 copy.38
  (17 shorter events, 0.1 us)
Async XLA Ops:
  7.2 431.3 %copy-start = (bf16[1,2,96,4096]{3,2,1,0:T(8,128)(2,1)S(1)}, bf16[1,2,96,4096]{3,2,1,0:T(8,128)(2,1)}, u32[]{:S(2)}) copy-start(bf16[1,2,96,4096]{3,2,1,0:T(8,128)(2,1)} %param.8) | copy-start | bytes 4718596
  7.2 468.7 %all-gather.2.cloned.1.call-start = ((), (), s32[]{:S(2)}) async-start(), calls=%async_computation.3 | async-start | bytes 1327104 | tf_op jit(solution)/shard_map/all_gather | solution.py:39
  438.5 37.5 %copy-start.5 = (bf16[1,768,512]{2,1,0:T(8,128)(2,1)S(1)}, bf16[1,768,512]{2,1,0:T(8,128)(2,1)}, u32[]{:S(2)}) copy-start(bf16[1,768,512]{2,1,0:T(8,128)(2,1)} %param.9) | copy-start | bytes 2359300
  443.5 0.8 copy-start.1
  445.9 43.4 %all-to-all-start.2 = ((bf16[64,1,1]{2,1,0:T(2,128)(2,1)}), bf16[64,1,1]{2,1,0:T(2,128)(2,1)S(1)}, u32[]{:S(2)}, u32[]{:S(2)}) async-start(bf16[64,1,1]{2,1,0:T(2,128)(2,1)} %copy.28), calls=%async_computation.2 | async-start | bytes 65536 | tf_op jit(solution)/shard_map/all_to_all | solution.py:35
  486.0 18.6 %copy-start.3 = (s32[64,8]{0,1:T(8,128)S(1)}, s32[64,8]{0,1:T(8,128)}, u32[]{:S(2)}) copy-start(s32[64,8]{0,1:T(8,128)} %param.6) | copy-start | bytes 6148
  486.0 18.8 %copy-start.4 = (f32[64,8]{0,1:T(8,128)S(1)}, f32[64,8]{0,1:T(8,128)}, u32[]{:S(2)}) copy-start(f32[64,8]{0,1:T(8,128)} %param.7) | copy-start | bytes 6148
  486.0 20.3 %copy-start.2 = (f32[1,768,2,96]{1,3,2,0:T(8,128)S(1)}, f32[1,768,2,96]{1,3,2,0:T(8,128)}, u32[]{:S(2)}) copy-start(f32[1,768,2,96]{1,3,2,0:T(8,128)} %copy-done.1) | copy-start | bytes 1769476
  489.2 55.7 %all-to-all-start.1 = ((bf16[64,2,3072]{2,1,0:T(2,128)(2,1)}), bf16[64,2,3072]{2,1,0:T(2,128)(2,1)S(1)}, u32[]{:S(2)}, u32[]{:S(2)}) async-start(bf16[64,2,3072]{2,1,0:T(2,128)(2,1)} %reshape.274), calls=%async_computation.1 | async-start | bytes 1572864 | tf_op jit(solution)/shard_map/all_to_all | solution.py:44
Sparse Core Ops, SparseCore 0:
  445.3 30.6 all-gather.1
where the time goes:
time: 561 us; the launch traced here: 558 us
  blocking collectives  395 us (70%)
  waiting for transfers between devices  52.3 us (9%)
  local copies, waits for them, and re-layouts  39.7 us (7%)
  starting transfers between devices  29.2 us (5%)
  other arithmetic  16.9 us (3%)
  between operations  14.9 us (3%)
  matrix products  9.91 us (2%)
    all_to_all x1, blocking collectives, body(): lax.all_to_all(outgoing, 'expert', split_axis=0, concat_axis=1, tiled=True)  375 us
    all_to_all x1, waiting for transfers between devices, body(): lax.all_to_all(out_part.astype(jnp.bfloat16), 'expert', split_axis=1, con...  36.1 us
    all_gather x1, blocking collectives, body(): features = lax.all_gather(tokens, 'hidden', axis=1, tiled=True)  20 us
    all_gather x1, waiting for transfers between devices, body(): part_rows = lax.all_gather(hidden, 'hidden', axis=2, tiled=True)  16.2 us
    gather x2, local copies, waits for them, and re-layouts, body(): features[source_row]  15.5 us
    all_to_all x1, starting transfers between devices, body(): lax.all_to_all(out_part.astype(jnp.bfloat16), 'expert', split_axis=1, con...  15.4 us
    all_to_all x1, starting transfers between devices, body(): lax.all_to_all(sent_counts, 'expert', split_axis=0, concat_axis=1, tiled=...  13.8 us
  transfers between devices with their start and end apart: 3, of which 2 were waited for; matrix products, arithmetic and copies ran while one was open for 3% of the time, Pallas kernels for 0%

commit v1 on v0

v1 whole, which is shorter than its diff:
```python
import jax
import jax.numpy as jnp
from jax import lax
from jax.experimental import pallas as pl
from jax.experimental.pallas import tpu as pltpu
from jax.sharding import PartitionSpec as P

BF = jnp.bfloat16
F32 = jnp.float32
I32 = jnp.int32

TOK = 64
TOP = 8
EXPERTS = 64
CAP = 12
LANES = 128
SLABS = 4
PACK = SLABS * CAP
GROUP = 8
GROWS = GROUP * CAP
GPACK = GROUP * PACK
CHIPS = 4
ROWS = EXPERTS * CAP
UNITS = 96
EMPTY = 64.0
NT = (((1,), (1,)), ((), ()))
TN = (((0,), (0,)), ((), ()))


def dot(a, b, dims=(((1,), (0,)), ((), ()))):
    return lax.dot_general(a, b, dims, preferred_element_type=F32)


def iota(shape, dim):
    return lax.broadcasted_iota(I32, shape, dim)


def codes(ids, shares=None):
    wide = SLABS * TOK
    expert = iota((EXPERTS, wide), 0)
    member = jnp.zeros((EXPERTS, wide), F32)
    weight = jnp.zeros((EXPERTS, wide), F32)
    for k in range(TOP):
        hit = ids[k : k + 1, :] == expert
        member = member + jnp.where(hit, 1.0, 0.0)
        if shares is not None:
            weight = weight + jnp.where(hit, shares[k : k + 1, :], 0.0)
    row, col = iota((wide, wide), 0), iota((wide, wide), 1)
    before = jnp.where((row < TOK) & (row < (col & (TOK - 1))), 1.0, 0.0).astype(BF)
    slot = dot(member.astype(BF), before)
    slab = (iota((EXPERTS, wide), 1) >> 6).astype(F32)
    code = jnp.where(member > 0.5, slot + 16.0 * slab, -1.0)
    return code, member, weight


def pack_kernel(tok_ref, ids_ref, out_ref):
    code, member, _ = codes(ids_ref[...])
    wide = SLABS * TOK
    ones = jnp.where(iota((wide, LANES), 0) < TOK, 1.0, 0.0).astype(BF)
    count = dot(member.astype(BF), ones)
    tok = tok_ref[...]
    slabs = jnp.concatenate([tok[:, l * LANES : (l + 1) * LANES] for l in range(SLABS)], axis=0)
    p = iota((PACK, wide), 0)
    slab = (p >= CAP).astype(I32) + (p >= 2 * CAP).astype(I32) + (p >= 3 * CAP).astype(I32)
    target = (p + 4 * slab).astype(F32)
    q = iota((PACK, LANES), 0)
    first = jnp.where(q < CAP, q, -1).astype(F32)
    for c in range(EXPERTS // GROUP):
        picks = [
            jnp.where(code[e : e + 1, :] == target, 1.0, 0.0).astype(BF)
            for e in range(c * GROUP, (c + 1) * GROUP)
        ]
        rows = dot(jnp.concatenate(picks, axis=0), slabs)
        for j in range(GROUP):
            e = c * GROUP + j
            block = rows[j * PACK : (j + 1) * PACK]
            out_ref[e] = jnp.where(first >= count[e : e + 1, :], EMPTY, block).astype(BF)


def unpack_matrix():
    out, src = iota((GPACK, GPACK), 0), iota((GPACK, GPACK), 1)
    l, rest = out // GROWS, out % GROWS
    return jnp.where(src == (rest // CAP) * PACK + l * CAP + rest % CAP, 1.0, 0.0).astype(BF)


def up_kernel(place_ref, a_ref, b_ref, w0_ref, w1_ref, w2_ref, w3_ref, perm_ref, out_ref, scale_ref, wa, wb):
    x, c = place_ref[0], place_ref[1]
    half = SLABS * LANES
    own = pl.multiple_of(c * half, half)
    other = pl.multiple_of((1 - c) * half, half)
    for k, w_ref in enumerate((w0_ref, w1_ref, w2_ref, w3_ref)):
        at = pl.multiple_of(((x + CHIPS - k) % CHIPS) * UNITS, 32)
        for g in range(2):
            wa[pl.ds(at + g * CHIPS * UNITS, UNITS), :] = w_ref[g * UNITS : (g + 1) * UNITS, pl.ds(own, half)]
            wb[pl.ds(at + g * CHIPS * UNITS, UNITS), :] = w_ref[g * UNITS : (g + 1) * UNITS, pl.ds(other, half)]
    perm = perm_ref[...]
    empty = jnp.zeros((GROWS, LANES), F32)

    def rows_of(block, empty):
        y = dot(perm, block.reshape(GPACK, LANES))
        first = y[:GROWS]
        gone = first > 0.5 * EMPTY
        empty = empty + jnp.where(gone, 1.0, 0.0)
        parts = [jnp.where(gone, 0.0, first)] + [y[l * GROWS : (l + 1) * GROWS] for l in range(1, SLABS)]
        return jnp.concatenate([part.astype(BF) for part in parts], axis=1), empty

    for g in range(EXPERTS // GROUP):
        own_rows, empty = rows_of(a_ref[g * GROUP : (g + 1) * GROUP], empty)
        other_rows, _ = rows_of(b_ref[g * GROUP : (g + 1) * GROUP], empty)
        part = dot(own_rows, wa[...], NT) + dot(other_rows, wb[...], NT)
        out_ref[g // 2, (g % 2) * GROWS : (g % 2 + 1) * GROWS, :] = part.astype(BF)
    gone = jnp.sum(empty, axis=0, keepdims=True)
    scale_ref[...] = jnp.broadcast_to(2.0 / (float(ROWS) - gone), scale_ref.shape)


def silu_kernel(in_ref, out_ref):
    total = in_ref[0].astype(F32)
    for k in range(1, CHIPS):
        total = total + in_ref[k].astype(F32)
    half = CHIPS * UNITS
    gate, up = total[:, :half], total[:, half:]
    out_ref[...] = (gate / (1.0 + jnp.exp(-gate)) * up).astype(BF)


def down_kernel(place_ref, own_ref, other_ref, down_ref, perm_ref, out_ref, da, db):
    c = place_ref[1]
    for i in range(CHIPS):
        mine = pl.multiple_of((2 * i + c) * UNITS, 32)
        theirs = pl.multiple_of((2 * i + 1 - c) * UNITS, 32)
        da[i * UNITS : (i + 1) * UNITS, :] = down_ref[pl.ds(mine, UNITS), :]
        db[i * UNITS : (i + 1) * UNITS, :] = down_ref[pl.ds(theirs, UNITS), :]
    perm = perm_ref[...]
    sources = EXPERTS // CHIPS
    for k in range(CHIPS):
        rows = (dot(own_ref[k], da[...]) + dot(other_ref[k], db[...])).astype(BF)
        for h in range(2):
            part = rows[h * GROWS : (h + 1) * GROWS]
            stack = jnp.concatenate([part[:, l * LANES : (l + 1) * LANES] for l in range(SLABS)], axis=0)
            packed = dot(perm, stack, TN).astype(BF).reshape(GROUP, PACK, LANES)
            out_ref[k * sources + h * GROUP : k * sources + (h + 1) * GROUP] = packed


def gram_kernel(place_ref, own_ref, other_ref, scale_ref, out_ref, acc):
    x, c = place_ref[0], place_ref[1]
    half = CHIPS * UNITS
    row, col = iota((half, 2 * half), 0), iota((half, 2 * half), 1)
    even = row + UNITS * (row // UNITS)
    put_own = jnp.where(col == even + UNITS * c, 1.0, 0.0).astype(BF)
    put_other = jnp.where(col == even + UNITS * (1 - c), 1.0, 0.0).astype(BF)
    for k in range(CHIPS):
        own = own_ref[k]
        every = (dot(own, put_own) + dot(other_ref[k], put_other)).astype(BF)
        gram = dot(own, every, TN)
        acc[...] = gram if k == 0 else acc[...] + gram
    mine = acc[pl.ds(pl.multiple_of(x * UNITS, 32), UNITS), :]
    out_ref[...] = mine * scale_ref[0:1, 0:1]


def combine_kernel(ids_ref, weights_ref, in_ref, out_ref):
    weights = weights_ref[...]
    shares = weights / jnp.sum(weights, axis=0, keepdims=True)
    code, _, share = codes(ids_ref[...], shares)
    code, share = code.astype(BF), share.astype(BF)
    total = jnp.zeros((SLABS * TOK, LANES), F32)
    for g in range(EXPERTS // GROUP):
        q = iota((EXPERTS, GPACK), 1)
        e = iota((EXPERTS, GPACK), 0) - g * GROUP
        spread = jnp.where((q >= e * PACK) & (q < (e + 1) * PACK), 1.0, 0.0).astype(BF)
        p = iota((SLABS * TOK, GPACK), 1) % PACK
        slab = (p >= CAP).astype(I32) + (p >= 2 * CAP).astype(I32) + (p >= 3 * CAP).astype(I32)
        target = (p + 4 * slab).astype(F32)
        pick = jnp.where(dot(code, spread, TN) == target, dot(share, spread, TN), 0.0).astype(BF)
        total = total + dot(pick, in_ref[g * GROUP : (g + 1) * GROUP].reshape(GPACK, LANES))
    out_ref[...] = jnp.concatenate(
        [total[l * TOK : (l + 1) * TOK] for l in range(SLABS)], axis=1
    ).astype(BF)


VMEM = pl.BlockSpec(memory_space=pltpu.VMEM)
SMEM = pl.BlockSpec(memory_space=pltpu.SMEM)


def call(kernel, outs, ins, scratch=(), smem=False, flops=0, size=0):
    return pl.pallas_call(
        kernel,
        out_shape=outs,
        in_specs=([SMEM] if smem else []) + [VMEM] * (len(ins) - int(smem)),
        out_specs=jax.tree.map(lambda _: VMEM, outs),
        scratch_shapes=list(scratch),
        compiler_params=pltpu.CompilerParams(vmem_limit_bytes=40 * 1024 * 1024),
        cost_estimate=pl.CostEstimate(flops=flops, bytes_accessed=size, transcendentals=0),
    )(*ins)


def shape(dims, dtype=BF):
    return jax.ShapeDtypeStruct(dims, dtype)


def body(tokens, route_ids, route_weights, gate_up, down_proj):
    place = lax.axis_index("hidden")
    x, c = place // 2, place % 2
    where = jnp.stack([x, c]).astype(I32)
    half = SLABS * LANES
    wide = 2 * half
    groups = [[2 * i + j for i in range(CHIPS)] for j in range(2)]
    swap = [(i, i ^ 1) for i in range(2 * CHIPS)]

    weights = gate_up.reshape(2 * UNITS, CHIPS * wide)
    pieces = []
    for k in range(CHIPS):
        piece = lax.dynamic_slice(weights, (0, ((x + k) % CHIPS) * wide), (2 * UNITS, wide))
        if k:
            piece = lax.ppermute(piece, "hidden", [(i, (i + 2 * k) % (2 * CHIPS)) for i in range(2 * CHIPS)])
        pieces.append(piece)

    ids = jnp.tile(route_ids.T, (1, SLABS))
    shares = jnp.tile(route_weights.T, (1, SLABS))
    perm = unpack_matrix()

    outgoing = call(pack_kernel, shape((EXPERTS, PACK, LANES)), (tokens, ids), flops=2 * 10**8, size=10**6)
    mine = lax.all_to_all(outgoing, "expert", 0, 0)
    theirs = lax.ppermute(mine, "hidden", swap)

    part, scale = call(
        up_kernel,
        (shape((CHIPS, ROWS // CHIPS, 2 * CHIPS * UNITS)), shape((8, LANES), F32)),
        (where, mine, theirs, *pieces, perm),
        (pltpu.VMEM((2 * CHIPS * UNITS, half), BF), pltpu.VMEM((2 * CHIPS * UNITS, half), BF)),
        smem=True,
        flops=2 * 10**9,
        size=5 * 10**6,
    )
    parts = lax.all_to_all(part, "hidden", 0, 0, axis_index_groups=groups)
    hidden = call(silu_kernel, shape((ROWS // CHIPS, CHIPS * UNITS)), (parts,), size=2 * 10**6)

    copies = jnp.broadcast_to(hidden[None], (CHIPS, *hidden.shape))
    own = lax.all_to_all(copies, "hidden", 0, 0, axis_index_groups=groups)
    other = lax.ppermute(own, "hidden", swap)

    returning = call(
        down_kernel,
        shape((EXPERTS, PACK, LANES)),
        (where, own, other, down_proj.reshape(ROWS, half), perm),
        (pltpu.VMEM((CHIPS * UNITS, half), BF), pltpu.VMEM((CHIPS * UNITS, half), BF)),
        smem=True,
        flops=10**9,
        size=4 * 10**6,
    )
    returned = lax.all_to_all(returning, "expert", 0, 0)
    hessian = call(
        gram_kernel,
        shape((UNITS, 2 * CHIPS * UNITS), F32),
        (where, own, other, scale),
        (pltpu.VMEM((CHIPS * UNITS, 2 * CHIPS * UNITS), F32),),
        smem=True,
        flops=2 * 10**9,
        size=3 * 10**6,
    )
    layer_out = call(combine_kernel, shape((TOK, half)), (ids, shares, returned), flops=4 * 10**8, size=10**6)
    return layer_out, hessian[None]


def solution(mesh):
    return jax.shard_map(
        body,
        mesh=mesh,
        in_specs=(
            P("expert", "hidden"),
            P("expert", None),
            P("expert", None),
            P("expert", None, "hidden", None),
            P("expert", None, "hidden"),
        ),
        out_specs=(P("expert", "hidden"), P("expert", "hidden", None)),
        check_vma=False,
    )
```

time: 561 us -> 193 us (0.34)
  blocking collectives: 395 us -> 29.9 us
  waiting for transfers between devices: 52.3 us -> 90.7 us
  local copies, waits for them, and re-layouts: 39.7 us -> 2.83 us
  Pallas kernels: 0 us -> 18.8 us
  starting transfers between devices: 29.2 us -> 47.2 us
  other arithmetic: 16.9 us -> 0.65 us
  between operations: 14.9 us -> 0.86 us
  matrix products: 9.91 us -> 0 us
    all_to_all x1 -> x2, blocking collectives: 375 us -> 29.9 us  [the longest x1 19.4 us: body(): parts = lax.all_to_all(part, 'hidden', 0, 0, axis_index_groups=groups)]
    all_to_all x2, waiting for transfers between devices: 36.1 us -> 75.6 us  [the longest x1 39.7 us: body(): mine = lax.all_to_all(outgoing, 'expert', 0, 0)]
    ppermute x0 -> x5, starting transfers between devices: none -> 21.4 us  [the longest x3 10.5 us: body(): lax.ppermute(piece, 'hidden', [(i, (i + 2 * k) % (2 * CHIPS)) for i in ra...]
    all_gather x1 -> x0, blocking collectives: 20 us -> none  [body(): features = lax.all_gather(tokens, 'hidden', axis=1, tiled=True)]
    pallas_call x0 -> x6, Pallas kernels: none -> 18.8 us  [call(): pl.pallas_call(kernel, out_shape=outs, in_specs=([SMEM] if smem else [])...]
    gather x3 -> x0, local copies, waits for them, and re-layouts: 17.4 us -> none  [the longest x2 15.5 us: body(): features[source_row]]
    all_gather x1 -> x0, waiting for transfers between devices: 16.2 us -> none  [body(): part_rows = lax.all_gather(hidden, 'hidden', axis=2, tiled=True)]
    ppermute x0 -> x5, waiting for transfers between devices: none -> 15.1 us  [the longest x3 13.4 us: body(): lax.ppermute(piece, 'hidden', [(i, (i + 2 * k) % (2 * CHIPS)) for i in ra...]
  transfers between devices with their start and end apart: 3 -> 7, of which waited for: 2 -> 6; matrix products, arithmetic and copies ran while one was open for 3% -> 1% of each run, Pallas kernels for 0% -> 2%
where the time goes in v1:
time: 193 us; the launch traced here: 191 us
  waiting for transfers between devices  90.7 us (47%)
  starting transfers between devices  47.2 us (24%)
  blocking collectives  29.9 us (15%)
  Pallas kernels  18.8 us (10%)
  local copies, waits for them, and re-layouts  2.83 us (1%)
    all_to_all x1, waiting for transfers between devices, body(): mine = lax.all_to_all(outgoing, 'expert', 0, 0)  39.7 us
    all_to_all x1, waiting for transfers between devices, body(): returned = lax.all_to_all(returning, 'expert', 0, 0)  35.9 us
    all_to_all x1, blocking collectives, body(): parts = lax.all_to_all(part, 'hidden', 0, 0, axis_index_groups=groups)  19.4 us
    all_to_all x1, starting transfers between devices, body(): mine = lax.all_to_all(outgoing, 'expert', 0, 0)  19.3 us
    pallas_call x6, Pallas kernels, call(): pl.pallas_call(kernel, out_shape=outs, in_specs=([SMEM] if smem else [])...  18.8 us
    ppermute x3, waiting for transfers between devices, body(): lax.ppermute(piece, 'hidden', [(i, (i + 2 * k) % (2 * CHIPS)) for i in ra...  13.4 us
    ppermute x3, starting transfers between devices, body(): lax.ppermute(piece, 'hidden', [(i, (i + 2 * k) % (2 * CHIPS)) for i in ra...  10.5 us
    all_to_all x1, blocking collectives, body(): own = lax.all_to_all(copies, 'hidden', 0, 0, axis_index_groups=groups)  10.5 us
  transfers between devices with their start and end apart: 7, of which 6 were waited for; matrix products, arithmetic and copies ran while one was open for 1% of the time, Pallas kernels for 2%

profile of v1, /device:TPU:1, one launch (start us, length us, event | category | flops | bytes accessed | tf_op | source)
XLA Modules:
  0.0 191.0 jit_solution(8497500448023755438)
XLA Ops:
  0.6 0.7 tile.8
  1.3 0.1 tile.9.ids_ref
  1.4 0.0 copy-start
  1.4 0.8 copy-done
  2.2 0.0 copy-start.2
  2.2 1.6 shard_map.68
  3.8 19.3 %all-to-all-start = ((bf16[64,48,128]{2,1,0:T(8,128)(2,1)}), bf16[64,48,128]{2,1,0:T(8,128)(2,1)S(1)}, u32[]{:S(2)}, u32[]{:S(2)}) async-start(bf16[64,48,128]{2,1,0:T(8,128)(2,1)} %shard_map.68), calls=%async_computation | async-start | bytes 1572864 | tf_op jit(solution)/shard_map/all_to_all | solution.py:221
  23.2 39.7 %all-to-all-done.a_ref = bf16[64,48,128]{2,1,0:T(8,128)(2,1)S(1)} async-done(((bf16[64,48,128]{2,1,0:T(8,128)(2,1)}), bf16[64,48,128]{2,1,0:T(8,128)(2,1)S(1)}, u32[]{:S(2)}, u32[]{:S(2)}) %all-to-all-start) | async-done | bytes 786464 | tf_op jit(solution)/shard_map/all_to_all | solution.py:221
  62.9 5.9 %collective-permute-start = (bf16[64,48,128]{2,1,0:T(8,128)(2,1)S(1)}, bf16[64,48,128]{2,1,0:T(8,128)(2,1)S(1)}, u32[]{:S(2)}, u32[]{:S(2)}) collective-permute-start(bf16[64,48,128]{2,1,0:T(8,128)(2,1)S(1)} %all-to-all-done.a_ref), channel_id=1, source_target_pairs={{0,1},{1,0},{2,3},{3,2},{4,5},{5,4},{6,7},{7,6},{8,9},{9,8},{10,11... | collective-permute-start | bytes 2359304 | tf_op jit(solution)/shard_map/ppermute | solution.py:222
  68.9 0.0 copy-done.2
  68.9 1.1 constant_dynamic-slice_fusion
  69.9 3.1 %collective-permute-start.1 = (bf16[192,1024]{1,0:T(8,128)(2,1)}, bf16[192,1024]{1,0:T(8,128)(2,1)S(1)}, u32[]{:S(2)}, u32[]{:S(2)}) collective-permute-start(bf16[192,1024]{1,0:T(8,128)(2,1)} %get-tuple-element.8), channel_id=1, source_target_pairs={{0,2},{1,3},{2,4},{3,5},{4,6},{5,7},{6,0},{7,1},{8,10},{9,11},{10,... | collective-permute-start | bytes 1179656 | tf_op jit(solution)/shard_map/ppermute | solution.py:213
  73.1 4.4 %collective-permute-start.2 = (bf16[192,1024]{1,0:T(8,128)(2,1)}, bf16[192,1024]{1,0:T(8,128)(2,1)S(1)}, u32[]{:S(2)}, u32[]{:S(2)}) collective-permute-start(bf16[192,1024]{1,0:T(8,128)(2,1)} %get-tuple-element.7), channel_id=1, source_target_pairs={{0,4},{1,5},{2,6},{3,7},{4,0},{5,1},{6,2},{7,3},{8,12},{9,13},{10,... | collective-permute-start | bytes 1179656 | tf_op jit(solution)/shard_map/ppermute | solution.py:213
  77.4 3.1 %collective-permute-start.3 = (bf16[192,1024]{1,0:T(8,128)(2,1)}, bf16[192,1024]{1,0:T(8,128)(2,1)S(1)}, u32[]{:S(2)}, u32[]{:S(2)}) collective-permute-start(bf16[192,1024]{1,0:T(8,128)(2,1)} %get-tuple-element.6), channel_id=1, source_target_pairs={{0,6},{1,7},{2,0},{3,1},{4,2},{5,3},{6,4},{7,5},{8,14},{9,15},{10,... | collective-permute-start | bytes 1179656 | tf_op jit(solution)/shard_map/ppermute | solution.py:213
  80.5 0.1 pad_add_fusion.place_ref
  80.6 0.5 select_convert_fusion.perm_ref
  81.2 2.8 %collective-permute-done.1.w1_ref = bf16[192,1024]{1,0:T(8,128)(2,1)S(1)} collective-permute-done((bf16[192,1024]{1,0:T(8,128)(2,1)}, bf16[192,1024]{1,0:T(8,128)(2,1)S(1)}, u32[]{:S(2)}, u32[]{:S(2)}) %collective-permute-start.1) | collective-permute-done | bytes 393248 | tf_op jit(solution)/shard_map/ppermute | solution.py:213
  84.0 9.4 %collective-permute-done.2.w2_ref = bf16[192,1024]{1,0:T(8,128)(2,1)S(1)} collective-permute-done((bf16[192,1024]{1,0:T(8,128)(2,1)}, bf16[192,1024]{1,0:T(8,128)(2,1)S(1)}, u32[]{:S(2)}, u32[]{:S(2)}) %collective-permute-start.2) | collective-permute-done | bytes 393248 | tf_op jit(solution)/shard_map/ppermute | solution.py:213
  93.4 1.2 collective-permute-done.3.w3_ref
  94.6 0.0 collective-permute-done.b_ref
  94.6 6.5 %shard_map.69 = (bf16[4,192,768]{2,1,0:T(8,128)(2,1)S(1)}, f32[8,128]{1,0:T(8,128)S(1)}) custom-call(s32[2]{0:T(128)S(1)} %pad_add_fusion.place_ref, bf16[64,48,128]{2,1,0:T(8,128)(2,1)S(1)} %all-to-all-done.a_ref, bf16[64,48,128]{2,1,0:T(8,128)(2,1)S(1)} %collective-permute-done.b_ref, bf16[192,1024]{1,0:T(8,128)(2,1)S(1)} %get-tuple-element.9.w0_ref, ...), custom_call_target="tpu_custom_call" | custom-call | flops 2000000000 | bytes 5000000 | tf_op jit(solution)/shard_map/pallas_call | solution.py:184
  101.2 19.4 %all_to_all.20.in_ref = bf16[4,192,768]{2,1,0:T(8,128)(2,1)S(1)} all-to-all(bf16[4,192,768]{2,1,0:T(8,128)(2,1)S(1)} %get-tuple-element.4), channel_id=1, replica_groups={{0,2,4,6},{1,3,5,7},{8,10,12,14},{9,11,13,15},{16,18,20,22},{17,19,21,2..., dimensions={0} | all-to-all | bytes 2359296 | tf_op jit(solution)/shard_map/all_to_all | solution.py:233
  120.5 0.0 copy-start.1
  120.5 0.2 shard_map.70
  120.8 0.1 broadcast_in_dim.19
  120.8 10.5 %all_to_all.21.own_ref = bf16[4,192,384]{2,1,0:T(8,128)(2,1)S(1)} all-to-all(bf16[4,192,384]{2,1,0:T(8,128)(2,1)S(1)} %broadcast_in_dim.19), channel_id=1, replica_groups={{0,2,4,6},{1,3,5,7},{8,10,12,14},{9,11,13,15},{16,18,20,22},{17,19,21,2..., dimensions={0} | all-to-all | bytes 1179648 | tf_op jit(solution)/shard_map/all_to_all | solution.py:237
  131.3 4.9 %collective-permute-start.4 = (bf16[4,192,384]{2,1,0:T(8,128)(2,1)S(1)}, bf16[4,192,384]{2,1,0:T(8,128)(2,1)S(1)}, u32[]{:S(2)}, u32[]{:S(2)}) collective-permute-start(bf16[4,192,384]{2,1,0:T(8,128)(2,1)S(1)} %all_to_all.21.own_ref), channel_id=1, source_target_pairs={{0,1},{1,0},{2,3},{3,2},{4,5},{5,4},{6,7},{7,6},{8,9},{9,8},{10,11... | collective-permute-start | bytes 1769480 | tf_op jit(solution)/shard_map/ppermute | solution.py:238
  136.2 1.6 collective-permute-done.4.other_ref
  137.9 0.0 copy-done.1
  137.9 3.5 %shard_map.71 = bf16[64,48,128]{2,1,0:T(8,128)(2,1)} custom-call(s32[2]{0:T(128)S(1)} %pad_add_fusion.place_ref, bf16[4,192,384]{2,1,0:T(8,128)(2,1)S(1)} %all_to_all.21.own_ref, bf16[4,192,384]{2,1,0:T(8,128)(2,1)S(1)} %collective-permute-done.4.other_ref, bf16[768,512]{1,0:T(8,128)(2,1)S(1)} %bitcast.7, bf16[384,384]{1,0:T(8,128)(2,1)S(1)} %select_convert_fusion.perm_ref), custom_call_target="tpu_custom_call" | custom-call | flops 1000000000 | bytes 4000000 | tf_op jit(solution)/shard_map/pallas_call | solution.py:184
  141.4 0.0 copy-start.3
  141.4 6.5 %all-to-all-start.3 = ((bf16[64,48,128]{2,1,0:T(8,128)(2,1)}), bf16[64,48,128]{2,1,0:T(8,128)(2,1)S(1)}, u32[]{:S(2)}, u32[]{:S(2)}) async-start(bf16[64,48,128]{2,1,0:T(8,128)(2,1)} %shard_map.71), calls=%async_computation.3 | async-start | bytes 1572864 | tf_op jit(solution)/shard_map/all_to_all | solution.py:249
  148.0 0.0 copy-done.3
  148.0 0.1 tile.21.weights_ref
  148.1 4.2 %shard_map.73 = f32[96,768]{1,0:T(8,128)} custom-call(s32[2]{0:T(128)S(1)} %pad_add_fusion.place_ref, bf16[4,192,384]{2,1,0:T(8,128)(2,1)S(1)} %all_to_all.21.own_ref, bf16[4,192,384]{2,1,0:T(8,128)(2,1)S(1)} %collective-permute-done.4.other_ref, f32[8,128]{1,0:T(8,128)S(1)} %get-tuple-element.5.scale_ref), custom_call_target="tpu_custom_call" | custom-call | flops 2000000000 | bytes 3000000 | tf_op jit(solution)/shard_map/pallas_call | solution.py:184
  152.2 35.9 %all-to-all-done.3.in_ref = bf16[64,48,128]{2,1,0:T(8,128)(2,1)S(1)} async-done(((bf16[64,48,128]{2,1,0:T(8,128)(2,1)}), bf16[64,48,128]{2,1,0:T(8,128)(2,1)S(1)}, u32[]{:S(2)}, u32[]{:S(2)}) %all-to-all-start.3) | async-done | bytes 786464 | tf_op jit(solution)/shard_map/all_to_all | solution.py:249
  188.1 2.8 %shard_map.72 = bf16[64,512]{1,0:T(8,128)(2,1)} custom-call(s32[8,256]{1,0:T(8,128)S(1)} %tile.9.ids_ref, f32[8,256]{1,0:T(8,128)S(1)} %tile.21.weights_ref, bf16[64,48,128]{2,1,0:T(8,128)(2,1)S(1)} %all-to-all-done.3.in_ref), custom_call_target="tpu_custom_call" | custom-call | flops 400000000 | bytes 1000000 | tf_op jit(solution)/shard_map/pallas_call | solution.py:184
  (4 shorter events, 0.0 us)
Async XLA Ops:
  1.4 0.8 copy-start
  2.2 66.6 %copy-start.2 = (bf16[1,2,96,4096]{3,2,1,0:T(8,128)(2,1)S(1)}, bf16[1,2,96,4096]{3,2,1,0:T(8,128)(2,1)}, u32[]{:S(2)}) copy-start(bf16[1,2,96,4096]{3,2,1,0:T(8,128)(2,1)} %param.8) | copy-start | bytes 4718596
  3.8 59.1 %all-to-all-start = ((bf16[64,48,128]{2,1,0:T(8,128)(2,1)}), bf16[64,48,128]{2,1,0:T(8,128)(2,1)S(1)}, u32[]{:S(2)}, u32[]{:S(2)}) async-start(bf16[64,48,128]{2,1,0:T(8,128)(2,1)} %shard_map.68), calls=%async_computation | async-start | bytes 1572864 | tf_op jit(solution)/shard_map/all_to_all | solution.py:221
  62.9 31.7 %collective-permute-start = (bf16[64,48,128]{2,1,0:T(8,128)(2,1)S(1)}, bf16[64,48,128]{2,1,0:T(8,128)(2,1)S(1)}, u32[]{:S(2)}, u32[]{:S(2)}) collective-permute-start(bf16[64,48,128]{2,1,0:T(8,128)(2,1)S(1)} %all-to-all-done.a_ref), channel_id=1, source_target_pairs={{0,1},{1,0},{2,3},{3,2},{4,5},{5,4},{6,7},{7,6},{8,9},{9,8},{10,11... | collective-permute-start | bytes 2359304 | tf_op jit(solution)/shard_map/ppermute | solution.py:222
  69.9 14.0 %collective-permute-start.1 = (bf16[192,1024]{1,0:T(8,128)(2,1)}, bf16[192,1024]{1,0:T(8,128)(2,1)S(1)}, u32[]{:S(2)}, u32[]{:S(2)}) collective-permute-start(bf16[192,1024]{1,0:T(8,128)(2,1)} %get-tuple-element.8), channel_id=1, source_target_pairs={{0,2},{1,3},{2,4},{3,5},{4,6},{5,7},{6,0},{7,1},{8,10},{9,11},{10,... | collective-permute-start | bytes 1179656 | tf_op jit(solution)/shard_map/ppermute | solution.py:213
  73.1 20.3 %collective-permute-start.2 = (bf16[192,1024]{1,0:T(8,128)(2,1)}, bf16[192,1024]{1,0:T(8,128)(2,1)S(1)}, u32[]{:S(2)}, u32[]{:S(2)}) collective-permute-start(bf16[192,1024]{1,0:T(8,128)(2,1)} %get-tuple-element.7), channel_id=1, source_target_pairs={{0,4},{1,5},{2,6},{3,7},{4,0},{5,1},{6,2},{7,3},{8,12},{9,13},{10,... | collective-permute-start | bytes 1179656 | tf_op jit(solution)/shard_map/ppermute | solution.py:213
  77.4 17.2 %collective-permute-start.3 = (bf16[192,1024]{1,0:T(8,128)(2,1)}, bf16[192,1024]{1,0:T(8,128)(2,1)S(1)}, u32[]{:S(2)}, u32[]{:S(2)}) collective-permute-start(bf16[192,1024]{1,0:T(8,128)(2,1)} %get-tuple-element.6), channel_id=1, source_target_pairs={{0,6},{1,7},{2,0},{3,1},{4,2},{5,3},{6,4},{7,5},{8,14},{9,15},{10,... | collective-permute-start | bytes 1179656 | tf_op jit(solution)/shard_map/ppermute | solution.py:213
  120.5 17.3 %copy-start.1 = (bf16[1,768,512]{2,1,0:T(8,128)(2,1)S(1)}, bf16[1,768,512]{2,1,0:T(8,128)(2,1)}, u32[]{:S(2)}) copy-start(bf16[1,768,512]{2,1,0:T(8,128)(2,1)} %param.9) | copy-start | bytes 2359300
  131.3 6.5 %collective-permute-start.4 = (bf16[4,192,384]{2,1,0:T(8,128)(2,1)S(1)}, bf16[4,192,384]{2,1,0:T(8,128)(2,1)S(1)}, u32[]{:S(2)}, u32[]{:S(2)}) collective-permute-start(bf16[4,192,384]{2,1,0:T(8,128)(2,1)S(1)} %all_to_all.21.own_ref), channel_id=1, source_target_pairs={{0,1},{1,0},{2,3},{3,2},{4,5},{5,4},{6,7},{7,6},{8,9},{9,8},{10,11... | collective-permute-start | bytes 1769480 | tf_op jit(solution)/shard_map/ppermute | solution.py:238
  141.4 6.6 %copy-start.3 = (f32[64,8]{0,1:T(8,128)S(1)}, f32[64,8]{0,1:T(8,128)}, u32[]{:S(2)}) copy-start(f32[64,8]{0,1:T(8,128)} %param.7) | copy-start | bytes 6148
  141.4 46.7 %all-to-all-start.3 = ((bf16[64,48,128]{2,1,0:T(8,128)(2,1)}), bf16[64,48,128]{2,1,0:T(8,128)(2,1)S(1)}, u32[]{:S(2)}, u32[]{:S(2)}) async-start(bf16[64,48,128]{2,1,0:T(8,128)(2,1)} %shard_map.71), calls=%async_computation.3 | async-start | bytes 1572864 | tf_op jit(solution)/shard_map/all_to_all | solution.py:249

commit v2 on v1

--- a/solution.py
+++ b/solution.py
@@ -37,6 +37,10 @@
 
 def codes(ids, shares=None):
     wide = SLABS * TOK
+    copies = jnp.where((iota((TOK, wide), 1) & (TOK - 1)) == iota((TOK, wide), 0), 1.0, 0.0).astype(BF)
+    ids = dot(ids.astype(F32).astype(BF), copies).astype(I32)
+    if shares is not None:
+        shares = dot(shares.astype(BF), copies)
     expert = iota((EXPERTS, wide), 0)
     member = jnp.zeros((EXPERTS, wide), F32)
     weight = jnp.zeros((EXPERTS, wide), F32)
@@ -53,11 +57,17 @@
     return code, member, weight
 
 
-def pack_kernel(tok_ref, ids_ref, out_ref):
+def pack_kernel(tok_hbm, ids_hbm, out_ref, tok_ref, ids_ref, tok_sem, ids_sem):
+    fetch_ids = pltpu.make_async_copy(ids_hbm, ids_ref, ids_sem)
+    fetch_ids.start()
+    fetch = pltpu.make_async_copy(tok_hbm, tok_ref, tok_sem)
+    fetch.start()
+    fetch_ids.wait()
     code, member, _ = codes(ids_ref[...])
     wide = SLABS * TOK
     ones = jnp.where(iota((wide, LANES), 0) < TOK, 1.0, 0.0).astype(BF)
     count = dot(member.astype(BF), ones)
+    fetch.wait()
     tok = tok_ref[...]
     slabs = jnp.concatenate([tok[:, l * LANES : (l + 1) * LANES] for l in range(SLABS)], axis=0)
     p = iota((PACK, wide), 0)
@@ -77,13 +87,20 @@
             out_ref[e] = jnp.where(first >= count[e : e + 1, :], EMPTY, block).astype(BF)
 
 
-def unpack_matrix():
-    out, src = iota((GPACK, GPACK), 0), iota((GPACK, GPACK), 1)
-    l, rest = out // GROWS, out % GROWS
-    return jnp.where(src == (rest // CAP) * PACK + l * CAP + rest % CAP, 1.0, 0.0).astype(BF)
-
-
-def up_kernel(place_ref, a_ref, b_ref, w0_ref, w1_ref, w2_ref, w3_ref, perm_ref, out_ref, scale_ref, wa, wb):
+def repack_matrix(packs):
+    loose = iota((GPACK, LANES), 0)
+    slab = sum((loose >= l * GROWS).astype(I32) for l in range(1, SLABS))
+    rest = loose - slab * GROWS
+    source = sum((rest >= j * CAP).astype(I32) for j in range(1, GROUP))
+    place = source * (PACK - CAP) + slab * CAP + rest
+    parts = [
+        jnp.where(place == iota((GPACK, LANES), 1) + j * LANES, 1.0, 0.0) for j in range(GPACK // LANES)
+    ]
+    matrix = jnp.concatenate(parts, axis=1)
+    return (matrix.T if packs else matrix).astype(BF)
+
+
+def weights_kernel(place_ref, w0_ref, w1_ref, w2_ref, w3_ref, down_ref, wa, wb, da, db, ready_ref):
     x, c = place_ref[0], place_ref[1]
     half = SLABS * LANES
     own = pl.multiple_of(c * half, half)
@@ -93,24 +110,37 @@
         for g in range(2):
             wa[pl.ds(at + g * CHIPS * UNITS, UNITS), :] = w_ref[g * UNITS : (g + 1) * UNITS, pl.ds(own, half)]
             wb[pl.ds(at + g * CHIPS * UNITS, UNITS), :] = w_ref[g * UNITS : (g + 1) * UNITS, pl.ds(other, half)]
-    perm = perm_ref[...]
+    for i in range(CHIPS):
+        mine = pl.multiple_of((2 * i + c) * UNITS, 32)
+        theirs = pl.multiple_of((2 * i + 1 - c) * UNITS, 32)
+        da[i * UNITS : (i + 1) * UNITS, :] = down_ref[pl.ds(mine, UNITS), :]
+        db[i * UNITS : (i + 1) * UNITS, :] = down_ref[pl.ds(theirs, UNITS), :]
+    ready_ref[...] = jnp.zeros_like(ready_ref)
+
+
+def unpack_kernel(in_ref, rows_ref, scale_ref):
+    perm = repack_matrix(False)
     empty = jnp.zeros((GROWS, LANES), F32)
-
-    def rows_of(block, empty):
-        y = dot(perm, block.reshape(GPACK, LANES))
+    for g in range(EXPERTS // GROUP):
+        y = dot(perm, in_ref[g * GROUP : (g + 1) * GROUP].reshape(GPACK, LANES))
         first = y[:GROWS]
         gone = first > 0.5 * EMPTY
         empty = empty + jnp.where(gone, 1.0, 0.0)
         parts = [jnp.where(gone, 0.0, first)] + [y[l * GROWS : (l + 1) * GROWS] for l in range(1, SLABS)]
-        return jnp.concatenate([part.astype(BF) for part in parts], axis=1), empty
-
-    for g in range(EXPERTS // GROUP):
-        own_rows, empty = rows_of(a_ref[g * GROUP : (g + 1) * GROUP], empty)
-        other_rows, _ = rows_of(b_ref[g * GROUP : (g + 1) * GROUP], empty)
-        part = dot(own_rows, wa[...], NT) + dot(other_rows, wb[...], NT)
-        out_ref[g // 2, (g % 2) * GROWS : (g % 2 + 1) * GROWS, :] = part.astype(BF)
+        rows_ref[g * GROWS : (g + 1) * GROWS, :] = jnp.concatenate([part.astype(BF) for part in parts], axis=1)
     gone = jnp.sum(empty, axis=0, keepdims=True)
     scale_ref[...] = jnp.broadcast_to(2.0 / (float(ROWS) - gone), scale_ref.shape)
+
+
+def own_kernel(rows_ref, w_ref, out_ref):
+    out_ref[...] = dot(rows_ref[...], w_ref[...], NT)
+
+
+def other_kernel(rows_ref, w_ref, part_ref, out_ref):
+    rows = ROWS // CHIPS
+    for i in range(CHIPS):
+        at = slice(i * rows, (i + 1) * rows)
+        out_ref[i] = (part_ref[at, :] + dot(rows_ref[at, :], w_ref[...], NT)).astype(BF)
 
 
 def silu_kernel(in_ref, out_ref):
@@ -122,21 +152,21 @@
     out_ref[...] = (gate / (1.0 + jnp.exp(-gate)) * up).astype(BF)
 
 
-def down_kernel(place_ref, own_ref, other_ref, down_ref, perm_ref, out_ref, da, db):
-    c = place_ref[1]
-    for i in range(CHIPS):
-        mine = pl.multiple_of((2 * i + c) * UNITS, 32)
-        theirs = pl.multiple_of((2 * i + 1 - c) * UNITS, 32)
-        da[i * UNITS : (i + 1) * UNITS, :] = down_ref[pl.ds(mine, UNITS), :]
-        db[i * UNITS : (i + 1) * UNITS, :] = down_ref[pl.ds(theirs, UNITS), :]
+def down_own_kernel(hidden_ref, down_ref, out_ref, perm_ref):
+    perm_ref[...] = repack_matrix(True)
+    for k in range(CHIPS):
+        out_ref[k] = dot(hidden_ref[k], down_ref[...])
+
+
+def down_other_kernel(hidden_ref, down_ref, part_ref, perm_ref, out_ref):
     perm = perm_ref[...]
     sources = EXPERTS // CHIPS
     for k in range(CHIPS):
-        rows = (dot(own_ref[k], da[...]) + dot(other_ref[k], db[...])).astype(BF)
+        rows = (part_ref[k] + dot(hidden_ref[k], down_ref[...])).astype(BF)
         for h in range(2):
             part = rows[h * GROWS : (h + 1) * GROWS]
             stack = jnp.concatenate([part[:, l * LANES : (l + 1) * LANES] for l in range(SLABS)], axis=0)
-            packed = dot(perm, stack, TN).astype(BF).reshape(GROUP, PACK, LANES)
+            packed = dot(perm, stack).astype(BF).reshape(GROUP, PACK, LANES)
             out_ref[k * sources + h * GROUP : k * sources + (h + 1) * GROUP] = packed
 
 
@@ -156,21 +186,25 @@
     out_ref[...] = mine * scale_ref[0:1, 0:1]
 
 
-def combine_kernel(ids_ref, weights_ref, in_ref, out_ref):
+def picks_kernel(ids_ref, weights_ref, out_ref):
     weights = weights_ref[...]
     shares = weights / jnp.sum(weights, axis=0, keepdims=True)
     code, _, share = codes(ids_ref[...], shares)
     code, share = code.astype(BF), share.astype(BF)
-    total = jnp.zeros((SLABS * TOK, LANES), F32)
+    wide = SLABS * TOK
+    p = iota((wide, GPACK), 1) % PACK
+    slab = (p >= CAP).astype(I32) + (p >= 2 * CAP).astype(I32) + (p >= 3 * CAP).astype(I32)
+    target = (p + 4 * slab).astype(F32)
+    q = iota((EXPERTS, GPACK), 1)
     for g in range(EXPERTS // GROUP):
-        q = iota((EXPERTS, GPACK), 1)
         e = iota((EXPERTS, GPACK), 0) - g * GROUP
         spread = jnp.where((q >= e * PACK) & (q < (e + 1) * PACK), 1.0, 0.0).astype(BF)
-        p = iota((SLABS * TOK, GPACK), 1) % PACK
-        slab = (p >= CAP).astype(I32) + (p >= 2 * CAP).astype(I32) + (p >= 3 * CAP).astype(I32)
-        target = (p + 4 * slab).astype(F32)
-        pick = jnp.where(dot(code, spread, TN) == target, dot(share, spread, TN), 0.0).astype(BF)
-        total = total + dot(pick, in_ref[g * GROUP : (g + 1) * GROUP].reshape(GPACK, LANES))
+        pick = jnp.where(dot(code, spread, TN) == target, dot(share, spread, TN), 0.0)
+        out_ref[:, g * GPACK : (g + 1) * GPACK] = pick.astype(BF)
+
+
+def combine_kernel(picks_ref, in_ref, out_ref):
+    total = dot(picks_ref[...], in_ref[...].reshape(EXPERTS * PACK, LANES))
     out_ref[...] = jnp.concatenate(
         [total[l * TOK : (l + 1) * TOK] for l in range(SLABS)], axis=1
     ).astype(BF)
@@ -178,18 +212,24 @@
 
 VMEM = pl.BlockSpec(memory_space=pltpu.VMEM)
 SMEM = pl.BlockSpec(memory_space=pltpu.SMEM)
-
-
-def call(kernel, outs, ins, scratch=(), smem=False, flops=0, size=0):
+ANY = pl.BlockSpec(memory_space=pl.ANY)
+
+
+def call(kernel, outs, ins, scratch=(), smem=False, after=(), specs=None, vmem=16, flops=0, size=0):
+    read = len(ins)
+
+    def run(*refs):
+        kernel(*refs[:read], *refs[read + len(after) :])
+
     return pl.pallas_call(
-        kernel,
+        run,
         out_shape=outs,
-        in_specs=([SMEM] if smem else []) + [VMEM] * (len(ins) - int(smem)),
+        in_specs=(specs or ([SMEM] if smem else []) + [VMEM] * (len(ins) - int(smem))) + [ANY] * len(after),
         out_specs=jax.tree.map(lambda _: VMEM, outs),
         scratch_shapes=list(scratch),
-        compiler_params=pltpu.CompilerParams(vmem_limit_bytes=40 * 1024 * 1024),
+        compiler_params=pltpu.CompilerParams(vmem_limit_bytes=vmem * 1024 * 1024),
         cost_estimate=pl.CostEstimate(flops=flops, bytes_accessed=size, transcendentals=0),
-    )(*ins)
+    )(*ins, *after)
 
 
 def shape(dims, dtype=BF):
@@ -213,38 +253,59 @@
             piece = lax.ppermute(piece, "hidden", [(i, (i + 2 * k) % (2 * CHIPS)) for i in range(2 * CHIPS)])
         pieces.append(piece)
 
-    ids = jnp.tile(route_ids.T, (1, SLABS))
-    shares = jnp.tile(route_weights.T, (1, SLABS))
-    perm = unpack_matrix()
-
-    outgoing = call(pack_kernel, shape((EXPERTS, PACK, LANES)), (tokens, ids), flops=2 * 10**8, size=10**6)
-    mine = lax.all_to_all(outgoing, "expert", 0, 0)
+    units = CHIPS * UNITS
+    wa, wb, da, db, ready = call(
+        weights_kernel,
+        (shape((2 * units, half)),) * 2 + (shape((units, half)),) * 2 + (shape((8, LANES), F32),),
+        (where, *pieces, down_proj.reshape(ROWS, half)),
+        smem=True,
+        size=5 * 10**6,
+    )
+
+    ids, shares = route_ids.T, route_weights.T
+    outgoing = call(
+        pack_kernel,
+        shape((EXPERTS, PACK, LANES)),
+        (tokens, ids),
+        (pltpu.VMEM((TOK, half), BF), pltpu.VMEM((TOP, TOK), I32), pltpu.SemaphoreType.DMA(()), pltpu.SemaphoreType.DMA(())),
+        specs=[ANY, ANY],
+        vmem=56,
+        flops=2 * 10**8,
+        size=10**6,
+    )
+    arrived = lax.all_to_all(outgoing, "expert", 0, 0)
+    mine, scale = call(
+        unpack_kernel,
+        (shape((ROWS, half)), shape((8, LANES), F32)),
+        (arrived,),
+        after=(ready,),
+        flops=3 * 10**8,
+        size=2 * 10**6,
+    )
     theirs = lax.ppermute(mine, "hidden", swap)
-
-    part, scale = call(
-        up_kernel,
-        (shape((CHIPS, ROWS // CHIPS, 2 * CHIPS * UNITS)), shape((8, LANES), F32)),
-        (where, mine, theirs, *pieces, perm),
-        (pltpu.VMEM((2 * CHIPS * UNITS, half), BF), pltpu.VMEM((2 * CHIPS * UNITS, half), BF)),
-        smem=True,
-        flops=2 * 10**9,
-        size=5 * 10**6,
+    first = call(own_kernel, shape((ROWS, 2 * units), F32), (mine, wa), flops=6 * 10**8, size=4 * 10**6)
+    part = call(
+        other_kernel, shape((CHIPS, ROWS // CHIPS, 2 * units)), (theirs, wb, first), flops=6 * 10**8, size=5 * 10**6
     )
     parts = lax.all_to_all(part, "hidden", 0, 0, axis_index_groups=groups)
-    hidden = call(silu_kernel, shape((ROWS // CHIPS, CHIPS * UNITS)), (parts,), size=2 * 10**6)
+    hidden = call(silu_kernel, shape((ROWS // CHIPS, units)), (parts,), size=2 * 10**6)
 
     copies = jnp.broadcast_to(hidden[None], (CHIPS, *hidden.shape))
     own = lax.all_to_all(copies, "hidden", 0, 0, axis_index_groups=groups)
     other = lax.ppermute(own, "hidden", swap)
-
+    first, pack = call(
+        down_own_kernel,
+        (shape((CHIPS, ROWS // CHIPS, half), F32), shape((GPACK, GPACK))),
+        (own, da),
+        flops=3 * 10**8,
+        size=3 * 10**6,
+    )
     returning = call(
-        down_kernel,
+        down_other_kernel,
         shape((EXPERTS, PACK, LANES)),
-        (where, own, other, down_proj.reshape(ROWS, half), perm),
-        (pltpu.VMEM((CHIPS * UNITS, half), BF), pltpu.VMEM((CHIPS * UNITS, half), BF)),
-        smem=True,
-        flops=10**9,
-        size=4 * 10**6,
+        (other, db, first, pack),
+        flops=6 * 10**8,
+        size=3 * 10**6,
     )
     returned = lax.all_to_all(returning, "expert", 0, 0)
     hessian = call(
@@ -256,7 +317,10 @@
         flops=2 * 10**9,
         size=3 * 10**6,
     )
-    layer_out = call(combine_kernel, shape((TOK, half)), (ids, shares, returned), flops=4 * 10**8, size=10**6)
+    picks = call(
+        picks_kernel, shape((SLABS * TOK, EXPERTS * PACK)), (ids, shares), after=(returning,), flops=2 * 10**8, size=2 * 10**6
+    )
+    layer_out = call(combine_kernel, shape((TOK, half)), (picks, returned), flops=2 * 10**8, size=10**6)
     return layer_out, hessian[None]
 
 

time: 193 us -> 162 us (0.84)
  waiting for transfers between devices: 90.7 us -> 55.9 us
  local copies, waits for them, and re-layouts: 2.83 us -> 9.36 us
  Pallas kernels: 18.8 us -> 16 us
    all_to_all x1, waiting for transfers between devices: 39.7 us -> 6.94 us  [body(): arrived = lax.all_to_all(outgoing, 'expert', 0, 0)]
    unnamed x8 -> x26, local copies, waits for them, and re-layouts: 0.85 us -> 6.8 us
    pallas_call x6 -> x11, Pallas kernels: 18.8 us -> 16 us  [call(): pl.pallas_call(run, out_shape=outs, in_specs=(specs or ([SMEM] if smem el...]
  transfers between devices with their start and end apart: 7 -> 7, of which waited for: 6 -> 7; matrix products, arithmetic and copies ran while one was open for 1% -> 2% of each run, Pallas kernels for 2% -> 5%
where the time goes in v2:
time: 162 us; the launch traced here: 159 us
  waiting for transfers between devices  55.9 us (35%)
  starting transfers between devices  47 us (29%)
  blocking collectives  30.1 us (19%)
  Pallas kernels  16 us (10%)
  local copies, waits for them, and re-layouts  9.36 us (6%)
    all_to_all x1, waiting for transfers between devices, body(): returned = lax.all_to_all(returning, 'expert', 0, 0)  34.7 us
    all_to_all x1, blocking collectives, body(): parts = lax.all_to_all(part, 'hidden', 0, 0, axis_index_groups=groups)  19.4 us
    all_to_all x1, starting transfers between devices, body(): arrived = lax.all_to_all(outgoing, 'expert', 0, 0)  19.3 us
    pallas_call x11, Pallas kernels, call(): pl.pallas_call(run, out_shape=outs, in_specs=(specs or ([SMEM] if smem el...  16 us
    ppermute x3, waiting for transfers between devices, body(): lax.ppermute(piece, 'hidden', [(i, (i + 2 * k) % (2 * CHIPS)) for i in ra...  12.1 us
    all_to_all x1, blocking collectives, body(): own = lax.all_to_all(copies, 'hidden', 0, 0, axis_index_groups=groups)  10.7 us
    ppermute x3, starting transfers between devices, body(): lax.ppermute(piece, 'hidden', [(i, (i + 2 * k) % (2 * CHIPS)) for i in ra...  10.5 us
    all_to_all x1, waiting for transfers between devices, body(): arrived = lax.all_to_all(outgoing, 'expert', 0, 0)  6.94 us
  transfers between devices with their start and end apart: 7, of which 7 were waited for; matrix products, arithmetic and copies ran while one was open for 2% of the time, Pallas kernels for 5%

profile of v2, /device:TPU:1, one launch (start us, length us, event | category | flops | bytes accessed | tf_op | source)
XLA Modules:
  0.0 159.3 jit_solution(13882605314855859720)
XLA Ops:
  0.6 2.5 %shard_map.68 = bf16[64,48,128]{2,1,0:T(8,128)(2,1)} custom-call(bf16[64,512]{1,0:T(8,128)(2,1)} %refs_0_.1, s32[8,64]{1,0:T(8,128)} %bitcast.8), custom_call_target="tpu_custom_call" | custom-call | flops 200000000 | bytes 1000000 | tf_op jit(solution)/shard_map/pallas_call | solution.py:224
  3.1 19.3 %all-to-all-start = ((bf16[64,48,128]{2,1,0:T(8,128)(2,1)}), bf16[64,48,128]{2,1,0:T(8,128)(2,1)S(1)}, u32[]{:S(2)}, u32[]{:S(2)}) async-start(bf16[64,48,128]{2,1,0:T(8,128)(2,1)} %shard_map.68), calls=%async_computation | async-start | bytes 1572864 | tf_op jit(solution)/shard_map/all_to_all | solution.py:276
  22.5 0.0 copy-start
  22.5 2.5 %constant_dynamic-slice_fusion = (bf16[192,1024]{1,0:T(8,128)(2,1)S(1)}, bf16[192,1024]{1,0:T(8,128)(2,1)}, bf16[192,1024]{1,0:T(8,128)(2,1)}, bf16[192,1024]{1,0:T(8,128)(2,1)S(1)}) fusion(bf16[192,4096]{1,0:T(8,128)(2,1)} %bitcast.11, s32[]{:T(128)S(6)} %select_n.48, s32[]{:T(128)S(6)} %select_n.46, s32[]{:T(128)S(6)} %select_n.44, s32[]{:T(128)S(6)} %select_n.42), kind=kLoop, calls=%fused_computation | loop fusion | bytes 3145744 | tf_op jit(solution)/shard_map/dynamic_slice | solution.py:251
  25.0 3.1 %collective-permute-start = (bf16[192,1024]{1,0:T(8,128)(2,1)}, bf16[192,1024]{1,0:T(8,128)(2,1)S(1)}, u32[]{:S(2)}, u32[]{:S(2)}) collective-permute-start(bf16[192,1024]{1,0:T(8,128)(2,1)} %get-tuple-element.22), channel_id=1, source_target_pairs={{0,2},{1,3},{2,4},{3,5},{4,6},{5,7},{6,0},{7,1},{8,10},{9,11},{10,... | collective-permute-start | bytes 1179656 | tf_op jit(solution)/shard_map/ppermute | solution.py:253
  28.1 4.4 %collective-permute-start.1 = (bf16[192,1024]{1,0:T(8,128)(2,1)}, bf16[192,1024]{1,0:T(8,128)(2,1)S(1)}, u32[]{:S(2)}, u32[]{:S(2)}) collective-permute-start(bf16[192,1024]{1,0:T(8,128)(2,1)} %get-tuple-element.21), channel_id=1, source_target_pairs={{0,4},{1,5},{2,6},{3,7},{4,0},{5,1},{6,2},{7,3},{8,12},{9,13},{10,... | collective-permute-start | bytes 1179656 | tf_op jit(solution)/shard_map/ppermute | solution.py:253
  32.5 3.1 %collective-permute-start.2 = (bf16[192,1024]{1,0:T(8,128)(2,1)S(1)}, bf16[192,1024]{1,0:T(8,128)(2,1)S(1)}, u32[]{:S(2)}, u32[]{:S(2)}) collective-permute-start(bf16[192,1024]{1,0:T(8,128)(2,1)S(1)} %get-tuple-element.20), channel_id=1, source_target_pairs={{0,6},{1,7},{2,0},{3,1},{4,2},{5,3},{6,4},{7,5},{8,14},{9,15},{10,... | collective-permute-start | bytes 1179656 | tf_op jit(solution)/shard_map/ppermute | solution.py:253
  35.6 0.1 pad_add_fusion.refs_0_
  35.7 2.3 %collective-permute-done.refs_2_ = bf16[192,1024]{1,0:T(8,128)(2,1)S(1)} collective-permute-done((bf16[192,1024]{1,0:T(8,128)(2,1)}, bf16[192,1024]{1,0:T(8,128)(2,1)S(1)}, u32[]{:S(2)}, u32[]{:S(2)}) %collective-permute-start) | collective-permute-done | bytes 393248 | tf_op jit(solution)/shard_map/ppermute | solution.py:253
  38.0 0.0 copy-start.3
  38.0 0.8 copy-done.3
  38.7 8.7 %collective-permute-done.1.refs_3_ = bf16[192,1024]{1,0:T(8,128)(2,1)S(1)} collective-permute-done((bf16[192,1024]{1,0:T(8,128)(2,1)}, bf16[192,1024]{1,0:T(8,128)(2,1)S(1)}, u32[]{:S(2)}, u32[]{:S(2)}) %collective-permute-start.1) | collective-permute-done | bytes 393248 | tf_op jit(solution)/shard_map/ppermute | solution.py:253
  47.4 0.7 copy-done.5
  48.1 1.1 collective-permute-done.2.refs_4_
  49.3 0.0 copy-start.7
  49.3 0.8 copy-done.7
  50.0 0.0 copy-done
  50.0 1.0 copy-done.4
  51.0 1.0 copy-done.6
  52.0 1.0 copy-done.8
  53.0 0.7 shard_map.69
  53.7 0.0 copy-start.1
  53.8 0.8 copy-done.1
  54.5 0.7 copy-done.11
  55.3 6.9 %all-to-all-done.refs_0_ = bf16[64,48,128]{2,1,0:T(8,128)(2,1)S(1)} async-done(((bf16[64,48,128]{2,1,0:T(8,128)(2,1)}), bf16[64,48,128]{2,1,0:T(8,128)(2,1)S(1)}, u32[]{:S(2)}, u32[]{:S(2)}) %all-to-all-start) | async-done | bytes 786464 | tf_op jit(solution)/shard_map/all_to_all | solution.py:276
  62.2 0.8 shard_map.70
  63.0 6.0 %collective-permute-start.3 = (bf16[768,512]{1,0:T(8,128)(2,1)S(1)}, bf16[768,512]{1,0:T(8,128)(2,1)S(1)}, u32[]{:S(2)}, u32[]{:S(2)}) collective-permute-start(bf16[768,512]{1,0:T(8,128)(2,1)S(1)} %get-tuple-element.12.refs_0_), channel_id=1, source_target_pairs={{0,1},{1,0},{2,3},{3,2},{4,5},{5,4},{6,7},{7,6},{8,9},{9,8},{10,11... | collective-permute-start | bytes 2359304 | tf_op jit(solution)/shard_map/ppermute | solution.py:285
  68.9 0.8 shard_map.71.refs_2_
  69.8 1.1 collective-permute-done.3.refs_0_
  70.8 1.2 shard_map.72
  72.0 19.4 %all_to_all.20.refs_0_ = bf16[4,192,768]{2,1,0:T(8,128)(2,1)S(1)} all-to-all(bf16[4,192,768]{2,1,0:T(8,128)(2,1)S(1)} %shard_map.72), channel_id=1, replica_groups={{0,2,4,6},{1,3,5,7},{8,10,12,14},{9,11,13,15},{16,18,20,22},{17,19,21,2..., dimensions={0} | all-to-all | bytes 2359296 | tf_op jit(solution)/shard_map/all_to_all | solution.py:290
  91.5 0.2 shard_map.73
  91.7 0.0 copy-start.2
  91.7 0.1 broadcast_in_dim.4
  91.8 10.7 %all_to_all.21.refs_0_.refs_1_ = bf16[4,192,384]{2,1,0:T(8,128)(2,1)S(1)} all-to-all(bf16[4,192,384]{2,1,0:T(8,128)(2,1)S(1)} %broadcast_in_dim.4), channel_id=1, replica_groups={{0,2,4,6},{1,3,5,7},{8,10,12,14},{9,11,13,15},{16,18,20,22},{17,19,21,2..., dimensions={0} | all-to-all | bytes 1179648 | tf_op jit(solution)/shard_map/all_to_all | solution.py:294
  102.4 4.9 %collective-permute-start.4 = (bf16[4,192,384]{2,1,0:T(8,128)(2,1)S(1)}, bf16[4,192,384]{2,1,0:T(8,128)(2,1)S(1)}, u32[]{:S(2)}, u32[]{:S(2)}) collective-permute-start(bf16[4,192,384]{2,1,0:T(8,128)(2,1)S(1)} %all_to_all.21.refs_0_.refs_1_), channel_id=1, source_target_pairs={{0,1},{1,0},{2,3},{3,2},{4,5},{5,4},{6,7},{7,6},{8,9},{9,8},{10,11... | collective-permute-start | bytes 1769480 | tf_op jit(solution)/shard_map/ppermute | solution.py:295
  107.3 0.0 copy-done.12
  107.3 0.6 shard_map.74
  107.9 1.0 collective-permute-done.4.refs_0_.refs_2_
  108.9 0.0 copy-done.2
  108.9 2.6 %shard_map.75.refs_2_ = bf16[64,48,128]{2,1,0:T(8,128)(2,1)} custom-call(bf16[4,192,384]{2,1,0:T(8,128)(2,1)S(1)} %collective-permute-done.4.refs_0_.refs_2_, bf16[384,512]{1,0:T(8,128)(2,1)S(1)} %copy-done.2, f32[4,192,512]{2,1,0:T(8,128)S(1)} %get-tuple-element.17.refs_2_, bf16[384,384]{1,0:T(8,128)(2,1)S(1)} %get-tuple-element.18.refs_3_), custom_call_target="tpu_custom_call" | custom-call | flops 600000000 | bytes 3000000 | tf_op jit(solution)/shard_map/pallas_call | solution.py:224
  111.5 6.4 %all-to-all-start.3 = ((bf16[64,48,128]{2,1,0:T(8,128)(2,1)}), bf16[64,48,128]{2,1,0:T(8,128)(2,1)S(1)}, u32[]{:S(2)}, u32[]{:S(2)}) async-start(bf16[64,48,128]{2,1,0:T(8,128)(2,1)} %shard_map.75.refs_2_), calls=%async_computation.3 | async-start | bytes 1572864 | tf_op jit(solution)/shard_map/all_to_all | solution.py:310
  117.9 0.0 copy-done.9
  117.9 0.0 copy-done.10
  117.9 1.3 shard_map.76.refs_0_
  119.2 4.2 %shard_map.78 = f32[96,768]{1,0:T(8,128)} custom-call(s32[2]{0:T(128)S(1)} %pad_add_fusion.refs_0_, bf16[4,192,384]{2,1,0:T(8,128)(2,1)S(1)} %all_to_all.21.refs_0_.refs_1_, bf16[4,192,384]{2,1,0:T(8,128)(2,1)S(1)} %collective-permute-done.4.refs_0_.refs_2_, f32[8,128]{1,0:T(8,128)S(1)} %get-tuple-element.19.refs_3_), custom_call_target="tpu_custom_call" | custom-call | flops 2000000000 | bytes 3000000 | tf_op jit(solution)/shard_map/pallas_call | solution.py:224
  123.4 34.7 %all-to-all-done.3.refs_1_ = bf16[64,48,128]{2,1,0:T(8,128)(2,1)S(1)} async-done(((bf16[64,48,128]{2,1,0:T(8,128)(2,1)}), bf16[64,48,128]{2,1,0:T(8,128)(2,1)S(1)}, u32[]{:S(2)}, u32[]{:S(2)}) %all-to-all-start.3) | async-done | bytes 786464 | tf_op jit(solution)/shard_map/all_to_all | solution.py:310
  158.1 1.2 shard_map.77
  (8 shorter events, 0.0 us)
Async XLA Ops:
  3.1 59.1 %all-to-all-start = ((bf16[64,48,128]{2,1,0:T(8,128)(2,1)}), bf16[64,48,128]{2,1,0:T(8,128)(2,1)S(1)}, u32[]{:S(2)}, u32[]{:S(2)}) async-start(bf16[64,48,128]{2,1,0:T(8,128)(2,1)} %shard_map.68), calls=%async_computation | async-start | bytes 1572864 | tf_op jit(solution)/shard_map/all_to_all | solution.py:276
  22.5 27.5 %copy-start = (bf16[1,768,512]{2,1,0:T(8,128)(2,1)S(1)}, bf16[1,768,512]{2,1,0:T(8,128)(2,1)}, u32[]{:S(2)}) copy-start(bf16[1,768,512]{2,1,0:T(8,128)(2,1)} %param.9) | copy-start | bytes 2359300
  25.0 13.0 %collective-permute-start = (bf16[192,1024]{1,0:T(8,128)(2,1)}, bf16[192,1024]{1,0:T(8,128)(2,1)S(1)}, u32[]{:S(2)}, u32[]{:S(2)}) collective-permute-start(bf16[192,1024]{1,0:T(8,128)(2,1)} %get-tuple-element.22), channel_id=1, source_target_pairs={{0,2},{1,3},{2,4},{3,5},{4,6},{5,7},{6,0},{7,1},{8,10},{9,11},{10,... | collective-permute-start | bytes 1179656 | tf_op jit(solution)/shard_map/ppermute | solution.py:253
  28.1 19.3 %collective-permute-start.1 = (bf16[192,1024]{1,0:T(8,128)(2,1)}, bf16[192,1024]{1,0:T(8,128)(2,1)S(1)}, u32[]{:S(2)}, u32[]{:S(2)}) collective-permute-start(bf16[192,1024]{1,0:T(8,128)(2,1)} %get-tuple-element.21), channel_id=1, source_target_pairs={{0,4},{1,5},{2,6},{3,7},{4,0},{5,1},{6,2},{7,3},{8,12},{9,13},{10,... | collective-permute-start | bytes 1179656 | tf_op jit(solution)/shard_map/ppermute | solution.py:253
  32.5 16.8 %collective-permute-start.2 = (bf16[192,1024]{1,0:T(8,128)(2,1)S(1)}, bf16[192,1024]{1,0:T(8,128)(2,1)S(1)}, u32[]{:S(2)}, u32[]{:S(2)}) collective-permute-start(bf16[192,1024]{1,0:T(8,128)(2,1)S(1)} %get-tuple-element.20), channel_id=1, source_target_pairs={{0,6},{1,7},{2,0},{3,1},{4,2},{5,3},{6,4},{7,5},{8,14},{9,15},{10,... | collective-permute-start | bytes 1179656 | tf_op jit(solution)/shard_map/ppermute | solution.py:253
  38.0 0.8 copy-start.3
  47.4 0.7 copy-start.5
  49.3 0.8 copy-start.7
  50.0 1.0 copy-start.4
  51.0 1.0 copy-start.6
  52.0 1.0 copy-start.8
  53.7 0.8 copy-start.1
  54.5 0.7 copy-start.11
  63.0 7.9 %collective-permute-start.3 = (bf16[768,512]{1,0:T(8,128)(2,1)S(1)}, bf16[768,512]{1,0:T(8,128)(2,1)S(1)}, u32[]{:S(2)}, u32[]{:S(2)}) collective-permute-start(bf16[768,512]{1,0:T(8,128)(2,1)S(1)} %get-tuple-element.12.refs_0_), channel_id=1, source_target_pairs={{0,1},{1,0},{2,3},{3,2},{4,5},{5,4},{6,7},{7,6},{8,9},{9,8},{10,11... | collective-permute-start | bytes 2359304 | tf_op jit(solution)/shard_map/ppermute | solution.py:285
  91.5 15.8 %copy-start.12 = (bf16[384,512]{1,0:T(8,128)(2,1)S(1)}, bf16[384,512]{1,0:T(8,128)(2,1)}, u32[]{:S(2)}) copy-start(bf16[384,512]{1,0:T(8,128)(2,1)} %copy-done.11) | copy-start | bytes 1179652
  91.7 17.2 %copy-start.2 = (bf16[384,512]{1,0:T(8,128)(2,1)S(1)}, bf16[384,512]{1,0:T(8,128)(2,1)}, u32[]{:S(2)}) copy-start(bf16[384,512]{1,0:T(8,128)(2,1)} %copy-done.1) | copy-start | bytes 1179652
  102.4 6.5 %collective-permute-start.4 = (bf16[4,192,384]{2,1,0:T(8,128)(2,1)S(1)}, bf16[4,192,384]{2,1,0:T(8,128)(2,1)S(1)}, u32[]{:S(2)}, u32[]{:S(2)}) collective-permute-start(bf16[4,192,384]{2,1,0:T(8,128)(2,1)S(1)} %all_to_all.21.refs_0_.refs_1_), channel_id=1, source_target_pairs={{0,1},{1,0},{2,3},{3,2},{4,5},{5,4},{6,7},{7,6},{8,9},{9,8},{10,11... | collective-permute-start | bytes 1769480 | tf_op jit(solution)/shard_map/ppermute | solution.py:295
  111.5 6.4 %copy-start.9 = (s32[64,8]{0,1:T(8,128)S(1)}, s32[64,8]{0,1:T(8,128)}, u32[]{:S(2)}) copy-start(s32[64,8]{0,1:T(8,128)} %param.6) | copy-start | bytes 6148
  111.5 6.4 %copy-start.10 = (f32[64,8]{0,1:T(8,128)S(1)}, f32[64,8]{0,1:T(8,128)}, u32[]{:S(2)}) copy-start(f32[64,8]{0,1:T(8,128)} %param.7) | copy-start | bytes 6148
  111.5 46.6 %all-to-all-start.3 = ((bf16[64,48,128]{2,1,0:T(8,128)(2,1)}), bf16[64,48,128]{2,1,0:T(8,128)(2,1)S(1)}, u32[]{:S(2)}, u32[]{:S(2)}) async-start(bf16[64,48,128]{2,1,0:T(8,128)(2,1)} %shard_map.75.refs_2_), calls=%async_computation.3 | async-start | bytes 1572864 | tf_op jit(solution)/shard_map/all_to_all | solution.py:310

commit v3 on v2

--- a/solution.py
+++ b/solution.py
@@ -57,24 +57,25 @@
     return code, member, weight
 
 
-def pack_kernel(tok_hbm, ids_hbm, out_ref, tok_ref, ids_ref, tok_sem, ids_sem):
+def pack_kernel(tok_hbm, ids_hbm, out_hbm, tok_ref, ids_ref, out_ref, tok_sem, ids_sem, out_sems):
     fetch_ids = pltpu.make_async_copy(ids_hbm, ids_ref, ids_sem)
     fetch_ids.start()
     fetch = pltpu.make_async_copy(tok_hbm, tok_ref, tok_sem)
     fetch.start()
+    wide = SLABS * TOK
+    p = iota((PACK, wide), 0)
+    slab = (p >= CAP).astype(I32) + (p >= 2 * CAP).astype(I32) + (p >= 3 * CAP).astype(I32)
+    target = (p + 4 * slab).astype(F32)
+    q = iota((PACK, LANES), 0)
+    first = jnp.where(q < CAP, q, -1).astype(F32)
     fetch_ids.wait()
     code, member, _ = codes(ids_ref[...])
-    wide = SLABS * TOK
     ones = jnp.where(iota((wide, LANES), 0) < TOK, 1.0, 0.0).astype(BF)
     count = dot(member.astype(BF), ones)
     fetch.wait()
     tok = tok_ref[...]
     slabs = jnp.concatenate([tok[:, l * LANES : (l + 1) * LANES] for l in range(SLABS)], axis=0)
-    p = iota((PACK, wide), 0)
-    slab = (p >= CAP).astype(I32) + (p >= 2 * CAP).astype(I32) + (p >= 3 * CAP).astype(I32)
-    target = (p + 4 * slab).astype(F32)
-    q = iota((PACK, LANES), 0)
-    first = jnp.where(q < CAP, q, -1).astype(F32)
+    sends = []
     for c in range(EXPERTS // GROUP):
         picks = [
             jnp.where(code[e : e + 1, :] == target, 1.0, 0.0).astype(BF)
@@ -85,6 +86,11 @@
             e = c * GROUP + j
             block = rows[j * PACK : (j + 1) * PACK]
             out_ref[e] = jnp.where(first >= count[e : e + 1, :], EMPTY, block).astype(BF)
+        at = slice(c * GROUP, (c + 1) * GROUP)
+        sends.append(pltpu.make_async_copy(out_ref.at[at], out_hbm.at[at], out_sems.at[c]))
+        sends[-1].start()
+    for send in sends:
+        send.wait()
 
 
 def repack_matrix(packs):
@@ -100,35 +106,52 @@
     return (matrix.T if packs else matrix).astype(BF)
 
 
-def weights_kernel(place_ref, w0_ref, w1_ref, w2_ref, w3_ref, down_ref, wa, wb, da, db, ready_ref):
+def weights_kernel(place_ref, w0_ref, w1_ref, w2_ref, w3_ref, down_ref, wa, wb, da, db, ready_ref, sems):
     x, c = place_ref[0], place_ref[1]
     half = SLABS * LANES
-    own = pl.multiple_of(c * half, half)
-    other = pl.multiple_of((1 - c) * half, half)
+    copies = []
+
+    def move(source, target):
+        copies.append(pltpu.make_async_copy(source, target, sems.at[len(copies)]))
+
     for k, w_ref in enumerate((w0_ref, w1_ref, w2_ref, w3_ref)):
         at = pl.multiple_of(((x + CHIPS - k) % CHIPS) * UNITS, 32)
+        base = x * (2 * half) if k == 0 else 0
+        own = pl.multiple_of(base + c * half, half)
+        other = pl.multiple_of(base + (1 - c) * half, half)
         for g in range(2):
-            wa[pl.ds(at + g * CHIPS * UNITS, UNITS), :] = w_ref[g * UNITS : (g + 1) * UNITS, pl.ds(own, half)]
-            wb[pl.ds(at + g * CHIPS * UNITS, UNITS), :] = w_ref[g * UNITS : (g + 1) * UNITS, pl.ds(other, half)]
+            source = slice(g * UNITS, (g + 1) * UNITS)
+            target = pl.ds(pl.multiple_of(at + g * CHIPS * UNITS, 32), UNITS)
+            move(w_ref.at[source, pl.ds(own, half)], wa.at[target, :])
+            move(w_ref.at[source, pl.ds(other, half)], wb.at[target, :])
     for i in range(CHIPS):
         mine = pl.multiple_of((2 * i + c) * UNITS, 32)
         theirs = pl.multiple_of((2 * i + 1 - c) * UNITS, 32)
-        da[i * UNITS : (i + 1) * UNITS, :] = down_ref[pl.ds(mine, UNITS), :]
-        db[i * UNITS : (i + 1) * UNITS, :] = down_ref[pl.ds(theirs, UNITS), :]
+        move(down_ref.at[pl.ds(mine, UNITS), :], da.at[i * UNITS : (i + 1) * UNITS, :])
+        move(down_ref.at[pl.ds(theirs, UNITS), :], db.at[i * UNITS : (i + 1) * UNITS, :])
+    for copy in copies:
+        copy.start()
     ready_ref[...] = jnp.zeros_like(ready_ref)
+    for copy in copies:
+        copy.wait()
 
 
 def unpack_kernel(in_ref, rows_ref, scale_ref):
     perm = repack_matrix(False)
-    empty = jnp.zeros((GROWS, LANES), F32)
-    for g in range(EXPERTS // GROUP):
-        y = dot(perm, in_ref[g * GROUP : (g + 1) * GROUP].reshape(GPACK, LANES))
+    empty = jnp.zeros((GROWS, 2 * LANES), F32)
+    for h in range(EXPERTS // GROUP // 2):
+        pair = [in_ref[g * GROUP : (g + 1) * GROUP].reshape(GPACK, LANES) for g in (2 * h, 2 * h + 1)]
+        y = dot(perm, jnp.concatenate(pair, axis=1))
         first = y[:GROWS]
         gone = first > 0.5 * EMPTY
         empty = empty + jnp.where(gone, 1.0, 0.0)
         parts = [jnp.where(gone, 0.0, first)] + [y[l * GROWS : (l + 1) * GROWS] for l in range(1, SLABS)]
-        rows_ref[g * GROWS : (g + 1) * GROWS, :] = jnp.concatenate([part.astype(BF) for part in parts], axis=1)
-    gone = jnp.sum(empty, axis=0, keepdims=True)
+        parts = [part.astype(BF) for part in parts]
+        for j in range(2):
+            at = slice((2 * h + j) * GROWS, (2 * h + j + 1) * GROWS)
+            lanes = slice(j * LANES, (j + 1) * LANES)
+            rows_ref[at, :] = jnp.concatenate([part[:, lanes] for part in parts], axis=1)
+    gone = jnp.sum(empty[:, :LANES] + empty[:, LANES:], axis=0, keepdims=True)
     scale_ref[...] = jnp.broadcast_to(2.0 / (float(ROWS) - gone), scale_ref.shape)
 
 
@@ -149,25 +172,39 @@
         total = total + in_ref[k].astype(F32)
     half = CHIPS * UNITS
     gate, up = total[:, :half], total[:, half:]
-    out_ref[...] = (gate / (1.0 + jnp.exp(-gate)) * up).astype(BF)
+    hidden = (gate / (1.0 + jnp.exp(-gate)) * up).astype(BF)
+    for k in range(CHIPS):
+        out_ref[k] = hidden
 
 
 def down_own_kernel(hidden_ref, down_ref, out_ref, perm_ref):
     perm_ref[...] = repack_matrix(True)
-    for k in range(CHIPS):
-        out_ref[k] = dot(hidden_ref[k], down_ref[...])
-
-
-def down_other_kernel(hidden_ref, down_ref, part_ref, perm_ref, out_ref):
+    out_ref[...] = dot(hidden_ref[...].reshape(ROWS, CHIPS * UNITS), down_ref[...])
+
+
+def down_other_kernel(hidden_ref, down_ref, part_ref, perm_ref, out_hbm, out_ref, sems):
     perm = perm_ref[...]
-    sources = EXPERTS // CHIPS
-    for k in range(CHIPS):
-        rows = (part_ref[k] + dot(hidden_ref[k], down_ref[...])).astype(BF)
-        for h in range(2):
-            part = rows[h * GROWS : (h + 1) * GROWS]
-            stack = jnp.concatenate([part[:, l * LANES : (l + 1) * LANES] for l in range(SLABS)], axis=0)
-            packed = dot(perm, stack).astype(BF).reshape(GROUP, PACK, LANES)
-            out_ref[k * sources + h * GROUP : k * sources + (h + 1) * GROUP] = packed
+    rows = (part_ref[...] + dot(hidden_ref[...].reshape(ROWS, CHIPS * UNITS), down_ref[...])).astype(BF)
+    sends = []
+    for h in range(EXPERTS // GROUP // 2):
+        stack = jnp.concatenate(
+            [
+                jnp.concatenate(
+                    [rows[g * GROWS : (g + 1) * GROWS, l * LANES : (l + 1) * LANES] for g in (2 * h, 2 * h + 1)], axis=1
+                )
+                for l in range(SLABS)
+            ],
+            axis=0,
+        )
+        packed = dot(perm, stack).astype(BF)
+        for j, g in enumerate((2 * h, 2 * h + 1)):
+            block = packed[:, j * LANES : (j + 1) * LANES]
+            out_ref[g * GROUP : (g + 1) * GROUP] = block.reshape(GROUP, PACK, LANES)
+        at = slice(2 * h * GROUP, 2 * (h + 1) * GROUP)
+        sends.append(pltpu.make_async_copy(out_ref.at[at], out_hbm.at[at], sems.at[h]))
+        sends[-1].start()
+    for send in sends:
+        send.wait()
 
 
 def gram_kernel(place_ref, own_ref, other_ref, scale_ref, out_ref, acc):
@@ -215,7 +252,7 @@
 ANY = pl.BlockSpec(memory_space=pl.ANY)
 
 
-def call(kernel, outs, ins, scratch=(), smem=False, after=(), specs=None, vmem=16, flops=0, size=0):
+def call(kernel, outs, ins, scratch=(), smem=False, after=(), specs=None, outs_in=None, vmem=12, flops=0, size=0):
     read = len(ins)
 
     def run(*refs):
@@ -225,7 +262,7 @@
         run,
         out_shape=outs,
         in_specs=(specs or ([SMEM] if smem else []) + [VMEM] * (len(ins) - int(smem))) + [ANY] * len(after),
-        out_specs=jax.tree.map(lambda _: VMEM, outs),
+        out_specs=jax.tree.map(lambda _: outs_in or VMEM, outs),
         scratch_shapes=list(scratch),
         compiler_params=pltpu.CompilerParams(vmem_limit_bytes=vmem * 1024 * 1024),
         cost_estimate=pl.CostEstimate(flops=flops, bytes_accessed=size, transcendentals=0),
@@ -245,20 +282,19 @@
     groups = [[2 * i + j for i in range(CHIPS)] for j in range(2)]
     swap = [(i, i ^ 1) for i in range(2 * CHIPS)]
 
+    units = CHIPS * UNITS
     weights = gate_up.reshape(2 * UNITS, CHIPS * wide)
     pieces = []
-    for k in range(CHIPS):
+    for k in range(1, CHIPS):
         piece = lax.dynamic_slice(weights, (0, ((x + k) % CHIPS) * wide), (2 * UNITS, wide))
-        if k:
-            piece = lax.ppermute(piece, "hidden", [(i, (i + 2 * k) % (2 * CHIPS)) for i in range(2 * CHIPS)])
-        pieces.append(piece)
-
-    units = CHIPS * UNITS
+        pieces.append(lax.ppermute(piece, "hidden", [(i, (i + 2 * k) % (2 * CHIPS)) for i in range(2 * CHIPS)]))
     wa, wb, da, db, ready = call(
         weights_kernel,
         (shape((2 * units, half)),) * 2 + (shape((units, half)),) * 2 + (shape((8, LANES), F32),),
-        (where, *pieces, down_proj.reshape(ROWS, half)),
-        smem=True,
+        (where, weights, *pieces, down_proj.reshape(ROWS, half)),
+        (pltpu.SemaphoreType.DMA((6 * CHIPS,)),),
+        specs=[SMEM] + [ANY] * 5,
+        vmem=12,
         size=5 * 10**6,
     )
 
@@ -267,8 +303,16 @@
         pack_kernel,
         shape((EXPERTS, PACK, LANES)),
         (tokens, ids),
-        (pltpu.VMEM((TOK, half), BF), pltpu.VMEM((TOP, TOK), I32), pltpu.SemaphoreType.DMA(()), pltpu.SemaphoreType.DMA(())),
+        (
+            pltpu.VMEM((TOK, half), BF),
+            pltpu.VMEM((TOP, TOK), I32),
+            pltpu.VMEM((EXPERTS, PACK, LANES), BF),
+            pltpu.SemaphoreType.DMA(()),
+            pltpu.SemaphoreType.DMA(()),
+            pltpu.SemaphoreType.DMA((EXPERTS // GROUP,)),
+        ),
         specs=[ANY, ANY],
+        outs_in=ANY,
         vmem=56,
         flops=2 * 10**8,
         size=10**6,
@@ -288,14 +332,12 @@
         other_kernel, shape((CHIPS, ROWS // CHIPS, 2 * units)), (theirs, wb, first), flops=6 * 10**8, size=5 * 10**6
     )
     parts = lax.all_to_all(part, "hidden", 0, 0, axis_index_groups=groups)
-    hidden = call(silu_kernel, shape((ROWS // CHIPS, units)), (parts,), size=2 * 10**6)
-
-    copies = jnp.broadcast_to(hidden[None], (CHIPS, *hidden.shape))
+    copies = call(silu_kernel, shape((CHIPS, ROWS // CHIPS, units)), (parts,), size=3 * 10**6)
     own = lax.all_to_all(copies, "hidden", 0, 0, axis_index_groups=groups)
     other = lax.ppermute(own, "hidden", swap)
     first, pack = call(
         down_own_kernel,
-        (shape((CHIPS, ROWS // CHIPS, half), F32), shape((GPACK, GPACK))),
+        (shape((ROWS, half), F32), shape((GPACK, GPACK))),
         (own, da),
         flops=3 * 10**8,
         size=3 * 10**6,
@@ -304,6 +346,8 @@
         down_other_kernel,
         shape((EXPERTS, PACK, LANES)),
         (other, db, first, pack),
+        (pltpu.VMEM((EXPERTS, PACK, LANES), BF), pltpu.SemaphoreType.DMA((EXPERTS // GROUP // 2,))),
+        outs_in=ANY,
         flops=6 * 10**8,
         size=3 * 10**6,
     )

time: 162 us -> 161 us (level)
    unnamed x26 -> x28, local copies, waits for them, and re-layouts: 6.8 us -> 7.13 us
  transfers between devices with their start and end apart: 7 -> 7, of which waited for: 7 -> 7; matrix products, arithmetic and copies ran while one was open for 2% -> 1% of each run, Pallas kernels for 5% -> 6%
where the time goes in v3:
time: 161 us; the launch traced here: 158 us
  waiting for transfers between devices  55.3 us (34%)
  starting transfers between devices  47 us (29%)
  blocking collectives  30.1 us (19%)
  Pallas kernels  16.6 us (10%)
  local copies, waits for them, and re-layouts  8.22 us (5%)
    all_to_all x1, waiting for transfers between devices, body(): returned = lax.all_to_all(returning, 'expert', 0, 0)  34.7 us
    all_to_all x1, blocking collectives, body(): parts = lax.all_to_all(part, 'hidden', 0, 0, axis_index_groups=groups)  19.5 us
    all_to_all x1, starting transfers between devices, body(): arrived = lax.all_to_all(outgoing, 'expert', 0, 0)  19.3 us
    pallas_call x11, Pallas kernels, call(): pl.pallas_call(run, out_shape=outs, in_specs=(specs or ([SMEM] if smem el...  16.6 us
    ppermute x3, waiting for transfers between devices, body(): lax.ppermute(piece, 'hidden', [(i, (i + 2 * k) % (2 * CHIPS)) for i in ra...  12.9 us
    all_to_all x1, blocking collectives, body(): own = lax.all_to_all(copies, 'hidden', 0, 0, axis_index_groups=groups)  10.7 us
    ppermute x3, starting transfers between devices, body(): lax.ppermute(piece, 'hidden', [(i, (i + 2 * k) % (2 * CHIPS)) for i in ra...  10.5 us
    unnamed x28, local copies, waits for them, and re-layouts  7.13 us
  transfers between devices with their start and end apart: 7, of which 7 were waited for; matrix products, arithmetic and copies ran while one was open for 1% of the time, Pallas kernels for 6%

profile of v3, /device:TPU:1, one launch (start us, length us, event | category | flops | bytes accessed | tf_op | source)
XLA Modules:
  0.0 158.3 jit_solution(1521971996244602338)
XLA Ops:
  0.6 0.0 copy-start
  0.6 2.5 %shard_map.68 = bf16[64,48,128]{2,1,0:T(8,128)(2,1)} custom-call(bf16[64,512]{1,0:T(8,128)(2,1)} %refs_0_.1, s32[8,64]{1,0:T(8,128)} %bitcast.10), custom_call_target="tpu_custom_call" | custom-call | flops 200000000 | bytes 1000000 | tf_op jit(solution)/shard_map/pallas_call | solution.py:261
  3.1 19.3 %all-to-all-start = ((bf16[64,48,128]{2,1,0:T(8,128)(2,1)}), bf16[64,48,128]{2,1,0:T(8,128)(2,1)S(1)}, u32[]{:S(2)}, u32[]{:S(2)}) async-start(bf16[64,48,128]{2,1,0:T(8,128)(2,1)} %shard_map.68), calls=%async_computation | async-start | bytes 1572864 | tf_op jit(solution)/shard_map/all_to_all | solution.py:320
  22.5 0.0 copy-done
  22.5 1.1 constant_dynamic-slice_fusion
  23.6 3.1 %collective-permute-start = (bf16[192,1024]{1,0:T(8,128)(2,1)}, bf16[192,1024]{1,0:T(8,128)(2,1)S(1)}, u32[]{:S(2)}, u32[]{:S(2)}) collective-permute-start(bf16[192,1024]{1,0:T(8,128)(2,1)} %get-tuple-element.22), channel_id=1, source_target_pairs={{0,2},{1,3},{2,4},{3,5},{4,6},{5,7},{6,0},{7,1},{8,10},{9,11},{10,... | collective-permute-start | bytes 1179656 | tf_op jit(solution)/shard_map/ppermute | solution.py:290
  26.7 4.4 %collective-permute-start.1 = (bf16[192,1024]{1,0:T(8,128)(2,1)}, bf16[192,1024]{1,0:T(8,128)(2,1)S(1)}, u32[]{:S(2)}, u32[]{:S(2)}) collective-permute-start(bf16[192,1024]{1,0:T(8,128)(2,1)} %get-tuple-element.21), channel_id=1, source_target_pairs={{0,4},{1,5},{2,6},{3,7},{4,0},{5,1},{6,2},{7,3},{8,12},{9,13},{10,... | collective-permute-start | bytes 1179656 | tf_op jit(solution)/shard_map/ppermute | solution.py:290
  31.1 3.1 %collective-permute-start.2 = (bf16[192,1024]{1,0:T(8,128)(2,1)}, bf16[192,1024]{1,0:T(8,128)(2,1)S(1)}, u32[]{:S(2)}, u32[]{:S(2)}) collective-permute-start(bf16[192,1024]{1,0:T(8,128)(2,1)} %get-tuple-element.20), channel_id=1, source_target_pairs={{0,6},{1,7},{2,0},{3,1},{4,2},{5,3},{6,4},{7,5},{8,14},{9,15},{10,... | collective-permute-start | bytes 1179656 | tf_op jit(solution)/shard_map/ppermute | solution.py:290
  34.1 0.1 pad_add_fusion.refs_0_
  34.2 2.3 %collective-permute-done.refs_2_ = bf16[192,1024]{1,0:T(8,128)(2,1)S(1)} collective-permute-done((bf16[192,1024]{1,0:T(8,128)(2,1)}, bf16[192,1024]{1,0:T(8,128)(2,1)S(1)}, u32[]{:S(2)}, u32[]{:S(2)}) %collective-permute-start) | collective-permute-done | bytes 393248 | tf_op jit(solution)/shard_map/ppermute | solution.py:290
  36.5 9.4 %collective-permute-done.1.refs_3_ = bf16[192,1024]{1,0:T(8,128)(2,1)S(1)} collective-permute-done((bf16[192,1024]{1,0:T(8,128)(2,1)}, bf16[192,1024]{1,0:T(8,128)(2,1)S(1)}, u32[]{:S(2)}, u32[]{:S(2)}) %collective-permute-start.1) | collective-permute-done | bytes 393248 | tf_op jit(solution)/shard_map/ppermute | solution.py:290
  45.9 0.8 copy-done.6
  46.7 1.2 collective-permute-done.2.refs_4_
  47.9 0.8 copy-done.8
  48.7 1.1 copy-done.1
  49.8 1.0 copy-done.7
  50.8 1.0 copy-done.9
  51.8 2.3 %shard_map.69 = (bf16[768,512]{1,0:T(8,128)(2,1)S(1)}, bf16[768,512]{1,0:T(8,128)(2,1)S(1)}, bf16[384,512]{1,0:T(8,128)(2,1)S(1)}, bf16[384,512]{1,0:T(8,128)(2,1)S(1)}, f32[8,128]{1,0:T(8,128)S(1)}) custom-call(s32[2]{0:T(128)S(1)} %pad_add_fusion.refs_0_, bf16[192,4096]{1,0:T(8,128)(2,1)S(1)} %bitcast.8, ...), custom_call_target="tpu_custom_call" | custom-call | bytes 5000000 | tf_op jit(solution)/shard_map/pallas_call | solution.py:261
  54.1 0.0 copy-start.2
  54.1 0.9 copy-done.2
  55.1 0.8 copy-done.4
  55.9 0.7 copy-done.12
  56.6 5.6 %all-to-all-done.refs_0_ = bf16[64,48,128]{2,1,0:T(8,128)(2,1)S(1)} async-done(((bf16[64,48,128]{2,1,0:T(8,128)(2,1)}), bf16[64,48,128]{2,1,0:T(8,128)(2,1)S(1)}, u32[]{:S(2)}, u32[]{:S(2)}) %all-to-all-start) | async-done | bytes 786464 | tf_op jit(solution)/shard_map/all_to_all | solution.py:320
  62.2 0.6 shard_map.70
  62.8 6.0 %collective-permute-start.3 = (bf16[768,512]{1,0:T(8,128)(2,1)S(1)}, bf16[768,512]{1,0:T(8,128)(2,1)S(1)}, u32[]{:S(2)}, u32[]{:S(2)}) collective-permute-start(bf16[768,512]{1,0:T(8,128)(2,1)S(1)} %get-tuple-element.12.refs_0_), channel_id=1, source_target_pairs={{0,1},{1,0},{2,3},{3,2},{4,5},{5,4},{6,7},{7,6},{8,9},{9,8},{10,11... | collective-permute-start | bytes 2359304 | tf_op jit(solution)/shard_map/ppermute | solution.py:329
  68.7 0.0 copy-done.3
  68.8 0.8 shard_map.71.refs_2_
  69.6 1.1 collective-permute-done.3.refs_0_
  70.6 1.2 shard_map.72
  71.8 19.5 %all_to_all.20.refs_0_ = bf16[4,192,768]{2,1,0:T(8,128)(2,1)S(1)} all-to-all(bf16[4,192,768]{2,1,0:T(8,128)(2,1)S(1)} %shard_map.72), channel_id=1, replica_groups={{0,2,4,6},{1,3,5,7},{8,10,12,14},{9,11,13,15},{16,18,20,22},{17,19,21,2..., dimensions={0} | all-to-all | bytes 2359296 | tf_op jit(solution)/shard_map/all_to_all | solution.py:334
  91.3 0.2 shard_map.73
  91.5 0.0 copy-start.5
  91.5 10.7 %all_to_all.21.refs_0_.refs_1_ = bf16[4,192,384]{2,1,0:T(8,128)(2,1)S(1)} all-to-all(bf16[4,192,384]{2,1,0:T(8,128)(2,1)S(1)} %shard_map.73), channel_id=1, replica_groups={{0,2,4,6},{1,3,5,7},{8,10,12,14},{9,11,13,15},{16,18,20,22},{17,19,21,2..., dimensions={0} | all-to-all | bytes 1179648 | tf_op jit(solution)/shard_map/all_to_all | solution.py:336
  102.2 4.9 %collective-permute-start.4 = (bf16[4,192,384]{2,1,0:T(8,128)(2,1)S(1)}, bf16[4,192,384]{2,1,0:T(8,128)(2,1)S(1)}, u32[]{:S(2)}, u32[]{:S(2)}) collective-permute-start(bf16[4,192,384]{2,1,0:T(8,128)(2,1)S(1)} %all_to_all.21.refs_0_.refs_1_), channel_id=1, source_target_pairs={{0,1},{1,0},{2,3},{3,2},{4,5},{5,4},{6,7},{7,6},{8,9},{9,8},{10,11... | collective-permute-start | bytes 1769480 | tf_op jit(solution)/shard_map/ppermute | solution.py:337
  107.1 0.0 copy-done.13
  107.1 0.6 shard_map.74
  107.6 1.0 collective-permute-done.4.refs_0_.refs_2_
  108.7 0.0 copy-done.5
  108.7 1.8 %shard_map.75.refs_2_ = bf16[64,48,128]{2,1,0:T(8,128)(2,1)} custom-call(bf16[4,192,384]{2,1,0:T(8,128)(2,1)S(1)} %collective-permute-done.4.refs_0_.refs_2_, bf16[384,512]{1,0:T(8,128)(2,1)S(1)} %copy-done.5, f32[768,512]{1,0:T(8,128)S(1)} %get-tuple-element.17.refs_2_, bf16[384,384]{1,0:T(8,128)(2,1)S(1)} %get-tuple-element.18.refs_3_), custom_call_target="tpu_custom_call" | custom-call | flops 600000000 | bytes 3000000 | tf_op jit(solution)/shard_map/pallas_call | solution.py:261
  110.4 0.0 copy-start.10
  110.5 0.0 copy-start.11
  110.5 6.4 %all-to-all-start.3 = ((bf16[64,48,128]{2,1,0:T(8,128)(2,1)}), bf16[64,48,128]{2,1,0:T(8,128)(2,1)S(1)}, u32[]{:S(2)}, u32[]{:S(2)}) async-start(bf16[64,48,128]{2,1,0:T(8,128)(2,1)} %shard_map.75.refs_2_), calls=%async_computation.3 | async-start | bytes 1572864 | tf_op jit(solution)/shard_map/all_to_all | solution.py:354
  116.8 0.0 copy-done.10
  116.8 0.0 copy-done.11
  116.9 1.3 shard_map.76.refs_0_
  118.2 4.2 %shard_map.78 = f32[96,768]{1,0:T(8,128)} custom-call(s32[2]{0:T(128)S(1)} %pad_add_fusion.refs_0_, bf16[4,192,384]{2,1,0:T(8,128)(2,1)S(1)} %all_to_all.21.refs_0_.refs_1_, bf16[4,192,384]{2,1,0:T(8,128)(2,1)S(1)} %collective-permute-done.4.refs_0_.refs_2_, f32[8,128]{1,0:T(8,128)S(1)} %get-tuple-element.19.refs_3_), custom_call_target="tpu_custom_call" | custom-call | flops 2000000000 | bytes 3000000 | tf_op jit(solution)/shard_map/pallas_call | solution.py:261
  122.4 34.7 %all-to-all-done.3.refs_1_ = bf16[64,48,128]{2,1,0:T(8,128)(2,1)S(1)} async-done(((bf16[64,48,128]{2,1,0:T(8,128)(2,1)}), bf16[64,48,128]{2,1,0:T(8,128)(2,1)S(1)}, u32[]{:S(2)}, u32[]{:S(2)}) %all-to-all-start.3) | async-done | bytes 786464 | tf_op jit(solution)/shard_map/all_to_all | solution.py:354
  157.1 1.2 shard_map.77
  (9 shorter events, 0.0 us)
Async XLA Ops:
  0.6 21.8 %copy-start = (bf16[1,2,96,4096]{3,2,1,0:T(8,128)(2,1)S(1)}, bf16[1,2,96,4096]{3,2,1,0:T(8,128)(2,1)}, u32[]{:S(2)}) copy-start(bf16[1,2,96,4096]{3,2,1,0:T(8,128)(2,1)} %param.8) | copy-start | bytes 4718596
  3.1 59.1 %all-to-all-start = ((bf16[64,48,128]{2,1,0:T(8,128)(2,1)}), bf16[64,48,128]{2,1,0:T(8,128)(2,1)S(1)}, u32[]{:S(2)}, u32[]{:S(2)}) async-start(bf16[64,48,128]{2,1,0:T(8,128)(2,1)} %shard_map.68), calls=%async_computation | async-start | bytes 1572864 | tf_op jit(solution)/shard_map/all_to_all | solution.py:320
  23.6 13.0 %collective-permute-start = (bf16[192,1024]{1,0:T(8,128)(2,1)}, bf16[192,1024]{1,0:T(8,128)(2,1)S(1)}, u32[]{:S(2)}, u32[]{:S(2)}) collective-permute-start(bf16[192,1024]{1,0:T(8,128)(2,1)} %get-tuple-element.22), channel_id=1, source_target_pairs={{0,2},{1,3},{2,4},{3,5},{4,6},{5,7},{6,0},{7,1},{8,10},{9,11},{10,... | collective-permute-start | bytes 1179656 | tf_op jit(solution)/shard_map/ppermute | solution.py:290
  26.7 19.3 %collective-permute-start.1 = (bf16[192,1024]{1,0:T(8,128)(2,1)}, bf16[192,1024]{1,0:T(8,128)(2,1)S(1)}, u32[]{:S(2)}, u32[]{:S(2)}) collective-permute-start(bf16[192,1024]{1,0:T(8,128)(2,1)} %get-tuple-element.21), channel_id=1, source_target_pairs={{0,4},{1,5},{2,6},{3,7},{4,0},{5,1},{6,2},{7,3},{8,12},{9,13},{10,... | collective-permute-start | bytes 1179656 | tf_op jit(solution)/shard_map/ppermute | solution.py:290
  31.1 16.9 %collective-permute-start.2 = (bf16[192,1024]{1,0:T(8,128)(2,1)}, bf16[192,1024]{1,0:T(8,128)(2,1)S(1)}, u32[]{:S(2)}, u32[]{:S(2)}) collective-permute-start(bf16[192,1024]{1,0:T(8,128)(2,1)} %get-tuple-element.20), channel_id=1, source_target_pairs={{0,6},{1,7},{2,0},{3,1},{4,2},{5,3},{6,4},{7,5},{8,14},{9,15},{10,... | collective-permute-start | bytes 1179656 | tf_op jit(solution)/shard_map/ppermute | solution.py:290
  45.9 0.8 copy-start.6
  47.9 0.8 copy-start.8
  48.7 1.1 copy-start.1
  49.8 1.0 copy-start.7
  50.8 1.0 copy-start.9
  54.1 0.9 copy-start.2
  55.1 0.8 copy-start.4
  55.9 0.7 copy-start.12
  62.2 6.6 %copy-start.3 = (bf16[768,512]{1,0:T(8,128)(2,1)S(1)}, bf16[768,512]{1,0:T(8,128)(2,1)}, u32[]{:S(2)}) copy-start(bf16[768,512]{1,0:T(8,128)(2,1)} %copy-done.2) | copy-start | bytes 2359300
  62.8 7.9 %collective-permute-start.3 = (bf16[768,512]{1,0:T(8,128)(2,1)S(1)}, bf16[768,512]{1,0:T(8,128)(2,1)S(1)}, u32[]{:S(2)}, u32[]{:S(2)}) collective-permute-start(bf16[768,512]{1,0:T(8,128)(2,1)S(1)} %get-tuple-element.12.refs_0_), channel_id=1, source_target_pairs={{0,1},{1,0},{2,3},{3,2},{4,5},{5,4},{6,7},{7,6},{8,9},{9,8},{10,11... | collective-permute-start | bytes 2359304 | tf_op jit(solution)/shard_map/ppermute | solution.py:329
  91.3 15.8 %copy-start.13 = (bf16[384,512]{1,0:T(8,128)(2,1)S(1)}, bf16[384,512]{1,0:T(8,128)(2,1)}, u32[]{:S(2)}) copy-start(bf16[384,512]{1,0:T(8,128)(2,1)} %copy-done.12) | copy-start | bytes 1179652
  91.5 17.2 %copy-start.5 = (bf16[384,512]{1,0:T(8,128)(2,1)S(1)}, bf16[384,512]{1,0:T(8,128)(2,1)}, u32[]{:S(2)}) copy-start(bf16[384,512]{1,0:T(8,128)(2,1)} %copy-done.4) | copy-start | bytes 1179652
  102.2 6.5 %collective-permute-start.4 = (bf16[4,192,384]{2,1,0:T(8,128)(2,1)S(1)}, bf16[4,192,384]{2,1,0:T(8,128)(2,1)S(1)}, u32[]{:S(2)}, u32[]{:S(2)}) collective-permute-start(bf16[4,192,384]{2,1,0:T(8,128)(2,1)S(1)} %all_to_all.21.refs_0_.refs_1_), channel_id=1, source_target_pairs={{0,1},{1,0},{2,3},{3,2},{4,5},{5,4},{6,7},{7,6},{8,9},{9,8},{10,11... | collective-permute-start | bytes 1769480 | tf_op jit(solution)/shard_map/ppermute | solution.py:337
  110.4 6.4 %copy-start.10 = (s32[64,8]{0,1:T(8,128)S(1)}, s32[64,8]{0,1:T(8,128)}, u32[]{:S(2)}) copy-start(s32[64,8]{0,1:T(8,128)} %param.6) | copy-start | bytes 6148
  110.5 6.4 %copy-start.11 = (f32[64,8]{0,1:T(8,128)S(1)}, f32[64,8]{0,1:T(8,128)}, u32[]{:S(2)}) copy-start(f32[64,8]{0,1:T(8,128)} %param.7) | copy-start | bytes 6148
  110.5 46.6 %all-to-all-start.3 = ((bf16[64,48,128]{2,1,0:T(8,128)(2,1)}), bf16[64,48,128]{2,1,0:T(8,128)(2,1)S(1)}, u32[]{:S(2)}, u32[]{:S(2)}) async-start(bf16[64,48,128]{2,1,0:T(8,128)(2,1)} %shard_map.75.refs_2_), calls=%async_computation.3 | async-start | bytes 1572864 | tf_op jit(solution)/shard_map/all_to_all | solution.py:354

commit v4 on v3

--- a/solution.py
+++ b/solution.py
@@ -23,6 +23,8 @@
 ROWS = EXPERTS * CAP
 UNITS = 96
 EMPTY = 64.0
+SENT = [16 * ((y + 3) % 4) + (z + 11) % 16 for y in range(4) for z in range(16)]
+BACK = [16 * ((y + 2) % 4) + (z + 8) % 16 for y in range(4) for z in range(16)]
 NT = (((1,), (1,)), ((), ()))
 TN = (((0,), (0,)), ((), ()))
 
@@ -79,13 +81,13 @@
     for c in range(EXPERTS // GROUP):
         picks = [
             jnp.where(code[e : e + 1, :] == target, 1.0, 0.0).astype(BF)
-            for e in range(c * GROUP, (c + 1) * GROUP)
+            for e in SENT[c * GROUP : (c + 1) * GROUP]
         ]
         rows = dot(jnp.concatenate(picks, axis=0), slabs)
         for j in range(GROUP):
-            e = c * GROUP + j
+            e = SENT[c * GROUP + j]
             block = rows[j * PACK : (j + 1) * PACK]
-            out_ref[e] = jnp.where(first >= count[e : e + 1, :], EMPTY, block).astype(BF)
+            out_ref[c * GROUP + j] = jnp.where(first >= count[e : e + 1, :], EMPTY, block).astype(BF)
         at = slice(c * GROUP, (c + 1) * GROUP)
         sends.append(pltpu.make_async_copy(out_ref.at[at], out_hbm.at[at], out_sems.at[c]))
         sends[-1].start()
@@ -139,8 +141,11 @@
 def unpack_kernel(in_ref, rows_ref, scale_ref):
     perm = repack_matrix(False)
     empty = jnp.zeros((GROWS, 2 * LANES), F32)
+    place = [SENT.index(source) for source in BACK]
     for h in range(EXPERTS // GROUP // 2):
-        pair = [in_ref[g * GROUP : (g + 1) * GROUP].reshape(GPACK, LANES) for g in (2 * h, 2 * h + 1)]
+        pair = [
+            jnp.concatenate([in_ref[place[g * GROUP + j]] for j in range(GROUP)], axis=0) for g in (2 * h, 2 * h + 1)
+        ]
         y = dot(perm, jnp.concatenate(pair, axis=1))
         first = y[:GROWS]
         gone = first > 0.5 * EMPTY
@@ -234,7 +239,7 @@
     target = (p + 4 * slab).astype(F32)
     q = iota((EXPERTS, GPACK), 1)
     for g in range(EXPERTS // GROUP):
-        e = iota((EXPERTS, GPACK), 0) - g * GROUP
+        e = iota((EXPERTS, GPACK), 0) - BACK[g * GROUP]
         spread = jnp.where((q >= e * PACK) & (q < (e + 1) * PACK), 1.0, 0.0).astype(BF)
         pick = jnp.where(dot(code, spread, TN) == target, dot(share, spread, TN), 0.0)
         out_ref[:, g * GPACK : (g + 1) * GPACK] = pick.astype(BF)
@@ -317,7 +322,7 @@
         flops=2 * 10**8,
         size=10**6,
     )
-    arrived = lax.all_to_all(outgoing, "expert", 0, 0)
+    arrived = lax.all_to_all(outgoing, "expert", 0, 0, axis_index_groups=[SENT])
     mine, scale = call(
         unpack_kernel,
         (shape((ROWS, half)), shape((8, LANES), F32)),
@@ -351,7 +356,7 @@
         flops=6 * 10**8,
         size=3 * 10**6,
     )
-    returned = lax.all_to_all(returning, "expert", 0, 0)
+    returned = lax.all_to_all(returning, "expert", 0, 0, axis_index_groups=[BACK])
     hessian = call(
         gram_kernel,
         shape((UNITS, 2 * CHIPS * UNITS), F32),

time: 161 us -> 156 us (0.969); the launches traced: 158 us -> 156 us
  waiting for transfers between devices: 55.3 us -> 45.6 us
  starting transfers between devices: 47 us -> 54.1 us
    all_to_all x2, waiting for transfers between devices: 40.3 us -> 30.6 us  [the longest x1 28.7 us: body(): lax.all_to_all(returning, 'expert', 0, 0, axis_index_groups=[BACK])]
    all_to_all x2, starting transfers between devices: 25.7 us -> 35 us  [the longest x1 20.1 us: body(): arrived = lax.all_to_all(outgoing, 'expert', 0, 0, axis_index_groups=[SENT])]
    ppermute x1, starting transfers between devices: 5.97 us -> 3.76 us  [body(): theirs = lax.ppermute(mine, 'hidden', swap)]
where the time goes in v4:
time: 156 us
  starting transfers between devices  54.1 us (35%)
  waiting for transfers between devices  45.6 us (29%)
  blocking collectives  30.1 us (19%)
  Pallas kernels  16.5 us (11%)
  local copies, waits for them, and re-layouts  8.22 us (5%)
    all_to_all x1, waiting for transfers between devices, body(): lax.all_to_all(returning, 'expert', 0, 0, axis_index_groups=[BACK])  28.7 us
    all_to_all x1, starting transfers between devices, body(): arrived = lax.all_to_all(outgoing, 'expert', 0, 0, axis_index_groups=[SENT])  20.1 us
    all_to_all x1, blocking collectives, body(): parts = lax.all_to_all(part, 'hidden', 0, 0, axis_index_groups=groups)  19.4 us
    pallas_call x11, Pallas kernels, call(): pl.pallas_call(run, out_shape=outs, in_specs=(specs or ([SMEM] if smem el...  16.5 us
    all_to_all x1, starting transfers between devices, body(): lax.all_to_all(returning, 'expert', 0, 0, axis_index_groups=[BACK])  14.8 us
    ppermute x3, waiting for transfers between devices, body(): lax.ppermute(piece, 'hidden', [(i, (i + 2 * k) % (2 * CHIPS)) for i in ra...  12.9 us
    all_to_all x1, blocking collectives, body(): own = lax.all_to_all(copies, 'hidden', 0, 0, axis_index_groups=groups)  10.7 us
    ppermute x3, starting transfers between devices, body(): lax.ppermute(piece, 'hidden', [(i, (i + 2 * k) % (2 * CHIPS)) for i in ra...  10.5 us
  transfers between devices with their start and end apart: 7, of which 7 were waited for; matrix products, arithmetic and copies ran while one was open for 1% of the time, Pallas kernels for 6%

profile of v4, /device:TPU:1, one launch (start us, length us, event | category | flops | bytes accessed | tf_op | source)
XLA Modules:
  0.0 155.6 jit_solution(16262741037138411676)
XLA Ops:
  0.6 0.0 copy-start
  0.6 2.5 %shard_map.68 = bf16[64,48,128]{2,1,0:T(8,128)(2,1)} custom-call(bf16[64,512]{1,0:T(8,128)(2,1)} %refs_0_.1, s32[8,64]{1,0:T(8,128)} %bitcast.10), custom_call_target="tpu_custom_call" | custom-call | flops 200000000 | bytes 1000000 | tf_op jit(solution)/shard_map/pallas_call | solution.py:266
  3.1 20.1 %all-to-all-start = ((bf16[64,48,128]{2,1,0:T(8,128)(2,1)}), bf16[64,48,128]{2,1,0:T(8,128)(2,1)S(1)}, u32[]{:S(2)}, u32[]{:S(2)}) async-start(bf16[64,48,128]{2,1,0:T(8,128)(2,1)} %shard_map.68), calls=%async_computation | async-start | bytes 1572864 | tf_op jit(solution)/shard_map/all_to_all | solution.py:325
  23.3 0.0 copy-done
  23.3 1.1 constant_dynamic-slice_fusion
  24.4 3.1 %collective-permute-start = (bf16[192,1024]{1,0:T(8,128)(2,1)}, bf16[192,1024]{1,0:T(8,128)(2,1)S(1)}, u32[]{:S(2)}, u32[]{:S(2)}) collective-permute-start(bf16[192,1024]{1,0:T(8,128)(2,1)} %get-tuple-element.22), channel_id=1, source_target_pairs={{0,2},{1,3},{2,4},{3,5},{4,6},{5,7},{6,0},{7,1},{8,10},{9,11},{10,... | collective-permute-start | bytes 1179656 | tf_op jit(solution)/shard_map/ppermute | solution.py:295
  27.5 4.4 %collective-permute-start.1 = (bf16[192,1024]{1,0:T(8,128)(2,1)}, bf16[192,1024]{1,0:T(8,128)(2,1)S(1)}, u32[]{:S(2)}, u32[]{:S(2)}) collective-permute-start(bf16[192,1024]{1,0:T(8,128)(2,1)} %get-tuple-element.21), channel_id=1, source_target_pairs={{0,4},{1,5},{2,6},{3,7},{4,0},{5,1},{6,2},{7,3},{8,12},{9,13},{10,... | collective-permute-start | bytes 1179656 | tf_op jit(solution)/shard_map/ppermute | solution.py:295
  31.9 3.1 %collective-permute-start.2 = (bf16[192,1024]{1,0:T(8,128)(2,1)}, bf16[192,1024]{1,0:T(8,128)(2,1)S(1)}, u32[]{:S(2)}, u32[]{:S(2)}) collective-permute-start(bf16[192,1024]{1,0:T(8,128)(2,1)} %get-tuple-element.20), channel_id=1, source_target_pairs={{0,6},{1,7},{2,0},{3,1},{4,2},{5,3},{6,4},{7,5},{8,14},{9,15},{10,... | collective-permute-start | bytes 1179656 | tf_op jit(solution)/shard_map/ppermute | solution.py:295
  35.0 0.1 pad_add_fusion.refs_0_
  35.0 2.0 %collective-permute-done.refs_2_ = bf16[192,1024]{1,0:T(8,128)(2,1)S(1)} collective-permute-done((bf16[192,1024]{1,0:T(8,128)(2,1)}, bf16[192,1024]{1,0:T(8,128)(2,1)S(1)}, u32[]{:S(2)}, u32[]{:S(2)}) %collective-permute-start) | collective-permute-done | bytes 393248 | tf_op jit(solution)/shard_map/ppermute | solution.py:295
  37.1 9.4 %collective-permute-done.1.refs_3_ = bf16[192,1024]{1,0:T(8,128)(2,1)S(1)} collective-permute-done((bf16[192,1024]{1,0:T(8,128)(2,1)}, bf16[192,1024]{1,0:T(8,128)(2,1)S(1)}, u32[]{:S(2)}, u32[]{:S(2)}) %collective-permute-start.1) | collective-permute-done | bytes 393248 | tf_op jit(solution)/shard_map/ppermute | solution.py:295
  46.5 0.8 copy-done.6
  47.3 1.5 collective-permute-done.2.refs_4_
  48.7 0.8 copy-done.8
  49.5 1.1 copy-done.1
  50.6 1.0 copy-done.7
  51.6 1.0 copy-done.9
  52.6 2.3 %shard_map.69 = (bf16[768,512]{1,0:T(8,128)(2,1)S(1)}, bf16[768,512]{1,0:T(8,128)(2,1)S(1)}, bf16[384,512]{1,0:T(8,128)(2,1)S(1)}, bf16[384,512]{1,0:T(8,128)(2,1)S(1)}, f32[8,128]{1,0:T(8,128)S(1)}) custom-call(s32[2]{0:T(128)S(1)} %pad_add_fusion.refs_0_, bf16[192,4096]{1,0:T(8,128)(2,1)S(1)} %bitcast.8, ...), custom_call_target="tpu_custom_call" | custom-call | bytes 5000000 | tf_op jit(solution)/shard_map/pallas_call | solution.py:266
  55.0 0.0 copy-start.2
  55.0 0.9 copy-done.2
  55.9 0.8 copy-done.4
  56.7 0.7 copy-done.12
  57.4 1.9 %all-to-all-done.refs_0_ = bf16[64,48,128]{2,1,0:T(8,128)(2,1)S(1)} async-done(((bf16[64,48,128]{2,1,0:T(8,128)(2,1)}), bf16[64,48,128]{2,1,0:T(8,128)(2,1)S(1)}, u32[]{:S(2)}, u32[]{:S(2)}) %all-to-all-start) | async-done | bytes 786464 | tf_op jit(solution)/shard_map/all_to_all | solution.py:325
  59.3 0.6 shard_map.70
  59.9 3.8 %collective-permute-start.3 = (bf16[768,512]{1,0:T(8,128)(2,1)S(1)}, bf16[768,512]{1,0:T(8,128)(2,1)S(1)}, u32[]{:S(2)}, u32[]{:S(2)}) collective-permute-start(bf16[768,512]{1,0:T(8,128)(2,1)S(1)} %get-tuple-element.12.refs_0_), channel_id=1, source_target_pairs={{0,1},{1,0},{2,3},{3,2},{4,5},{5,4},{6,7},{7,6},{8,9},{9,8},{10,11... | collective-permute-start | bytes 2359304 | tf_op jit(solution)/shard_map/ppermute | solution.py:334
  63.7 0.0 copy-done.3
  63.7 0.8 shard_map.71.refs_2_
  64.5 1.1 collective-permute-done.3.refs_0_
  65.6 1.2 shard_map.72
  66.7 19.4 %all_to_all.20.refs_0_ = bf16[4,192,768]{2,1,0:T(8,128)(2,1)S(1)} all-to-all(bf16[4,192,768]{2,1,0:T(8,128)(2,1)S(1)} %shard_map.72), channel_id=1, replica_groups={{0,2,4,6},{1,3,5,7},{8,10,12,14},{9,11,13,15},{16,18,20,22},{17,19,21,2..., dimensions={0} | all-to-all | bytes 2359296 | tf_op jit(solution)/shard_map/all_to_all | solution.py:339
  86.2 0.2 shard_map.73
  86.4 0.0 copy-start.5
  86.4 10.7 %all_to_all.21.refs_0_.refs_1_ = bf16[4,192,384]{2,1,0:T(8,128)(2,1)S(1)} all-to-all(bf16[4,192,384]{2,1,0:T(8,128)(2,1)S(1)} %shard_map.73), channel_id=1, replica_groups={{0,2,4,6},{1,3,5,7},{8,10,12,14},{9,11,13,15},{16,18,20,22},{17,19,21,2..., dimensions={0} | all-to-all | bytes 1179648 | tf_op jit(solution)/shard_map/all_to_all | solution.py:341
  97.1 4.9 %collective-permute-start.4 = (bf16[4,192,384]{2,1,0:T(8,128)(2,1)S(1)}, bf16[4,192,384]{2,1,0:T(8,128)(2,1)S(1)}, u32[]{:S(2)}, u32[]{:S(2)}) collective-permute-start(bf16[4,192,384]{2,1,0:T(8,128)(2,1)S(1)} %all_to_all.21.refs_0_.refs_1_), channel_id=1, source_target_pairs={{0,1},{1,0},{2,3},{3,2},{4,5},{5,4},{6,7},{7,6},{8,9},{9,8},{10,11... | collective-permute-start | bytes 1769480 | tf_op jit(solution)/shard_map/ppermute | solution.py:342
  102.0 0.0 copy-done.13
  102.0 0.6 shard_map.74
  102.6 1.0 collective-permute-done.4.refs_0_.refs_2_
  103.6 0.0 copy-done.5
  103.6 1.8 %shard_map.75.refs_2_ = bf16[64,48,128]{2,1,0:T(8,128)(2,1)} custom-call(bf16[4,192,384]{2,1,0:T(8,128)(2,1)S(1)} %collective-permute-done.4.refs_0_.refs_2_, bf16[384,512]{1,0:T(8,128)(2,1)S(1)} %copy-done.5, f32[768,512]{1,0:T(8,128)S(1)} %get-tuple-element.17.refs_2_, bf16[384,384]{1,0:T(8,128)(2,1)S(1)} %get-tuple-element.18.refs_3_), custom_call_target="tpu_custom_call" | custom-call | flops 600000000 | bytes 3000000 | tf_op jit(solution)/shard_map/pallas_call | solution.py:266
  105.3 0.0 copy-start.10
  105.4 0.0 copy-start.11
  105.4 14.8 %all-to-all-start.3 = ((bf16[64,48,128]{2,1,0:T(8,128)(2,1)}), bf16[64,48,128]{2,1,0:T(8,128)(2,1)S(1)}, u32[]{:S(2)}, u32[]{:S(2)}) async-start(bf16[64,48,128]{2,1,0:T(8,128)(2,1)} %shard_map.75.refs_2_), calls=%async_computation.3 | async-start | bytes 1572864 | tf_op jit(solution)/shard_map/all_to_all | solution.py:359
  120.2 0.0 copy-done.10
  120.2 0.0 copy-done.11
  120.2 1.3 shard_map.76.refs_0_
  121.6 4.2 %shard_map.78 = f32[96,768]{1,0:T(8,128)} custom-call(s32[2]{0:T(128)S(1)} %pad_add_fusion.refs_0_, bf16[4,192,384]{2,1,0:T(8,128)(2,1)S(1)} %all_to_all.21.refs_0_.refs_1_, bf16[4,192,384]{2,1,0:T(8,128)(2,1)S(1)} %collective-permute-done.4.refs_0_.refs_2_, f32[8,128]{1,0:T(8,128)S(1)} %get-tuple-element.19.refs_3_), custom_call_target="tpu_custom_call" | custom-call | flops 2000000000 | bytes 3000000 | tf_op jit(solution)/shard_map/pallas_call | solution.py:266
  125.7 28.7 %all-to-all-done.3.refs_1_ = bf16[64,48,128]{2,1,0:T(8,128)(2,1)S(1)} async-done(((bf16[64,48,128]{2,1,0:T(8,128)(2,1)}), bf16[64,48,128]{2,1,0:T(8,128)(2,1)S(1)}, u32[]{:S(2)}, u32[]{:S(2)}) %all-to-all-start.3) | async-done | bytes 786464 | tf_op jit(solution)/shard_map/all_to_all | solution.py:359
  154.5 1.2 shard_map.77
  (9 shorter events, 0.0 us)
Async XLA Ops:
  0.6 22.7 %copy-start = (bf16[1,2,96,4096]{3,2,1,0:T(8,128)(2,1)S(1)}, bf16[1,2,96,4096]{3,2,1,0:T(8,128)(2,1)}, u32[]{:S(2)}) copy-start(bf16[1,2,96,4096]{3,2,1,0:T(8,128)(2,1)} %param.8) | copy-start | bytes 4718596
  3.1 56.2 %all-to-all-start = ((bf16[64,48,128]{2,1,0:T(8,128)(2,1)}), bf16[64,48,128]{2,1,0:T(8,128)(2,1)S(1)}, u32[]{:S(2)}, u32[]{:S(2)}) async-start(bf16[64,48,128]{2,1,0:T(8,128)(2,1)} %shard_map.68), calls=%async_computation | async-start | bytes 1572864 | tf_op jit(solution)/shard_map/all_to_all | solution.py:325
  24.4 12.7 %collective-permute-start = (bf16[192,1024]{1,0:T(8,128)(2,1)}, bf16[192,1024]{1,0:T(8,128)(2,1)S(1)}, u32[]{:S(2)}, u32[]{:S(2)}) collective-permute-start(bf16[192,1024]{1,0:T(8,128)(2,1)} %get-tuple-element.22), channel_id=1, source_target_pairs={{0,2},{1,3},{2,4},{3,5},{4,6},{5,7},{6,0},{7,1},{8,10},{9,11},{10,... | collective-permute-start | bytes 1179656 | tf_op jit(solution)/shard_map/ppermute | solution.py:295
  27.5 19.0 %collective-permute-start.1 = (bf16[192,1024]{1,0:T(8,128)(2,1)}, bf16[192,1024]{1,0:T(8,128)(2,1)S(1)}, u32[]{:S(2)}, u32[]{:S(2)}) collective-permute-start(bf16[192,1024]{1,0:T(8,128)(2,1)} %get-tuple-element.21), channel_id=1, source_target_pairs={{0,4},{1,5},{2,6},{3,7},{4,0},{5,1},{6,2},{7,3},{8,12},{9,13},{10,... | collective-permute-start | bytes 1179656 | tf_op jit(solution)/shard_map/ppermute | solution.py:295
  31.9 16.9 %collective-permute-start.2 = (bf16[192,1024]{1,0:T(8,128)(2,1)}, bf16[192,1024]{1,0:T(8,128)(2,1)S(1)}, u32[]{:S(2)}, u32[]{:S(2)}) collective-permute-start(bf16[192,1024]{1,0:T(8,128)(2,1)} %get-tuple-element.20), channel_id=1, source_target_pairs={{0,6},{1,7},{2,0},{3,1},{4,2},{5,3},{6,4},{7,5},{8,14},{9,15},{10,... | collective-permute-start | bytes 1179656 | tf_op jit(solution)/shard_map/ppermute | solution.py:295
  46.5 0.8 copy-start.6
  48.7 0.8 copy-start.8
  49.5 1.1 copy-start.1
  50.6 1.0 copy-start.7
  51.6 1.0 copy-start.9
  55.0 0.9 copy-start.2
  55.9 0.8 copy-start.4
  56.7 0.7 copy-start.12
  59.3 4.4 %copy-start.3 = (bf16[768,512]{1,0:T(8,128)(2,1)S(1)}, bf16[768,512]{1,0:T(8,128)(2,1)}, u32[]{:S(2)}) copy-start(bf16[768,512]{1,0:T(8,128)(2,1)} %copy-done.2) | copy-start | bytes 2359300
  59.9 5.7 %collective-permute-start.3 = (bf16[768,512]{1,0:T(8,128)(2,1)S(1)}, bf16[768,512]{1,0:T(8,128)(2,1)S(1)}, u32[]{:S(2)}, u32[]{:S(2)}) collective-permute-start(bf16[768,512]{1,0:T(8,128)(2,1)S(1)} %get-tuple-element.12.refs_0_), channel_id=1, source_target_pairs={{0,1},{1,0},{2,3},{3,2},{4,5},{5,4},{6,7},{7,6},{8,9},{9,8},{10,11... | collective-permute-start | bytes 2359304 | tf_op jit(solution)/shard_map/ppermute | solution.py:334
  86.2 15.8 %copy-start.13 = (bf16[384,512]{1,0:T(8,128)(2,1)S(1)}, bf16[384,512]{1,0:T(8,128)(2,1)}, u32[]{:S(2)}) copy-start(bf16[384,512]{1,0:T(8,128)(2,1)} %copy-done.12) | copy-start | bytes 1179652
  86.4 17.2 %copy-start.5 = (bf16[384,512]{1,0:T(8,128)(2,1)S(1)}, bf16[384,512]{1,0:T(8,128)(2,1)}, u32[]{:S(2)}) copy-start(bf16[384,512]{1,0:T(8,128)(2,1)} %copy-done.4) | copy-start | bytes 1179652
  97.1 6.5 %collective-permute-start.4 = (bf16[4,192,384]{2,1,0:T(8,128)(2,1)S(1)}, bf16[4,192,384]{2,1,0:T(8,128)(2,1)S(1)}, u32[]{:S(2)}, u32[]{:S(2)}) collective-permute-start(bf16[4,192,384]{2,1,0:T(8,128)(2,1)S(1)} %all_to_all.21.refs_0_.refs_1_), channel_id=1, source_target_pairs={{0,1},{1,0},{2,3},{3,2},{4,5},{5,4},{6,7},{7,6},{8,9},{9,8},{10,11... | collective-permute-start | bytes 1769480 | tf_op jit(solution)/shard_map/ppermute | solution.py:342
  105.3 14.9 %copy-start.10 = (s32[64,8]{0,1:T(8,128)S(1)}, s32[64,8]{0,1:T(8,128)}, u32[]{:S(2)}) copy-start(s32[64,8]{0,1:T(8,128)} %param.6) | copy-start | bytes 6148
  105.4 14.9 %copy-start.11 = (f32[64,8]{0,1:T(8,128)S(1)}, f32[64,8]{0,1:T(8,128)}, u32[]{:S(2)}) copy-start(f32[64,8]{0,1:T(8,128)} %param.7) | copy-start | bytes 6148
  105.4 49.1 %all-to-all-start.3 = ((bf16[64,48,128]{2,1,0:T(8,128)(2,1)}), bf16[64,48,128]{2,1,0:T(8,128)(2,1)S(1)}, u32[]{:S(2)}, u32[]{:S(2)}) async-start(bf16[64,48,128]{2,1,0:T(8,128)(2,1)} %shard_map.75.refs_2_), calls=%async_computation.3 | async-start | bytes 1572864 | tf_op jit(solution)/shard_map/all_to_all | solution.py:359

commit v5 on v4

--- a/solution.py
+++ b/solution.py
@@ -64,23 +64,31 @@
     fetch_ids.start()
     fetch = pltpu.make_async_copy(tok_hbm, tok_ref, tok_sem)
     fetch.start()
-    wide = SLABS * TOK
-    p = iota((PACK, wide), 0)
+    p = iota((PACK, LANES), 0)
     slab = (p >= CAP).astype(I32) + (p >= 2 * CAP).astype(I32) + (p >= 3 * CAP).astype(I32)
     target = (p + 4 * slab).astype(F32)
-    q = iota((PACK, LANES), 0)
-    first = jnp.where(q < CAP, q, -1).astype(F32)
+    first = jnp.where(p < CAP, p, -1).astype(F32)
+    expert, token = iota((EXPERTS, LANES), 0), iota((EXPERTS, LANES), 1)
+    before = jnp.where(iota((TOK, LANES), 0) < (iota((TOK, LANES), 1) & (TOK - 1)), 1.0, 0.0).astype(BF)
     fetch_ids.wait()
-    code, member, _ = codes(ids_ref[...])
-    ones = jnp.where(iota((wide, LANES), 0) < TOK, 1.0, 0.0).astype(BF)
-    count = dot(member.astype(BF), ones)
+    ids = ids_ref[...]
+    ids = jnp.concatenate([ids, ids], axis=1)
+    member = jnp.zeros((EXPERTS, LANES), F32)
+    for k in range(TOP):
+        member = member + jnp.where(ids[k : k + 1, :] == expert, 1.0, 0.0)
+    single = member[:, :TOK].astype(BF)
+    slot = dot(single, before)
+    code = jnp.where(member > 0.5, slot + 16.0 * (token >> 6).astype(F32), -1.0)
+    count = dot(single, jnp.ones((TOK, LANES), BF))
     fetch.wait()
     tok = tok_ref[...]
     slabs = jnp.concatenate([tok[:, l * LANES : (l + 1) * LANES] for l in range(SLABS)], axis=0)
     sends = []
     for c in range(EXPERTS // GROUP):
         picks = [
-            jnp.where(code[e : e + 1, :] == target, 1.0, 0.0).astype(BF)
+            jnp.concatenate(
+                [jnp.where(code[e : e + 1, :] == target - 32.0 * i, 1.0, 0.0).astype(BF) for i in range(2)], axis=1
+            )
             for e in SENT[c * GROUP : (c + 1) * GROUP]
         ]
         rows = dot(jnp.concatenate(picks, axis=0), slabs)
@@ -284,7 +292,7 @@
     where = jnp.stack([x, c]).astype(I32)
     half = SLABS * LANES
     wide = 2 * half
-    groups = [[2 * i + j for i in range(CHIPS)] for j in range(2)]
+    groups = [[2 * i + j for i in (0, 2, 1, 3)] for j in range(2)]
     swap = [(i, i ^ 1) for i in range(2 * CHIPS)]
 
     units = CHIPS * UNITS

time: 156 us -> 156 us (level)
  no operation moved by 1% of the time
where the time goes in v5:
time: 156 us; the launch traced here: 155 us
  starting transfers between devices  54.3 us (35%)
  waiting for transfers between devices  45.6 us (29%)
  blocking collectives  29.6 us (19%)
  Pallas kernels  16.5 us (11%)
  local copies, waits for them, and re-layouts  8.22 us (5%)
    all_to_all x1, waiting for transfers between devices, body(): lax.all_to_all(returning, 'expert', 0, 0, axis_index_groups=[BACK])  28.7 us
    all_to_all x1, starting transfers between devices, body(): arrived = lax.all_to_all(outgoing, 'expert', 0, 0, axis_index_groups=[SENT])  20.1 us
    all_to_all x1, blocking collectives, body(): parts = lax.all_to_all(part, 'hidden', 0, 0, axis_index_groups=groups)  19.2 us
    pallas_call x11, Pallas kernels, call(): pl.pallas_call(run, out_shape=outs, in_specs=(specs or ([SMEM] if smem el...  16.5 us
    all_to_all x1, starting transfers between devices, body(): lax.all_to_all(returning, 'expert', 0, 0, axis_index_groups=[BACK])  14.8 us
    ppermute x3, waiting for transfers between devices, body(): lax.ppermute(piece, 'hidden', [(i, (i + 2 * k) % (2 * CHIPS)) for i in ra...  12.9 us
    ppermute x3, starting transfers between devices, body(): lax.ppermute(piece, 'hidden', [(i, (i + 2 * k) % (2 * CHIPS)) for i in ra...  10.5 us
    all_to_all x1, blocking collectives, body(): own = lax.all_to_all(copies, 'hidden', 0, 0, axis_index_groups=groups)  10.4 us
  transfers between devices with their start and end apart: 7, of which 7 were waited for; matrix products, arithmetic and copies ran while one was open for 1% of the time, Pallas kernels for 6%

profile of v5, /device:TPU:1, one launch (start us, length us, event | category | flops | bytes accessed | tf_op | source)
XLA Modules:
  0.0 155.3 jit_solution(2191375728336236659)
XLA Ops:
  0.6 0.0 copy-start
  0.6 2.4 %shard_map.68 = bf16[64,48,128]{2,1,0:T(8,128)(2,1)} custom-call(bf16[64,512]{1,0:T(8,128)(2,1)} %refs_0_.1, s32[8,64]{1,0:T(8,128)} %bitcast.10), custom_call_target="tpu_custom_call" | custom-call | flops 200000000 | bytes 1000000 | tf_op jit(solution)/shard_map/pallas_call | solution.py:274
  3.0 20.1 %all-to-all-start = ((bf16[64,48,128]{2,1,0:T(8,128)(2,1)}), bf16[64,48,128]{2,1,0:T(8,128)(2,1)S(1)}, u32[]{:S(2)}, u32[]{:S(2)}) async-start(bf16[64,48,128]{2,1,0:T(8,128)(2,1)} %shard_map.68), calls=%async_computation | async-start | bytes 1572864 | tf_op jit(solution)/shard_map/all_to_all | solution.py:333
  23.2 0.0 copy-done
  23.2 1.1 constant_dynamic-slice_fusion
  24.3 3.1 %collective-permute-start = (bf16[192,1024]{1,0:T(8,128)(2,1)}, bf16[192,1024]{1,0:T(8,128)(2,1)S(1)}, u32[]{:S(2)}, u32[]{:S(2)}) collective-permute-start(bf16[192,1024]{1,0:T(8,128)(2,1)} %get-tuple-element.22), channel_id=1, source_target_pairs={{0,2},{1,3},{2,4},{3,5},{4,6},{5,7},{6,0},{7,1},{8,10},{9,11},{10,... | collective-permute-start | bytes 1179656 | tf_op jit(solution)/shard_map/ppermute | solution.py:303
  27.4 4.4 %collective-permute-start.1 = (bf16[192,1024]{1,0:T(8,128)(2,1)}, bf16[192,1024]{1,0:T(8,128)(2,1)S(1)}, u32[]{:S(2)}, u32[]{:S(2)}) collective-permute-start(bf16[192,1024]{1,0:T(8,128)(2,1)} %get-tuple-element.21), channel_id=1, source_target_pairs={{0,4},{1,5},{2,6},{3,7},{4,0},{5,1},{6,2},{7,3},{8,12},{9,13},{10,... | collective-permute-start | bytes 1179656 | tf_op jit(solution)/shard_map/ppermute | solution.py:303
  31.8 3.1 %collective-permute-start.2 = (bf16[192,1024]{1,0:T(8,128)(2,1)}, bf16[192,1024]{1,0:T(8,128)(2,1)S(1)}, u32[]{:S(2)}, u32[]{:S(2)}) collective-permute-start(bf16[192,1024]{1,0:T(8,128)(2,1)} %get-tuple-element.20), channel_id=1, source_target_pairs={{0,6},{1,7},{2,0},{3,1},{4,2},{5,3},{6,4},{7,5},{8,14},{9,15},{10,... | collective-permute-start | bytes 1179656 | tf_op jit(solution)/shard_map/ppermute | solution.py:303
  34.9 0.1 pad_add_fusion.refs_0_
  35.0 2.0 %collective-permute-done.refs_2_ = bf16[192,1024]{1,0:T(8,128)(2,1)S(1)} collective-permute-done((bf16[192,1024]{1,0:T(8,128)(2,1)}, bf16[192,1024]{1,0:T(8,128)(2,1)S(1)}, u32[]{:S(2)}, u32[]{:S(2)}) %collective-permute-start) | collective-permute-done | bytes 393248 | tf_op jit(solution)/shard_map/ppermute | solution.py:303
  37.0 9.4 %collective-permute-done.1.refs_3_ = bf16[192,1024]{1,0:T(8,128)(2,1)S(1)} collective-permute-done((bf16[192,1024]{1,0:T(8,128)(2,1)}, bf16[192,1024]{1,0:T(8,128)(2,1)S(1)}, u32[]{:S(2)}, u32[]{:S(2)}) %collective-permute-start.1) | collective-permute-done | bytes 393248 | tf_op jit(solution)/shard_map/ppermute | solution.py:303
  46.4 0.8 copy-done.6
  47.2 1.5 collective-permute-done.2.refs_4_
  48.7 0.8 copy-done.8
  49.4 1.1 copy-done.1
  50.6 1.0 copy-done.7
  51.6 1.0 copy-done.9
  52.6 2.3 %shard_map.69 = (bf16[768,512]{1,0:T(8,128)(2,1)S(1)}, bf16[768,512]{1,0:T(8,128)(2,1)S(1)}, bf16[384,512]{1,0:T(8,128)(2,1)S(1)}, bf16[384,512]{1,0:T(8,128)(2,1)S(1)}, f32[8,128]{1,0:T(8,128)S(1)}) custom-call(s32[2]{0:T(128)S(1)} %pad_add_fusion.refs_0_, bf16[192,4096]{1,0:T(8,128)(2,1)S(1)} %bitcast.8, ...), custom_call_target="tpu_custom_call" | custom-call | bytes 5000000 | tf_op jit(solution)/shard_map/pallas_call | solution.py:274
  54.9 0.0 copy-start.2
  54.9 0.9 copy-done.2
  55.8 0.8 copy-done.4
  56.6 0.7 copy-done.12
  57.3 1.9 %all-to-all-done.refs_0_ = bf16[64,48,128]{2,1,0:T(8,128)(2,1)S(1)} async-done(((bf16[64,48,128]{2,1,0:T(8,128)(2,1)}), bf16[64,48,128]{2,1,0:T(8,128)(2,1)S(1)}, u32[]{:S(2)}, u32[]{:S(2)}) %all-to-all-start) | async-done | bytes 786464 | tf_op jit(solution)/shard_map/all_to_all | solution.py:333
  59.2 0.6 shard_map.70
  59.8 3.8 %collective-permute-start.3 = (bf16[768,512]{1,0:T(8,128)(2,1)S(1)}, bf16[768,512]{1,0:T(8,128)(2,1)S(1)}, u32[]{:S(2)}, u32[]{:S(2)}) collective-permute-start(bf16[768,512]{1,0:T(8,128)(2,1)S(1)} %get-tuple-element.12.refs_0_), channel_id=1, source_target_pairs={{0,1},{1,0},{2,3},{3,2},{4,5},{5,4},{6,7},{7,6},{8,9},{9,8},{10,11... | collective-permute-start | bytes 2359304 | tf_op jit(solution)/shard_map/ppermute | solution.py:342
  63.6 0.0 copy-done.3
  63.6 0.8 shard_map.71.refs_2_
  64.4 1.1 collective-permute-done.3.refs_0_
  65.5 1.2 shard_map.72
  66.7 19.2 %all_to_all.20.refs_0_ = bf16[4,192,768]{2,1,0:T(8,128)(2,1)S(1)} all-to-all(bf16[4,192,768]{2,1,0:T(8,128)(2,1)S(1)} %shard_map.72), channel_id=1, replica_groups={{0,4,2,6},{1,5,3,7},{8,12,10,14},{9,13,11,15},{16,20,18,22},{17,21,19,2..., dimensions={0} | all-to-all | bytes 2359296 | tf_op jit(solution)/shard_map/all_to_all | solution.py:347
  85.9 0.2 shard_map.73
  86.1 0.0 copy-start.5
  86.1 10.4 %all_to_all.21.refs_0_.refs_1_ = bf16[4,192,384]{2,1,0:T(8,128)(2,1)S(1)} all-to-all(bf16[4,192,384]{2,1,0:T(8,128)(2,1)S(1)} %shard_map.73), channel_id=1, replica_groups={{0,4,2,6},{1,5,3,7},{8,12,10,14},{9,13,11,15},{16,20,18,22},{17,21,19,2..., dimensions={0} | all-to-all | bytes 1179648 | tf_op jit(solution)/shard_map/all_to_all | solution.py:349
  96.5 5.0 %collective-permute-start.4 = (bf16[4,192,384]{2,1,0:T(8,128)(2,1)S(1)}, bf16[4,192,384]{2,1,0:T(8,128)(2,1)S(1)}, u32[]{:S(2)}, u32[]{:S(2)}) collective-permute-start(bf16[4,192,384]{2,1,0:T(8,128)(2,1)S(1)} %all_to_all.21.refs_0_.refs_1_), channel_id=1, source_target_pairs={{0,1},{1,0},{2,3},{3,2},{4,5},{5,4},{6,7},{7,6},{8,9},{9,8},{10,11... | collective-permute-start | bytes 1769480 | tf_op jit(solution)/shard_map/ppermute | solution.py:350
  101.6 0.0 copy-done.13
  101.6 0.6 shard_map.74
  102.2 1.0 collective-permute-done.4.refs_0_.refs_2_
  103.2 0.0 copy-done.5
  103.2 1.8 %shard_map.75.refs_2_ = bf16[64,48,128]{2,1,0:T(8,128)(2,1)} custom-call(bf16[4,192,384]{2,1,0:T(8,128)(2,1)S(1)} %collective-permute-done.4.refs_0_.refs_2_, bf16[384,512]{1,0:T(8,128)(2,1)S(1)} %copy-done.5, f32[768,512]{1,0:T(8,128)S(1)} %get-tuple-element.17.refs_2_, bf16[384,384]{1,0:T(8,128)(2,1)S(1)} %get-tuple-element.18.refs_3_), custom_call_target="tpu_custom_call" | custom-call | flops 600000000 | bytes 3000000 | tf_op jit(solution)/shard_map/pallas_call | solution.py:274
  105.0 0.0 copy-start.10
  105.0 0.0 copy-start.11
  105.0 14.8 %all-to-all-start.3 = ((bf16[64,48,128]{2,1,0:T(8,128)(2,1)}), bf16[64,48,128]{2,1,0:T(8,128)(2,1)S(1)}, u32[]{:S(2)}, u32[]{:S(2)}) async-start(bf16[64,48,128]{2,1,0:T(8,128)(2,1)} %shard_map.75.refs_2_), calls=%async_computation.3 | async-start | bytes 1572864 | tf_op jit(solution)/shard_map/all_to_all | solution.py:367
  119.8 0.0 copy-done.10
  119.8 0.0 copy-done.11
  119.9 1.3 shard_map.76.refs_0_
  121.2 4.2 %shard_map.78 = f32[96,768]{1,0:T(8,128)} custom-call(s32[2]{0:T(128)S(1)} %pad_add_fusion.refs_0_, bf16[4,192,384]{2,1,0:T(8,128)(2,1)S(1)} %all_to_all.21.refs_0_.refs_1_, bf16[4,192,384]{2,1,0:T(8,128)(2,1)S(1)} %collective-permute-done.4.refs_0_.refs_2_, f32[8,128]{1,0:T(8,128)S(1)} %get-tuple-element.19.refs_3_), custom_call_target="tpu_custom_call" | custom-call | flops 2000000000 | bytes 3000000 | tf_op jit(solution)/shard_map/pallas_call | solution.py:274
  125.4 28.7 %all-to-all-done.3.refs_1_ = bf16[64,48,128]{2,1,0:T(8,128)(2,1)S(1)} async-done(((bf16[64,48,128]{2,1,0:T(8,128)(2,1)}), bf16[64,48,128]{2,1,0:T(8,128)(2,1)S(1)}, u32[]{:S(2)}, u32[]{:S(2)}) %all-to-all-start.3) | async-done | bytes 786464 | tf_op jit(solution)/shard_map/all_to_all | solution.py:367
  154.1 1.2 shard_map.77
  (9 shorter events, 0.0 us)
Async XLA Ops:
  0.6 22.6 %copy-start = (bf16[1,2,96,4096]{3,2,1,0:T(8,128)(2,1)S(1)}, bf16[1,2,96,4096]{3,2,1,0:T(8,128)(2,1)}, u32[]{:S(2)}) copy-start(bf16[1,2,96,4096]{3,2,1,0:T(8,128)(2,1)} %param.8) | copy-start | bytes 4718596
  3.0 56.2 %all-to-all-start = ((bf16[64,48,128]{2,1,0:T(8,128)(2,1)}), bf16[64,48,128]{2,1,0:T(8,128)(2,1)S(1)}, u32[]{:S(2)}, u32[]{:S(2)}) async-start(bf16[64,48,128]{2,1,0:T(8,128)(2,1)} %shard_map.68), calls=%async_computation | async-start | bytes 1572864 | tf_op jit(solution)/shard_map/all_to_all | solution.py:333
  24.3 12.7 %collective-permute-start = (bf16[192,1024]{1,0:T(8,128)(2,1)}, bf16[192,1024]{1,0:T(8,128)(2,1)S(1)}, u32[]{:S(2)}, u32[]{:S(2)}) collective-permute-start(bf16[192,1024]{1,0:T(8,128)(2,1)} %get-tuple-element.22), channel_id=1, source_target_pairs={{0,2},{1,3},{2,4},{3,5},{4,6},{5,7},{6,0},{7,1},{8,10},{9,11},{10,... | collective-permute-start | bytes 1179656 | tf_op jit(solution)/shard_map/ppermute | solution.py:303
  27.4 19.0 %collective-permute-start.1 = (bf16[192,1024]{1,0:T(8,128)(2,1)}, bf16[192,1024]{1,0:T(8,128)(2,1)S(1)}, u32[]{:S(2)}, u32[]{:S(2)}) collective-permute-start(bf16[192,1024]{1,0:T(8,128)(2,1)} %get-tuple-element.21), channel_id=1, source_target_pairs={{0,4},{1,5},{2,6},{3,7},{4,0},{5,1},{6,2},{7,3},{8,12},{9,13},{10,... | collective-permute-start | bytes 1179656 | tf_op jit(solution)/shard_map/ppermute | solution.py:303
  31.8 16.9 %collective-permute-start.2 = (bf16[192,1024]{1,0:T(8,128)(2,1)}, bf16[192,1024]{1,0:T(8,128)(2,1)S(1)}, u32[]{:S(2)}, u32[]{:S(2)}) collective-permute-start(bf16[192,1024]{1,0:T(8,128)(2,1)} %get-tuple-element.20), channel_id=1, source_target_pairs={{0,6},{1,7},{2,0},{3,1},{4,2},{5,3},{6,4},{7,5},{8,14},{9,15},{10,... | collective-permute-start | bytes 1179656 | tf_op jit(solution)/shard_map/ppermute | solution.py:303
  46.4 0.8 copy-start.6
  48.7 0.8 copy-start.8
  49.4 1.1 copy-start.1
  50.6 1.0 copy-start.7
  51.6 1.0 copy-start.9
  54.9 0.9 copy-start.2
  55.8 0.8 copy-start.4
  56.6 0.7 copy-start.12
  59.2 4.4 %copy-start.3 = (bf16[768,512]{1,0:T(8,128)(2,1)S(1)}, bf16[768,512]{1,0:T(8,128)(2,1)}, u32[]{:S(2)}) copy-start(bf16[768,512]{1,0:T(8,128)(2,1)} %copy-done.2) | copy-start | bytes 2359300
  59.8 5.7 %collective-permute-start.3 = (bf16[768,512]{1,0:T(8,128)(2,1)S(1)}, bf16[768,512]{1,0:T(8,128)(2,1)S(1)}, u32[]{:S(2)}, u32[]{:S(2)}) collective-permute-start(bf16[768,512]{1,0:T(8,128)(2,1)S(1)} %get-tuple-element.12.refs_0_), channel_id=1, source_target_pairs={{0,1},{1,0},{2,3},{3,2},{4,5},{5,4},{6,7},{7,6},{8,9},{9,8},{10,11... | collective-permute-start | bytes 2359304 | tf_op jit(solution)/shard_map/ppermute | solution.py:342
  85.9 15.7 %copy-start.13 = (bf16[384,512]{1,0:T(8,128)(2,1)S(1)}, bf16[384,512]{1,0:T(8,128)(2,1)}, u32[]{:S(2)}) copy-start(bf16[384,512]{1,0:T(8,128)(2,1)} %copy-done.12) | copy-start | bytes 1179652
  86.1 17.1 %copy-start.5 = (bf16[384,512]{1,0:T(8,128)(2,1)S(1)}, bf16[384,512]{1,0:T(8,128)(2,1)}, u32[]{:S(2)}) copy-start(bf16[384,512]{1,0:T(8,128)(2,1)} %copy-done.4) | copy-start | bytes 1179652
  96.5 6.7 %collective-permute-start.4 = (bf16[4,192,384]{2,1,0:T(8,128)(2,1)S(1)}, bf16[4,192,384]{2,1,0:T(8,128)(2,1)S(1)}, u32[]{:S(2)}, u32[]{:S(2)}) collective-permute-start(bf16[4,192,384]{2,1,0:T(8,128)(2,1)S(1)} %all_to_all.21.refs_0_.refs_1_), channel_id=1, source_target_pairs={{0,1},{1,0},{2,3},{3,2},{4,5},{5,4},{6,7},{7,6},{8,9},{9,8},{10,11... | collective-permute-start | bytes 1769480 | tf_op jit(solution)/shard_map/ppermute | solution.py:350
  105.0 14.9 %copy-start.10 = (s32[64,8]{0,1:T(8,128)S(1)}, s32[64,8]{0,1:T(8,128)}, u32[]{:S(2)}) copy-start(s32[64,8]{0,1:T(8,128)} %param.6) | copy-start | bytes 6148
  105.0 14.9 %copy-start.11 = (f32[64,8]{0,1:T(8,128)S(1)}, f32[64,8]{0,1:T(8,128)}, u32[]{:S(2)}) copy-start(f32[64,8]{0,1:T(8,128)} %param.7) | copy-start | bytes 6148
  105.0 49.1 %all-to-all-start.3 = ((bf16[64,48,128]{2,1,0:T(8,128)(2,1)}), bf16[64,48,128]{2,1,0:T(8,128)(2,1)S(1)}, u32[]{:S(2)}, u32[]{:S(2)}) async-start(bf16[64,48,128]{2,1,0:T(8,128)(2,1)} %shard_map.75.refs_2_), calls=%async_computation.3 | async-start | bytes 1572864 | tf_op jit(solution)/shard_map/all_to_all | solution.py:367

commit v6 on v5

--- a/solution.py
+++ b/solution.py
@@ -173,10 +173,10 @@
 
 
 def other_kernel(rows_ref, w_ref, part_ref, out_ref):
+    part = (part_ref[...] + dot(rows_ref[...], w_ref[...], NT)).astype(BF)
     rows = ROWS // CHIPS
     for i in range(CHIPS):
-        at = slice(i * rows, (i + 1) * rows)
-        out_ref[i] = (part_ref[at, :] + dot(rows_ref[at, :], w_ref[...], NT)).astype(BF)
+        out_ref[i] = part[i * rows : (i + 1) * rows]
 
 
 def silu_kernel(in_ref, out_ref):

time: 156 us -> 156 us (level)
  no operation moved by 1% of the time
where the time goes in v6:
time: 156 us; the launch traced here: 155 us
  starting transfers between devices  54.3 us (35%)
  waiting for transfers between devices  45.6 us (29%)
  blocking collectives  29.6 us (19%)
  Pallas kernels  16.1 us (10%)
  local copies, waits for them, and re-layouts  8.22 us (5%)
    all_to_all x1, waiting for transfers between devices, body(): lax.all_to_all(returning, 'expert', 0, 0, axis_index_groups=[BACK])  28.7 us
    all_to_all x1, starting transfers between devices, body(): arrived = lax.all_to_all(outgoing, 'expert', 0, 0, axis_index_groups=[SENT])  20.1 us
    all_to_all x1, blocking collectives, body(): parts = lax.all_to_all(part, 'hidden', 0, 0, axis_index_groups=groups)  19.2 us
    pallas_call x11, Pallas kernels, call(): pl.pallas_call(run, out_shape=outs, in_specs=(specs or ([SMEM] if smem el...  16.1 us
    all_to_all x1, starting transfers between devices, body(): lax.all_to_all(returning, 'expert', 0, 0, axis_index_groups=[BACK])  14.9 us
    ppermute x3, waiting for transfers between devices, body(): lax.ppermute(piece, 'hidden', [(i, (i + 2 * k) % (2 * CHIPS)) for i in ra...  12.9 us
    ppermute x3, starting transfers between devices, body(): lax.ppermute(piece, 'hidden', [(i, (i + 2 * k) % (2 * CHIPS)) for i in ra...  10.5 us
    all_to_all x1, blocking collectives, body(): own = lax.all_to_all(copies, 'hidden', 0, 0, axis_index_groups=groups)  10.4 us
  transfers between devices with their start and end apart: 7, of which 7 were waited for; matrix products, arithmetic and copies ran while one was open for 1% of the time, Pallas kernels for 6%

profile of v6, /device:TPU:1, one launch (start us, length us, event | category | flops | bytes accessed | tf_op | source)
XLA Modules:
  0.0 154.9 jit_solution(10933679368565448209)
XLA Ops:
  0.6 0.0 copy-start
  0.6 2.4 %shard_map.68 = bf16[64,48,128]{2,1,0:T(8,128)(2,1)} custom-call(bf16[64,512]{1,0:T(8,128)(2,1)} %refs_0_.1, s32[8,64]{1,0:T(8,128)} %bitcast.10), custom_call_target="tpu_custom_call" | custom-call | flops 200000000 | bytes 1000000 | tf_op jit(solution)/shard_map/pallas_call | solution.py:274
  3.0 20.1 %all-to-all-start = ((bf16[64,48,128]{2,1,0:T(8,128)(2,1)}), bf16[64,48,128]{2,1,0:T(8,128)(2,1)S(1)}, u32[]{:S(2)}, u32[]{:S(2)}) async-start(bf16[64,48,128]{2,1,0:T(8,128)(2,1)} %shard_map.68), calls=%async_computation | async-start | bytes 1572864 | tf_op jit(solution)/shard_map/all_to_all | solution.py:333
  23.2 0.0 copy-done
  23.2 1.1 constant_dynamic-slice_fusion
  24.3 3.1 %collective-permute-start = (bf16[192,1024]{1,0:T(8,128)(2,1)}, bf16[192,1024]{1,0:T(8,128)(2,1)S(1)}, u32[]{:S(2)}, u32[]{:S(2)}) collective-permute-start(bf16[192,1024]{1,0:T(8,128)(2,1)} %get-tuple-element.22), channel_id=1, source_target_pairs={{0,2},{1,3},{2,4},{3,5},{4,6},{5,7},{6,0},{7,1},{8,10},{9,11},{10,... | collective-permute-start | bytes 1179656 | tf_op jit(solution)/shard_map/ppermute | solution.py:303
  27.4 4.4 %collective-permute-start.1 = (bf16[192,1024]{1,0:T(8,128)(2,1)}, bf16[192,1024]{1,0:T(8,128)(2,1)S(1)}, u32[]{:S(2)}, u32[]{:S(2)}) collective-permute-start(bf16[192,1024]{1,0:T(8,128)(2,1)} %get-tuple-element.21), channel_id=1, source_target_pairs={{0,4},{1,5},{2,6},{3,7},{4,0},{5,1},{6,2},{7,3},{8,12},{9,13},{10,... | collective-permute-start | bytes 1179656 | tf_op jit(solution)/shard_map/ppermute | solution.py:303
  31.8 3.1 %collective-permute-start.2 = (bf16[192,1024]{1,0:T(8,128)(2,1)}, bf16[192,1024]{1,0:T(8,128)(2,1)S(1)}, u32[]{:S(2)}, u32[]{:S(2)}) collective-permute-start(bf16[192,1024]{1,0:T(8,128)(2,1)} %get-tuple-element.20), channel_id=1, source_target_pairs={{0,6},{1,7},{2,0},{3,1},{4,2},{5,3},{6,4},{7,5},{8,14},{9,15},{10,... | collective-permute-start | bytes 1179656 | tf_op jit(solution)/shard_map/ppermute | solution.py:303
  34.9 0.1 pad_add_fusion.refs_0_
  35.0 2.0 %collective-permute-done.refs_2_ = bf16[192,1024]{1,0:T(8,128)(2,1)S(1)} collective-permute-done((bf16[192,1024]{1,0:T(8,128)(2,1)}, bf16[192,1024]{1,0:T(8,128)(2,1)S(1)}, u32[]{:S(2)}, u32[]{:S(2)}) %collective-permute-start) | collective-permute-done | bytes 393248 | tf_op jit(solution)/shard_map/ppermute | solution.py:303
  37.0 9.4 %collective-permute-done.1.refs_3_ = bf16[192,1024]{1,0:T(8,128)(2,1)S(1)} collective-permute-done((bf16[192,1024]{1,0:T(8,128)(2,1)}, bf16[192,1024]{1,0:T(8,128)(2,1)S(1)}, u32[]{:S(2)}, u32[]{:S(2)}) %collective-permute-start.1) | collective-permute-done | bytes 393248 | tf_op jit(solution)/shard_map/ppermute | solution.py:303
  46.4 0.8 copy-done.6
  47.2 1.5 collective-permute-done.2.refs_4_
  48.7 0.8 copy-done.8
  49.4 1.1 copy-done.1
  50.6 1.0 copy-done.7
  51.6 1.0 copy-done.9
  52.6 2.3 %shard_map.69 = (bf16[768,512]{1,0:T(8,128)(2,1)S(1)}, bf16[768,512]{1,0:T(8,128)(2,1)S(1)}, bf16[384,512]{1,0:T(8,128)(2,1)S(1)}, bf16[384,512]{1,0:T(8,128)(2,1)S(1)}, f32[8,128]{1,0:T(8,128)S(1)}) custom-call(s32[2]{0:T(128)S(1)} %pad_add_fusion.refs_0_, bf16[192,4096]{1,0:T(8,128)(2,1)S(1)} %bitcast.8, ...), custom_call_target="tpu_custom_call" | custom-call | bytes 5000000 | tf_op jit(solution)/shard_map/pallas_call | solution.py:274
  54.9 0.0 copy-start.2
  54.9 0.9 copy-done.2
  55.8 0.8 copy-done.4
  56.6 0.7 copy-done.12
  57.3 1.9 %all-to-all-done.refs_0_ = bf16[64,48,128]{2,1,0:T(8,128)(2,1)S(1)} async-done(((bf16[64,48,128]{2,1,0:T(8,128)(2,1)}), bf16[64,48,128]{2,1,0:T(8,128)(2,1)S(1)}, u32[]{:S(2)}, u32[]{:S(2)}) %all-to-all-start) | async-done | bytes 786464 | tf_op jit(solution)/shard_map/all_to_all | solution.py:333
  59.2 0.6 shard_map.70
  59.8 3.8 %collective-permute-start.3 = (bf16[768,512]{1,0:T(8,128)(2,1)S(1)}, bf16[768,512]{1,0:T(8,128)(2,1)S(1)}, u32[]{:S(2)}, u32[]{:S(2)}) collective-permute-start(bf16[768,512]{1,0:T(8,128)(2,1)S(1)} %get-tuple-element.12.refs_0_), channel_id=1, source_target_pairs={{0,1},{1,0},{2,3},{3,2},{4,5},{5,4},{6,7},{7,6},{8,9},{9,8},{10,11... | collective-permute-start | bytes 2359304 | tf_op jit(solution)/shard_map/ppermute | solution.py:342
  63.6 0.0 copy-done.3
  63.6 0.8 shard_map.71.refs_2_
  64.4 1.1 collective-permute-done.3.refs_0_
  65.5 0.8 shard_map.72
  66.3 19.2 %all_to_all.20.refs_0_ = bf16[4,192,768]{2,1,0:T(8,128)(2,1)S(1)} all-to-all(bf16[4,192,768]{2,1,0:T(8,128)(2,1)S(1)} %shard_map.72), channel_id=1, replica_groups={{0,4,2,6},{1,5,3,7},{8,12,10,14},{9,13,11,15},{16,20,18,22},{17,21,19,2..., dimensions={0} | all-to-all | bytes 2359296 | tf_op jit(solution)/shard_map/all_to_all | solution.py:347
  85.5 0.2 shard_map.73
  85.7 0.0 copy-start.5
  85.7 10.4 %all_to_all.21.refs_0_.refs_1_ = bf16[4,192,384]{2,1,0:T(8,128)(2,1)S(1)} all-to-all(bf16[4,192,384]{2,1,0:T(8,128)(2,1)S(1)} %shard_map.73), channel_id=1, replica_groups={{0,4,2,6},{1,5,3,7},{8,12,10,14},{9,13,11,15},{16,20,18,22},{17,21,19,2..., dimensions={0} | all-to-all | bytes 1179648 | tf_op jit(solution)/shard_map/all_to_all | solution.py:349
  96.2 5.1 %collective-permute-start.4 = (bf16[4,192,384]{2,1,0:T(8,128)(2,1)S(1)}, bf16[4,192,384]{2,1,0:T(8,128)(2,1)S(1)}, u32[]{:S(2)}, u32[]{:S(2)}) collective-permute-start(bf16[4,192,384]{2,1,0:T(8,128)(2,1)S(1)} %all_to_all.21.refs_0_.refs_1_), channel_id=1, source_target_pairs={{0,1},{1,0},{2,3},{3,2},{4,5},{5,4},{6,7},{7,6},{8,9},{9,8},{10,11... | collective-permute-start | bytes 1769480 | tf_op jit(solution)/shard_map/ppermute | solution.py:350
  101.2 0.0 copy-done.13
  101.2 0.6 shard_map.74
  101.8 1.0 collective-permute-done.4.refs_0_.refs_2_
  102.8 0.0 copy-done.5
  102.8 1.8 %shard_map.75.refs_2_ = bf16[64,48,128]{2,1,0:T(8,128)(2,1)} custom-call(bf16[4,192,384]{2,1,0:T(8,128)(2,1)S(1)} %collective-permute-done.4.refs_0_.refs_2_, bf16[384,512]{1,0:T(8,128)(2,1)S(1)} %copy-done.5, f32[768,512]{1,0:T(8,128)S(1)} %get-tuple-element.17.refs_2_, bf16[384,384]{1,0:T(8,128)(2,1)S(1)} %get-tuple-element.18.refs_3_), custom_call_target="tpu_custom_call" | custom-call | flops 600000000 | bytes 3000000 | tf_op jit(solution)/shard_map/pallas_call | solution.py:274
  104.6 0.0 copy-start.10
  104.6 0.0 copy-start.11
  104.6 14.9 %all-to-all-start.3 = ((bf16[64,48,128]{2,1,0:T(8,128)(2,1)}), bf16[64,48,128]{2,1,0:T(8,128)(2,1)S(1)}, u32[]{:S(2)}, u32[]{:S(2)}) async-start(bf16[64,48,128]{2,1,0:T(8,128)(2,1)} %shard_map.75.refs_2_), calls=%async_computation.3 | async-start | bytes 1572864 | tf_op jit(solution)/shard_map/all_to_all | solution.py:367
  119.5 0.0 copy-done.10
  119.5 0.0 copy-done.11
  119.5 1.3 shard_map.76.refs_0_
  120.8 4.2 %shard_map.78 = f32[96,768]{1,0:T(8,128)} custom-call(s32[2]{0:T(128)S(1)} %pad_add_fusion.refs_0_, bf16[4,192,384]{2,1,0:T(8,128)(2,1)S(1)} %all_to_all.21.refs_0_.refs_1_, bf16[4,192,384]{2,1,0:T(8,128)(2,1)S(1)} %collective-permute-done.4.refs_0_.refs_2_, f32[8,128]{1,0:T(8,128)S(1)} %get-tuple-element.19.refs_3_), custom_call_target="tpu_custom_call" | custom-call | flops 2000000000 | bytes 3000000 | tf_op jit(solution)/shard_map/pallas_call | solution.py:274
  125.0 28.7 %all-to-all-done.3.refs_1_ = bf16[64,48,128]{2,1,0:T(8,128)(2,1)S(1)} async-done(((bf16[64,48,128]{2,1,0:T(8,128)(2,1)}), bf16[64,48,128]{2,1,0:T(8,128)(2,1)S(1)}, u32[]{:S(2)}, u32[]{:S(2)}) %all-to-all-start.3) | async-done | bytes 786464 | tf_op jit(solution)/shard_map/all_to_all | solution.py:367
  153.7 1.2 shard_map.77
  (9 shorter events, 0.0 us)
Async XLA Ops:
  0.6 22.6 %copy-start = (bf16[1,2,96,4096]{3,2,1,0:T(8,128)(2,1)S(1)}, bf16[1,2,96,4096]{3,2,1,0:T(8,128)(2,1)}, u32[]{:S(2)}) copy-start(bf16[1,2,96,4096]{3,2,1,0:T(8,128)(2,1)} %param.8) | copy-start | bytes 4718596
  3.0 56.2 %all-to-all-start = ((bf16[64,48,128]{2,1,0:T(8,128)(2,1)}), bf16[64,48,128]{2,1,0:T(8,128)(2,1)S(1)}, u32[]{:S(2)}, u32[]{:S(2)}) async-start(bf16[64,48,128]{2,1,0:T(8,128)(2,1)} %shard_map.68), calls=%async_computation | async-start | bytes 1572864 | tf_op jit(solution)/shard_map/all_to_all | solution.py:333
  24.3 12.7 %collective-permute-start = (bf16[192,1024]{1,0:T(8,128)(2,1)}, bf16[192,1024]{1,0:T(8,128)(2,1)S(1)}, u32[]{:S(2)}, u32[]{:S(2)}) collective-permute-start(bf16[192,1024]{1,0:T(8,128)(2,1)} %get-tuple-element.22), channel_id=1, source_target_pairs={{0,2},{1,3},{2,4},{3,5},{4,6},{5,7},{6,0},{7,1},{8,10},{9,11},{10,... | collective-permute-start | bytes 1179656 | tf_op jit(solution)/shard_map/ppermute | solution.py:303
  27.4 19.0 %collective-permute-start.1 = (bf16[192,1024]{1,0:T(8,128)(2,1)}, bf16[192,1024]{1,0:T(8,128)(2,1)S(1)}, u32[]{:S(2)}, u32[]{:S(2)}) collective-permute-start(bf16[192,1024]{1,0:T(8,128)(2,1)} %get-tuple-element.21), channel_id=1, source_target_pairs={{0,4},{1,5},{2,6},{3,7},{4,0},{5,1},{6,2},{7,3},{8,12},{9,13},{10,... | collective-permute-start | bytes 1179656 | tf_op jit(solution)/shard_map/ppermute | solution.py:303
  31.8 16.9 %collective-permute-start.2 = (bf16[192,1024]{1,0:T(8,128)(2,1)}, bf16[192,1024]{1,0:T(8,128)(2,1)S(1)}, u32[]{:S(2)}, u32[]{:S(2)}) collective-permute-start(bf16[192,1024]{1,0:T(8,128)(2,1)} %get-tuple-element.20), channel_id=1, source_target_pairs={{0,6},{1,7},{2,0},{3,1},{4,2},{5,3},{6,4},{7,5},{8,14},{9,15},{10,... | collective-permute-start | bytes 1179656 | tf_op jit(solution)/shard_map/ppermute | solution.py:303
  46.4 0.8 copy-start.6
  48.7 0.8 copy-start.8
  49.4 1.1 copy-start.1
  50.6 1.0 copy-start.7
  51.6 1.0 copy-start.9
  54.9 0.9 copy-start.2
  55.8 0.8 copy-start.4
  56.6 0.7 copy-start.12
  59.2 4.4 %copy-start.3 = (bf16[768,512]{1,0:T(8,128)(2,1)S(1)}, bf16[768,512]{1,0:T(8,128)(2,1)}, u32[]{:S(2)}) copy-start(bf16[768,512]{1,0:T(8,128)(2,1)} %copy-done.2) | copy-start | bytes 2359300
  59.8 5.7 %collective-permute-start.3 = (bf16[768,512]{1,0:T(8,128)(2,1)S(1)}, bf16[768,512]{1,0:T(8,128)(2,1)S(1)}, u32[]{:S(2)}, u32[]{:S(2)}) collective-permute-start(bf16[768,512]{1,0:T(8,128)(2,1)S(1)} %get-tuple-element.12.refs_0_), channel_id=1, source_target_pairs={{0,1},{1,0},{2,3},{3,2},{4,5},{5,4},{6,7},{7,6},{8,9},{9,8},{10,11... | collective-permute-start | bytes 2359304 | tf_op jit(solution)/shard_map/ppermute | solution.py:342
  85.5 15.7 %copy-start.13 = (bf16[384,512]{1,0:T(8,128)(2,1)S(1)}, bf16[384,512]{1,0:T(8,128)(2,1)}, u32[]{:S(2)}) copy-start(bf16[384,512]{1,0:T(8,128)(2,1)} %copy-done.12) | copy-start | bytes 1179652
  85.7 17.1 %copy-start.5 = (bf16[384,512]{1,0:T(8,128)(2,1)S(1)}, bf16[384,512]{1,0:T(8,128)(2,1)}, u32[]{:S(2)}) copy-start(bf16[384,512]{1,0:T(8,128)(2,1)} %copy-done.4) | copy-start | bytes 1179652
  96.2 6.7 %collective-permute-start.4 = (bf16[4,192,384]{2,1,0:T(8,128)(2,1)S(1)}, bf16[4,192,384]{2,1,0:T(8,128)(2,1)S(1)}, u32[]{:S(2)}, u32[]{:S(2)}) collective-permute-start(bf16[4,192,384]{2,1,0:T(8,128)(2,1)S(1)} %all_to_all.21.refs_0_.refs_1_), channel_id=1, source_target_pairs={{0,1},{1,0},{2,3},{3,2},{4,5},{5,4},{6,7},{7,6},{8,9},{9,8},{10,11... | collective-permute-start | bytes 1769480 | tf_op jit(solution)/shard_map/ppermute | solution.py:350
  104.6 14.9 %copy-start.10 = (s32[64,8]{0,1:T(8,128)S(1)}, s32[64,8]{0,1:T(8,128)}, u32[]{:S(2)}) copy-start(s32[64,8]{0,1:T(8,128)} %param.6) | copy-start | bytes 6148
  104.6 14.9 %copy-start.11 = (f32[64,8]{0,1:T(8,128)S(1)}, f32[64,8]{0,1:T(8,128)}, u32[]{:S(2)}) copy-start(f32[64,8]{0,1:T(8,128)} %param.7) | copy-start | bytes 6148
  104.6 49.1 %all-to-all-start.3 = ((bf16[64,48,128]{2,1,0:T(8,128)(2,1)}), bf16[64,48,128]{2,1,0:T(8,128)(2,1)S(1)}, u32[]{:S(2)}, u32[]{:S(2)}) async-start(bf16[64,48,128]{2,1,0:T(8,128)(2,1)} %shard_map.75.refs_2_), calls=%async_computation.3 | async-start | bytes 1572864 | tf_op jit(solution)/shard_map/all_to_all | solution.py:367

commit v7 on v6

--- a/solution.py
+++ b/solution.py
@@ -84,19 +84,20 @@
     tok = tok_ref[...]
     slabs = jnp.concatenate([tok[:, l * LANES : (l + 1) * LANES] for l in range(SLABS)], axis=0)
     sends = []
-    for c in range(EXPERTS // GROUP):
+    step = 2 * GROUP
+    for c in range(EXPERTS // step):
         picks = [
             jnp.concatenate(
                 [jnp.where(code[e : e + 1, :] == target - 32.0 * i, 1.0, 0.0).astype(BF) for i in range(2)], axis=1
             )
-            for e in SENT[c * GROUP : (c + 1) * GROUP]
+            for e in SENT[c * step : (c + 1) * step]
         ]
         rows = dot(jnp.concatenate(picks, axis=0), slabs)
-        for j in range(GROUP):
-            e = SENT[c * GROUP + j]
+        for j in range(step):
+            e = SENT[c * step + j]
             block = rows[j * PACK : (j + 1) * PACK]
-            out_ref[c * GROUP + j] = jnp.where(first >= count[e : e + 1, :], EMPTY, block).astype(BF)
-        at = slice(c * GROUP, (c + 1) * GROUP)
+            out_ref[c * step + j] = jnp.where(first >= count[e : e + 1, :], EMPTY, block).astype(BF)
+        at = slice(c * step, (c + 1) * step)
         sends.append(pltpu.make_async_copy(out_ref.at[at], out_hbm.at[at], out_sems.at[c]))
         sends[-1].start()
     for send in sends:

time: 156 us -> 156 us (level)
  no operation moved by 1% of the time
where the time goes in v7:
time: 156 us; the launch traced here: 155 us
  starting transfers between devices  54.3 us (35%)
  waiting for transfers between devices  45.6 us (29%)
  blocking collectives  29.6 us (19%)
  Pallas kernels  16.2 us (10%)
  local copies, waits for them, and re-layouts  8.22 us (5%)
    all_to_all x1, waiting for transfers between devices, body(): lax.all_to_all(returning, 'expert', 0, 0, axis_index_groups=[BACK])  28.7 us
    all_to_all x1, starting transfers between devices, body(): arrived = lax.all_to_all(outgoing, 'expert', 0, 0, axis_index_groups=[SENT])  20.1 us
    all_to_all x1, blocking collectives, body(): parts = lax.all_to_all(part, 'hidden', 0, 0, axis_index_groups=groups)  19.2 us
    pallas_call x11, Pallas kernels, call(): pl.pallas_call(run, out_shape=outs, in_specs=(specs or ([SMEM] if smem el...  16.2 us
    all_to_all x1, starting transfers between devices, body(): lax.all_to_all(returning, 'expert', 0, 0, axis_index_groups=[BACK])  14.8 us
    ppermute x3, waiting for transfers between devices, body(): lax.ppermute(piece, 'hidden', [(i, (i + 2 * k) % (2 * CHIPS)) for i in ra...  12.9 us
    ppermute x3, starting transfers between devices, body(): lax.ppermute(piece, 'hidden', [(i, (i + 2 * k) % (2 * CHIPS)) for i in ra...  10.5 us
    all_to_all x1, blocking collectives, body(): own = lax.all_to_all(copies, 'hidden', 0, 0, axis_index_groups=groups)  10.4 us
  transfers between devices with their start and end apart: 7, of which 7 were waited for; matrix products, arithmetic and copies ran while one was open for 1% of the time, Pallas kernels for 6%

profile of v7, /device:TPU:1, one launch (start us, length us, event | category | flops | bytes accessed | tf_op | source)
XLA Modules:
  0.0 155.0 jit_solution(5305589728121921336)
XLA Ops:
  0.6 0.0 copy-start
  0.6 2.4 %shard_map.68 = bf16[64,48,128]{2,1,0:T(8,128)(2,1)} custom-call(bf16[64,512]{1,0:T(8,128)(2,1)} %refs_0_.1, s32[8,64]{1,0:T(8,128)} %bitcast.10), custom_call_target="tpu_custom_call" | custom-call | flops 200000000 | bytes 1000000 | tf_op jit(solution)/shard_map/pallas_call | solution.py:275
  3.1 20.1 %all-to-all-start = ((bf16[64,48,128]{2,1,0:T(8,128)(2,1)}), bf16[64,48,128]{2,1,0:T(8,128)(2,1)S(1)}, u32[]{:S(2)}, u32[]{:S(2)}) async-start(bf16[64,48,128]{2,1,0:T(8,128)(2,1)} %shard_map.68), calls=%async_computation | async-start | bytes 1572864 | tf_op jit(solution)/shard_map/all_to_all | solution.py:334
  23.3 0.0 copy-done
  23.3 1.1 constant_dynamic-slice_fusion
  24.4 3.1 %collective-permute-start = (bf16[192,1024]{1,0:T(8,128)(2,1)}, bf16[192,1024]{1,0:T(8,128)(2,1)S(1)}, u32[]{:S(2)}, u32[]{:S(2)}) collective-permute-start(bf16[192,1024]{1,0:T(8,128)(2,1)} %get-tuple-element.22), channel_id=1, source_target_pairs={{0,2},{1,3},{2,4},{3,5},{4,6},{5,7},{6,0},{7,1},{8,10},{9,11},{10,... | collective-permute-start | bytes 1179656 | tf_op jit(solution)/shard_map/ppermute | solution.py:304
  27.5 4.4 %collective-permute-start.1 = (bf16[192,1024]{1,0:T(8,128)(2,1)}, bf16[192,1024]{1,0:T(8,128)(2,1)S(1)}, u32[]{:S(2)}, u32[]{:S(2)}) collective-permute-start(bf16[192,1024]{1,0:T(8,128)(2,1)} %get-tuple-element.21), channel_id=1, source_target_pairs={{0,4},{1,5},{2,6},{3,7},{4,0},{5,1},{6,2},{7,3},{8,12},{9,13},{10,... | collective-permute-start | bytes 1179656 | tf_op jit(solution)/shard_map/ppermute | solution.py:304
  31.9 3.1 %collective-permute-start.2 = (bf16[192,1024]{1,0:T(8,128)(2,1)}, bf16[192,1024]{1,0:T(8,128)(2,1)S(1)}, u32[]{:S(2)}, u32[]{:S(2)}) collective-permute-start(bf16[192,1024]{1,0:T(8,128)(2,1)} %get-tuple-element.20), channel_id=1, source_target_pairs={{0,6},{1,7},{2,0},{3,1},{4,2},{5,3},{6,4},{7,5},{8,14},{9,15},{10,... | collective-permute-start | bytes 1179656 | tf_op jit(solution)/shard_map/ppermute | solution.py:304
  34.9 0.1 pad_add_fusion.refs_0_
  35.0 2.0 %collective-permute-done.refs_2_ = bf16[192,1024]{1,0:T(8,128)(2,1)S(1)} collective-permute-done((bf16[192,1024]{1,0:T(8,128)(2,1)}, bf16[192,1024]{1,0:T(8,128)(2,1)S(1)}, u32[]{:S(2)}, u32[]{:S(2)}) %collective-permute-start) | collective-permute-done | bytes 393248 | tf_op jit(solution)/shard_map/ppermute | solution.py:304
  37.1 9.4 %collective-permute-done.1.refs_3_ = bf16[192,1024]{1,0:T(8,128)(2,1)S(1)} collective-permute-done((bf16[192,1024]{1,0:T(8,128)(2,1)}, bf16[192,1024]{1,0:T(8,128)(2,1)S(1)}, u32[]{:S(2)}, u32[]{:S(2)}) %collective-permute-start.1) | collective-permute-done | bytes 393248 | tf_op jit(solution)/shard_map/ppermute | solution.py:304
  46.5 0.8 copy-done.6
  47.2 1.5 collective-permute-done.2.refs_4_
  48.7 0.8 copy-done.8
  49.5 1.1 copy-done.1
  50.6 1.0 copy-done.7
  51.6 1.0 copy-done.9
  52.6 2.3 %shard_map.69 = (bf16[768,512]{1,0:T(8,128)(2,1)S(1)}, bf16[768,512]{1,0:T(8,128)(2,1)S(1)}, bf16[384,512]{1,0:T(8,128)(2,1)S(1)}, bf16[384,512]{1,0:T(8,128)(2,1)S(1)}, f32[8,128]{1,0:T(8,128)S(1)}) custom-call(s32[2]{0:T(128)S(1)} %pad_add_fusion.refs_0_, bf16[192,4096]{1,0:T(8,128)(2,1)S(1)} %bitcast.8, ...), custom_call_target="tpu_custom_call" | custom-call | bytes 5000000 | tf_op jit(solution)/shard_map/pallas_call | solution.py:275
  54.9 0.0 copy-start.2
  55.0 0.9 copy-done.2
  55.9 0.8 copy-done.4
  56.7 0.7 copy-done.12
  57.4 1.9 %all-to-all-done.refs_0_ = bf16[64,48,128]{2,1,0:T(8,128)(2,1)S(1)} async-done(((bf16[64,48,128]{2,1,0:T(8,128)(2,1)}), bf16[64,48,128]{2,1,0:T(8,128)(2,1)S(1)}, u32[]{:S(2)}, u32[]{:S(2)}) %all-to-all-start) | async-done | bytes 786464 | tf_op jit(solution)/shard_map/all_to_all | solution.py:334
  59.3 0.6 shard_map.70
  59.9 3.8 %collective-permute-start.3 = (bf16[768,512]{1,0:T(8,128)(2,1)S(1)}, bf16[768,512]{1,0:T(8,128)(2,1)S(1)}, u32[]{:S(2)}, u32[]{:S(2)}) collective-permute-start(bf16[768,512]{1,0:T(8,128)(2,1)S(1)} %get-tuple-element.12.refs_0_), channel_id=1, source_target_pairs={{0,1},{1,0},{2,3},{3,2},{4,5},{5,4},{6,7},{7,6},{8,9},{9,8},{10,11... | collective-permute-start | bytes 2359304 | tf_op jit(solution)/shard_map/ppermute | solution.py:343
  63.7 0.0 copy-done.3
  63.7 0.8 shard_map.71.refs_2_
  64.5 1.1 collective-permute-done.3.refs_0_
  65.5 0.8 shard_map.72
  66.4 19.2 %all_to_all.20.refs_0_ = bf16[4,192,768]{2,1,0:T(8,128)(2,1)S(1)} all-to-all(bf16[4,192,768]{2,1,0:T(8,128)(2,1)S(1)} %shard_map.72), channel_id=1, replica_groups={{0,4,2,6},{1,5,3,7},{8,12,10,14},{9,13,11,15},{16,20,18,22},{17,21,19,2..., dimensions={0} | all-to-all | bytes 2359296 | tf_op jit(solution)/shard_map/all_to_all | solution.py:348
  85.6 0.2 shard_map.73
  85.8 0.0 copy-start.5
  85.8 10.4 %all_to_all.21.refs_0_.refs_1_ = bf16[4,192,384]{2,1,0:T(8,128)(2,1)S(1)} all-to-all(bf16[4,192,384]{2,1,0:T(8,128)(2,1)S(1)} %shard_map.73), channel_id=1, replica_groups={{0,4,2,6},{1,5,3,7},{8,12,10,14},{9,13,11,15},{16,20,18,22},{17,21,19,2..., dimensions={0} | all-to-all | bytes 1179648 | tf_op jit(solution)/shard_map/all_to_all | solution.py:350
  96.2 5.0 %collective-permute-start.4 = (bf16[4,192,384]{2,1,0:T(8,128)(2,1)S(1)}, bf16[4,192,384]{2,1,0:T(8,128)(2,1)S(1)}, u32[]{:S(2)}, u32[]{:S(2)}) collective-permute-start(bf16[4,192,384]{2,1,0:T(8,128)(2,1)S(1)} %all_to_all.21.refs_0_.refs_1_), channel_id=1, source_target_pairs={{0,1},{1,0},{2,3},{3,2},{4,5},{5,4},{6,7},{7,6},{8,9},{9,8},{10,11... | collective-permute-start | bytes 1769480 | tf_op jit(solution)/shard_map/ppermute | solution.py:351
  101.3 0.0 copy-done.13
  101.3 0.6 shard_map.74
  101.9 1.0 collective-permute-done.4.refs_0_.refs_2_
  102.9 0.0 copy-done.5
  102.9 1.8 %shard_map.75.refs_2_ = bf16[64,48,128]{2,1,0:T(8,128)(2,1)} custom-call(bf16[4,192,384]{2,1,0:T(8,128)(2,1)S(1)} %collective-permute-done.4.refs_0_.refs_2_, bf16[384,512]{1,0:T(8,128)(2,1)S(1)} %copy-done.5, f32[768,512]{1,0:T(8,128)S(1)} %get-tuple-element.17.refs_2_, bf16[384,384]{1,0:T(8,128)(2,1)S(1)} %get-tuple-element.18.refs_3_), custom_call_target="tpu_custom_call" | custom-call | flops 600000000 | bytes 3000000 | tf_op jit(solution)/shard_map/pallas_call | solution.py:275
  104.7 0.0 copy-start.10
  104.7 0.0 copy-start.11
  104.7 14.8 %all-to-all-start.3 = ((bf16[64,48,128]{2,1,0:T(8,128)(2,1)}), bf16[64,48,128]{2,1,0:T(8,128)(2,1)S(1)}, u32[]{:S(2)}, u32[]{:S(2)}) async-start(bf16[64,48,128]{2,1,0:T(8,128)(2,1)} %shard_map.75.refs_2_), calls=%async_computation.3 | async-start | bytes 1572864 | tf_op jit(solution)/shard_map/all_to_all | solution.py:368
  119.5 0.0 copy-done.10
  119.5 0.0 copy-done.11
  119.6 1.3 shard_map.76.refs_0_
  120.9 4.2 %shard_map.78 = f32[96,768]{1,0:T(8,128)} custom-call(s32[2]{0:T(128)S(1)} %pad_add_fusion.refs_0_, bf16[4,192,384]{2,1,0:T(8,128)(2,1)S(1)} %all_to_all.21.refs_0_.refs_1_, bf16[4,192,384]{2,1,0:T(8,128)(2,1)S(1)} %collective-permute-done.4.refs_0_.refs_2_, f32[8,128]{1,0:T(8,128)S(1)} %get-tuple-element.19.refs_3_), custom_call_target="tpu_custom_call" | custom-call | flops 2000000000 | bytes 3000000 | tf_op jit(solution)/shard_map/pallas_call | solution.py:275
  125.0 28.7 %all-to-all-done.3.refs_1_ = bf16[64,48,128]{2,1,0:T(8,128)(2,1)S(1)} async-done(((bf16[64,48,128]{2,1,0:T(8,128)(2,1)}), bf16[64,48,128]{2,1,0:T(8,128)(2,1)S(1)}, u32[]{:S(2)}, u32[]{:S(2)}) %all-to-all-start.3) | async-done | bytes 786464 | tf_op jit(solution)/shard_map/all_to_all | solution.py:368
  153.8 1.2 shard_map.77
  (9 shorter events, 0.0 us)
Async XLA Ops:
  0.6 22.7 %copy-start = (bf16[1,2,96,4096]{3,2,1,0:T(8,128)(2,1)S(1)}, bf16[1,2,96,4096]{3,2,1,0:T(8,128)(2,1)}, u32[]{:S(2)}) copy-start(bf16[1,2,96,4096]{3,2,1,0:T(8,128)(2,1)} %param.8) | copy-start | bytes 4718596
  3.1 56.2 %all-to-all-start = ((bf16[64,48,128]{2,1,0:T(8,128)(2,1)}), bf16[64,48,128]{2,1,0:T(8,128)(2,1)S(1)}, u32[]{:S(2)}, u32[]{:S(2)}) async-start(bf16[64,48,128]{2,1,0:T(8,128)(2,1)} %shard_map.68), calls=%async_computation | async-start | bytes 1572864 | tf_op jit(solution)/shard_map/all_to_all | solution.py:334
  24.4 12.7 %collective-permute-start = (bf16[192,1024]{1,0:T(8,128)(2,1)}, bf16[192,1024]{1,0:T(8,128)(2,1)S(1)}, u32[]{:S(2)}, u32[]{:S(2)}) collective-permute-start(bf16[192,1024]{1,0:T(8,128)(2,1)} %get-tuple-element.22), channel_id=1, source_target_pairs={{0,2},{1,3},{2,4},{3,5},{4,6},{5,7},{6,0},{7,1},{8,10},{9,11},{10,... | collective-permute-start | bytes 1179656 | tf_op jit(solution)/shard_map/ppermute | solution.py:304
  27.5 19.0 %collective-permute-start.1 = (bf16[192,1024]{1,0:T(8,128)(2,1)}, bf16[192,1024]{1,0:T(8,128)(2,1)S(1)}, u32[]{:S(2)}, u32[]{:S(2)}) collective-permute-start(bf16[192,1024]{1,0:T(8,128)(2,1)} %get-tuple-element.21), channel_id=1, source_target_pairs={{0,4},{1,5},{2,6},{3,7},{4,0},{5,1},{6,2},{7,3},{8,12},{9,13},{10,... | collective-permute-start | bytes 1179656 | tf_op jit(solution)/shard_map/ppermute | solution.py:304
  31.9 16.9 %collective-permute-start.2 = (bf16[192,1024]{1,0:T(8,128)(2,1)}, bf16[192,1024]{1,0:T(8,128)(2,1)S(1)}, u32[]{:S(2)}, u32[]{:S(2)}) collective-permute-start(bf16[192,1024]{1,0:T(8,128)(2,1)} %get-tuple-element.20), channel_id=1, source_target_pairs={{0,6},{1,7},{2,0},{3,1},{4,2},{5,3},{6,4},{7,5},{8,14},{9,15},{10,... | collective-permute-start | bytes 1179656 | tf_op jit(solution)/shard_map/ppermute | solution.py:304
  46.5 0.8 copy-start.6
  48.7 0.8 copy-start.8
  49.5 1.1 copy-start.1
  50.6 1.0 copy-start.7
  51.6 1.0 copy-start.9
  54.9 0.9 copy-start.2
  55.9 0.8 copy-start.4
  56.7 0.7 copy-start.12
  59.3 4.4 %copy-start.3 = (bf16[768,512]{1,0:T(8,128)(2,1)S(1)}, bf16[768,512]{1,0:T(8,128)(2,1)}, u32[]{:S(2)}) copy-start(bf16[768,512]{1,0:T(8,128)(2,1)} %copy-done.2) | copy-start | bytes 2359300
  59.9 5.7 %collective-permute-start.3 = (bf16[768,512]{1,0:T(8,128)(2,1)S(1)}, bf16[768,512]{1,0:T(8,128)(2,1)S(1)}, u32[]{:S(2)}, u32[]{:S(2)}) collective-permute-start(bf16[768,512]{1,0:T(8,128)(2,1)S(1)} %get-tuple-element.12.refs_0_), channel_id=1, source_target_pairs={{0,1},{1,0},{2,3},{3,2},{4,5},{5,4},{6,7},{7,6},{8,9},{9,8},{10,11... | collective-permute-start | bytes 2359304 | tf_op jit(solution)/shard_map/ppermute | solution.py:343
  85.6 15.7 %copy-start.13 = (bf16[384,512]{1,0:T(8,128)(2,1)S(1)}, bf16[384,512]{1,0:T(8,128)(2,1)}, u32[]{:S(2)}) copy-start(bf16[384,512]{1,0:T(8,128)(2,1)} %copy-done.12) | copy-start | bytes 1179652
  85.8 17.1 %copy-start.5 = (bf16[384,512]{1,0:T(8,128)(2,1)S(1)}, bf16[384,512]{1,0:T(8,128)(2,1)}, u32[]{:S(2)}) copy-start(bf16[384,512]{1,0:T(8,128)(2,1)} %copy-done.4) | copy-start | bytes 1179652
  96.2 6.7 %collective-permute-start.4 = (bf16[4,192,384]{2,1,0:T(8,128)(2,1)S(1)}, bf16[4,192,384]{2,1,0:T(8,128)(2,1)S(1)}, u32[]{:S(2)}, u32[]{:S(2)}) collective-permute-start(bf16[4,192,384]{2,1,0:T(8,128)(2,1)S(1)} %all_to_all.21.refs_0_.refs_1_), channel_id=1, source_target_pairs={{0,1},{1,0},{2,3},{3,2},{4,5},{5,4},{6,7},{7,6},{8,9},{9,8},{10,11... | collective-permute-start | bytes 1769480 | tf_op jit(solution)/shard_map/ppermute | solution.py:351
  104.7 14.9 %copy-start.10 = (s32[64,8]{0,1:T(8,128)S(1)}, s32[64,8]{0,1:T(8,128)}, u32[]{:S(2)}) copy-start(s32[64,8]{0,1:T(8,128)} %param.6) | copy-start | bytes 6148
  104.7 14.9 %copy-start.11 = (f32[64,8]{0,1:T(8,128)S(1)}, f32[64,8]{0,1:T(8,128)}, u32[]{:S(2)}) copy-start(f32[64,8]{0,1:T(8,128)} %param.7) | copy-start | bytes 6148
  104.7 49.1 %all-to-all-start.3 = ((bf16[64,48,128]{2,1,0:T(8,128)(2,1)}), bf16[64,48,128]{2,1,0:T(8,128)(2,1)S(1)}, u32[]{:S(2)}, u32[]{:S(2)}) async-start(bf16[64,48,128]{2,1,0:T(8,128)(2,1)} %shard_map.75.refs_2_), calls=%async_computation.3 | async-start | bytes 1572864 | tf_op jit(solution)/shard_map/all_to_all | solution.py:368
